TPU v7x, 128 devices: a whole 4x4x4 slice. The times are simulated.
128 devices in a mesh: ctx: 16 (over x, y_lo, core), mp: 8 (over z, y_hi).
Axes of the slice: x: 4, y: 4 (y_hi: 2, y_lo: 2; y = y_hi * 2 + y_lo), z: 4, core: 2. Of those that a mesh axis runs over, the one named last changes fastest.
Arguments:
- layer_input: bfloat16 [16384, 1024], P(('ctx', 'mp')), may hold values from -6 to 6
- positions: int32 [16384], P('ctx'), may hold values from 0 to 24575, as said below
- expert_ids: int32 [16384, 8], P(('ctx', 'mp')), may hold values from 0 to 31, all different within a row; in each aligned block of 128 rows (0 to 127, 128 to 255, ...) at most 36 rows name the same one
- attn_gain: bfloat16 [1024], P('ctx'), may hold values from 0.5 to 1.5
- w_query: bfloat16 [1024, 1024], P('ctx', 'mp'), may hold values from -0.75 to 0.75
- w_key: bfloat16 [1024, 512], P('ctx', 'mp'), may hold values from -0.75 to 0.75
- w_value: bfloat16 [1024, 512], P('ctx', 'mp'), may hold values from -0.1875 to 0.1875
- w_attn_out: bfloat16 [1024, 1024], P('mp', 'ctx'), may hold values from -4 to 4
- ffn_gain: bfloat16 [1024], P('ctx'), may hold values from 0.5 to 1.5
- router: bfloat16 [1024, 32], P('ctx'), may hold values from -0.09375 to 0.09375
- w_in: bfloat16 [32, 1024, 1024], P('mp', 'ctx'), may hold values from -0.1875 to 0.1875
- w_out: bfloat16 [32, 512, 1024], P('mp', None, 'ctx'), may hold values from -4 to 4
- cotangent: bfloat16 [16384, 1024], P(('ctx', 'mp')), may hold values from -6 to 6
Outputs:
- activations: bfloat16 [16384, 1024], P(('ctx', 'mp'))
- input_grad: bfloat16 [16384, 1024], P(('ctx', 'mp'))
- attn_gain_grad: float32 [1024], P(('ctx', 'mp'))
- query_grad: float32 [1024, 1024], P('ctx', 'mp')
- key_grad: float32 [1024, 512], P('ctx', 'mp')
- value_grad: float32 [1024, 512], P('ctx', 'mp')
- attn_out_grad: float32 [1024, 1024], P('mp', 'ctx')
- ffn_gain_grad: float32 [1024], P(('ctx', 'mp'))
- router_grad: float32 [1024, 32], P(('ctx', 'mp'))
- expert_in_grad: float32 [32, 1024, 1024], P('mp', 'ctx')
- expert_out_grad: float32 [32, 512, 1024], P('mp', None, 'ctx')
Inputs may be any that keep to these rules, and one draw needn't show every extreme that they name: `expert_ids`: each row names 8 different experts. Among the rows of one device (aligned blocks of 128 rows, in order) no expert is named more than 36 times, a bound that some block reaches. `positions`: the first position is 0 and each next one is larger by 1 or 2; exactly 8192 of these steps are 2.
All inputs are finite; a program needn't handle non-finite values.
Results may differ from a plain program's by a relative error of at most 0.038.
Values may be sent and summed in bfloat16 or wider, within the bound.
A program may use at most 128 MiB of HBM per device.

v0:
```python
import jax
import jax.numpy as jnp
from jax import lax
from jax.sharding import PartitionSpec as P

epsilon = 1e-06
branch_scale = 0.22
score_scale = 0.015625
rope_base = 10000.0
highest = lax.Precision.HIGHEST


def phases(positions, head_width):
    steps_up = jnp.arange(head_width // 2).astype(jnp.float32)
    frequency = rope_base ** (-2.0 * steps_up / head_width)
    angles = positions.astype(jnp.float32)[:, None] * frequency[None, :]
    angles = jnp.concatenate([angles, angles], axis=1)
    return (jnp.cos(angles), jnp.sin(angles))


def rotate(values, cosine, sine):
    half_width = values.shape[-1] // 2
    turned = jnp.concatenate([-values[..., half_width:], values[..., :half_width]], axis=-1)
    return values * cosine + turned * sine


def rotate_back(grads, cosine, sine):
    half_width = grads.shape[-1] // 2
    turned = grads * sine
    turned = jnp.concatenate([turned[..., half_width:], -turned[..., :half_width]], axis=-1)
    return grads * cosine + turned


def contract(left, right, left_dim, right_dim):
    return lax.dot_general(
        left, right, (((left_dim,), (right_dim,)), ((), ())), preferred_element_type=jnp.float32
    )


def normalize(values, gain):
    inverse = lax.rsqrt(jnp.mean(values * values, axis=-1, keepdims=True) + epsilon)
    scaled = values * inverse
    return (scaled, inverse, scaled * gain)


def norm_back(grads, scaled, inverse, gain):
    inner = grads * gain
    return (
        inverse * (inner - scaled * jnp.mean(inner * scaled, axis=-1, keepdims=True)),
        jnp.sum(grads * scaled, axis=0),
    )


def fetch_keys(key_rows, value_rows):
    return (
        lax.all_gather(key_rows, "ctx", axis=0, tiled=True),
        lax.all_gather(value_rows, "ctx", axis=0, tiled=True),
    )


def key_blocks():
    return 1024


def body(
    layer_input,
    positions,
    expert_ids,
    attn_gain,
    w_query,
    w_key,
    w_value,
    w_attn_out,
    ffn_gain,
    router,
    w_in,
    w_out,
    cotangent,
):
    gathered = (
        lax.all_gather(attn_gain, "ctx", axis=0, tiled=True),
        lax.all_gather(w_query, "ctx", axis=0, tiled=True),
        lax.all_gather(w_key, "ctx", axis=0, tiled=True),
        lax.all_gather(w_value, "ctx", axis=0, tiled=True),
        lax.all_gather(w_attn_out, "ctx", axis=1, tiled=True),
        lax.all_gather(ffn_gain, "ctx", axis=0, tiled=True),
        lax.all_gather(router, "ctx", axis=0, tiled=True),
        lax.all_gather(w_in, "ctx", axis=1, tiled=True),
        lax.all_gather(w_out, "ctx", axis=2, tiled=True),
    )
    gain_one, query_w, key_w, value_w, out_w, gain_two, router_w, in_w, out_expert = gathered
    gain_one = gain_one.astype(jnp.float32)
    gain_two = gain_two.astype(jnp.float32)
    local_rows = layer_input.shape[0]
    top_count = expert_ids.shape[1]
    experts = router_w.shape[1]
    group_size = lax.axis_size("mp")
    head_width = key_w.shape[1]
    groups = query_w.shape[1] // head_width
    capacity = local_rows * top_count * 9 // (experts * 8)
    experts_here = in_w.shape[0]
    hidden_units = out_expert.shape[1]
    features = layer_input.shape[1]
    inputs = layer_input.astype(jnp.float32)
    scaled_one, inverse_one, normed = normalize(inputs, gain_one)
    normed_rows = lax.all_gather(normed.astype(jnp.bfloat16), "mp", axis=0, tiled=True)
    block_len = normed_rows.shape[0]
    queries = jnp.dot(normed_rows, query_w, preferred_element_type=jnp.float32)
    keys_raw = jnp.dot(normed_rows, key_w, preferred_element_type=jnp.float32)
    values_new = jnp.dot(normed_rows, value_w, preferred_element_type=jnp.float32).astype(
        jnp.bfloat16
    )
    cosine, sine = phases(positions, head_width)
    turned_queries = rotate(
        queries.reshape(block_len, groups, head_width), cosine[:, None, :], sine[:, None, :]
    )
    query_rows = (
        turned_queries.astype(jnp.bfloat16)
        .transpose(1, 0, 2)
        .reshape(groups * block_len, head_width)
    )
    key_new = rotate(keys_raw, cosine, sine).astype(jnp.bfloat16)
    query_start = lax.axis_index("ctx") * block_len
    row_place = query_start + jnp.tile(jnp.arange(block_len, dtype=jnp.int32), groups)
    last_row = query_start + block_len - 1
    initial = (
        jnp.full((groups * block_len,), -1e30, jnp.float32),
        jnp.zeros((groups * block_len,), jnp.float32),
        jnp.zeros((groups * block_len, head_width), jnp.float32),
    )
    state = initial
    key_piece = lax.all_gather(key_new, "ctx", axis=0, tiled=True)
    value_piece = lax.all_gather(values_new, "ctx", axis=0, tiled=True)
    total_rows = key_piece.shape[0]
    block_size = key_blocks()
    count = total_rows // block_size
    offsets = block_size * jnp.arange(count, dtype=jnp.int32)

    def visit(inner, item):
        key_block, value_block, offset = item

        def visit_work(current):
            best, total, summed = current
            scores = contract(query_rows, key_block, 1, 1) * score_scale
            visible = (
                offset + jnp.arange(block_size, dtype=jnp.int32)[None, :] <= row_place[:, None]
            )
            scores = jnp.where(visible, scores, -jnp.inf)
            top_now = jnp.maximum(best, jnp.max(scores, axis=1))
            fading = jnp.exp(best - top_now)
            weights = jnp.exp(scores - top_now[:, None])
            total = total * fading + jnp.sum(weights, axis=1)
            summed = summed * fading[:, None] + jnp.dot(
                weights.astype(jnp.bfloat16), value_block, preferred_element_type=jnp.float32
            )
            return (top_now, total, summed)

        return (lax.cond(offset > last_row, lambda current: current, visit_work, inner), None)

    key_stack = key_piece.reshape(count, block_size, head_width)
    value_stack = value_piece.reshape(count, block_size, head_width)
    state, unused = lax.scan(visit, state, (key_stack, value_stack, offsets))
    best, total, summed = state
    log_total = best + jnp.log(total)
    attended = summed / total[:, None]
    out_rows = (
        attended.astype(jnp.bfloat16)
        .reshape(groups, block_len, head_width)
        .transpose(1, 0, 2)
        .reshape(block_len, groups * head_width)
    )
    branch = lax.psum_scatter(
        jnp.dot(out_rows, out_w, preferred_element_type=jnp.float32).astype(jnp.bfloat16),
        "mp",
        scatter_dimension=0,
        tiled=True,
    ).astype(jnp.float32)
    hidden = inputs + branch_scale * branch
    scaled_two, inverse_two, normed_two = normalize(hidden, gain_two)
    routed = normed_two.astype(jnp.bfloat16)
    logits = jnp.dot(routed, router_w, preferred_element_type=jnp.float32)
    member = (expert_ids[:, :, None] == jnp.arange(experts, dtype=jnp.int32)[None, None, :]).astype(
        jnp.float32
    )
    chosen = jnp.sum(member * logits[:, None, :], axis=2)
    gates = jax.nn.softmax(chosen, axis=-1)
    picked = expert_ids.reshape(-1)
    counted = (picked[:, None] == jnp.arange(experts, dtype=jnp.int32)[None, :]).astype(jnp.int32)
    slots = jnp.sum(counted * (jnp.cumsum(counted, axis=0) - 1), axis=1)
    target = picked * capacity + slots
    placing = (target[:, None] == jnp.arange(experts * capacity, dtype=jnp.int32)[None, :]).astype(
        jnp.bfloat16
    )
    sources = jnp.repeat(routed, top_count, axis=0)
    outgoing = (
        contract(placing, sources, 0, 0)
        .astype(jnp.bfloat16)
        .reshape(group_size, experts_here, capacity, features)
    )
    incoming = lax.all_to_all(outgoing, "mp", split_axis=0, concat_axis=0, tiled=True)
    gate_up = jnp.einsum("secd,edf->secf", incoming, in_w, preferred_element_type=jnp.float32)
    active = (jax.nn.silu(gate_up[..., :hidden_units]) * gate_up[..., hidden_units:]).astype(
        jnp.bfloat16
    )
    produced = jnp.einsum(
        "secf,efd->secd", active, out_expert, preferred_element_type=jnp.float32
    ).astype(jnp.bfloat16)
    returned = lax.all_to_all(produced, "mp", split_axis=0, concat_axis=0, tiled=True)
    returned, incoming, gate_up, active = (returned, incoming, gate_up, active)
    chosen_rows = jnp.take(returned.reshape(experts * capacity, features), target, axis=0).reshape(
        local_rows, top_count, features
    )
    mixed = jnp.einsum(
        "tk,tkd->td", gates, chosen_rows, precision=highest, preferred_element_type=jnp.float32
    )
    outputs = hidden + branch_scale * mixed
    out_grad_in = cotangent.astype(jnp.float32)
    grad_rows = (
        (branch_scale * gates[:, :, None] * out_grad_in[:, None, :])
        .astype(jnp.bfloat16)
        .reshape(local_rows * top_count, features)
    )
    grad_out = (
        contract(placing, grad_rows, 0, 0)
        .astype(jnp.bfloat16)
        .reshape(group_size, experts_here, capacity, features)
    )
    grad_in = lax.all_to_all(grad_out, "mp", split_axis=0, concat_axis=0, tiled=True)
    gate_part = gate_up[..., :hidden_units]
    up_part = gate_up[..., hidden_units:]
    squashed = jax.nn.sigmoid(gate_part)
    silu_part = gate_part * squashed
    slope = squashed * (1.0 + gate_part * (1.0 - squashed))
    active_grad = jnp.einsum(
        "secd,efd->secf", grad_in, out_expert, preferred_element_type=jnp.float32
    )
    gate_up_grad = jnp.concatenate(
        [active_grad * up_part * slope, active_grad * silu_part], axis=-1
    ).astype(jnp.bfloat16)
    out_expert_grad = jnp.einsum(
        "secf,secd->efd", active, grad_in, preferred_element_type=jnp.float32
    )
    in_expert_grad = jnp.einsum(
        "secd,secf->edf", incoming, gate_up_grad, preferred_element_type=jnp.float32
    )
    row_grads = jnp.einsum("secf,edf->secd", gate_up_grad, in_w, preferred_element_type=jnp.float32)
    row_back = lax.all_to_all(
        row_grads.astype(jnp.bfloat16), "mp", split_axis=0, concat_axis=0, tiled=True
    ).astype(row_grads.dtype)
    routed_grad = jnp.sum(
        jnp.take(row_back.reshape(experts * capacity, features), target, axis=0).reshape(
            local_rows, top_count, features
        ),
        axis=1,
    )
    share_grad = branch_scale * jnp.einsum(
        "tkd,td->tk",
        chosen_rows,
        out_grad_in,
        precision=highest,
        preferred_element_type=jnp.float32,
    )
    chosen_grad = gates * (share_grad - jnp.sum(gates * share_grad, axis=1, keepdims=True))
    logit_grad = jnp.sum(member * chosen_grad[:, :, None], axis=1)
    routed_grad = routed_grad + jnp.dot(
        logit_grad, router_w.astype(jnp.float32).T, precision=highest
    )
    router_grad = jnp.dot(routed.astype(jnp.float32).T, logit_grad, precision=highest)
    hidden_grad, gain_two_grad = norm_back(routed_grad, scaled_two, inverse_two, gain_two)
    hidden_grad = hidden_grad + out_grad_in
    branch_grad = (branch_scale * hidden_grad).astype(jnp.bfloat16)
    branch_rows = lax.all_gather(branch_grad, "mp", axis=0, tiled=True)
    out_w_grad = contract(out_rows, branch_rows, 0, 0)
    out_grad = contract(branch_rows, out_w, 1, 1).astype(jnp.bfloat16)
    out_grad_rows = (
        out_grad.reshape(block_len, groups, head_width)
        .transpose(1, 0, 2)
        .reshape(groups * block_len, head_width)
    )
    delta = jnp.sum(out_grad_rows.astype(jnp.float32) * attended, axis=1)
    key_all, value_all = fetch_keys(key_new, values_new)
    total_keys = key_all.shape[0]
    back_size = key_blocks()
    back_count = total_keys // back_size
    back_offsets = back_size * jnp.arange(back_count, dtype=jnp.int32)

    def reverse(query_grad, item):
        key_block, value_block, offset = item

        def reverse_work(current):
            scores = contract(query_rows, key_block, 1, 1) * score_scale
            visible = offset + jnp.arange(back_size, dtype=jnp.int32)[None, :] <= row_place[:, None]
            probs = jnp.where(visible, jnp.exp(scores - log_total[:, None]), 0.0)
            value_part = contract(probs.astype(jnp.bfloat16), out_grad_rows, 0, 0)
            prob_grad = contract(out_grad_rows, value_block, 1, 1)
            score_grad = (probs * (prob_grad - delta[:, None])).astype(jnp.bfloat16)
            current = (
                current
                + jnp.dot(score_grad, key_block, preferred_element_type=jnp.float32) * score_scale
            )
            key_part = contract(score_grad, query_rows, 0, 0) * score_scale
            return (current, jnp.concatenate([key_part, value_part], axis=1))

        def skip(current):
            return (current, jnp.zeros((back_size, 2 * head_width), jnp.float32))

        return lax.cond(offset > last_row, skip, reverse_work, query_grad)

    key_stack = key_all.reshape(back_count, back_size, head_width)
    value_stack = value_all.reshape(back_count, back_size, head_width)
    query_grad, key_terms = lax.scan(
        reverse,
        jnp.zeros((groups * block_len, head_width), jnp.float32),
        (key_stack, value_stack, back_offsets),
    )
    key_value_grad = lax.psum_scatter(
        key_terms.reshape(total_keys, 2 * head_width).astype(jnp.bfloat16),
        "ctx",
        scatter_dimension=0,
        tiled=True,
    ).astype(jnp.float32)
    key_grad = rotate_back(key_value_grad[:, :head_width], cosine, sine).astype(jnp.bfloat16)
    value_grad = key_value_grad[:, head_width:].astype(jnp.bfloat16)
    query_back = query_grad.reshape(groups, block_len, head_width).transpose(1, 0, 2)
    query_grad = (
        rotate_back(query_back, cosine[:, None, :], sine[:, None, :])
        .reshape(block_len, groups * head_width)
        .astype(jnp.bfloat16)
    )
    query_w_grad = contract(normed_rows, query_grad, 0, 0)
    key_w_grad = contract(normed_rows, key_grad, 0, 0)
    value_w_grad = contract(normed_rows, value_grad, 0, 0)
    total_term = contract(query_grad, query_w, 1, 1)
    total_term = total_term + contract(key_grad, key_w, 1, 1)
    normed_grad = lax.psum_scatter(
        (total_term + contract(value_grad, value_w, 1, 1)).astype(jnp.bfloat16),
        "mp",
        scatter_dimension=0,
        tiled=True,
    ).astype(jnp.float32)
    input_grad, gain_one_grad = norm_back(normed_grad, scaled_one, inverse_one, gain_one)
    input_grad = input_grad + hidden_grad
    weight_grads = (
        lax.psum_scatter(
            query_w_grad.astype(jnp.bfloat16), "ctx", scatter_dimension=0, tiled=True
        ).astype(jnp.float32),
        lax.psum_scatter(
            key_w_grad.astype(jnp.bfloat16), "ctx", scatter_dimension=0, tiled=True
        ).astype(jnp.float32),
        lax.psum_scatter(
            value_w_grad.astype(jnp.bfloat16), "ctx", scatter_dimension=0, tiled=True
        ).astype(jnp.float32),
        lax.psum_scatter(
            out_w_grad.astype(jnp.bfloat16), "ctx", scatter_dimension=1, tiled=True
        ).astype(jnp.float32),
        lax.psum_scatter(
            in_expert_grad.astype(jnp.bfloat16), "ctx", scatter_dimension=1, tiled=True
        ).astype(jnp.float32),
        lax.psum_scatter(
            out_expert_grad.astype(jnp.bfloat16), "ctx", scatter_dimension=2, tiled=True
        ).astype(jnp.float32),
    )
    small_sums = (
        lax.psum_scatter(gain_one_grad, ("ctx", "mp"), scatter_dimension=0, tiled=True),
        lax.psum_scatter(gain_two_grad, ("ctx", "mp"), scatter_dimension=0, tiled=True),
        lax.psum_scatter(router_grad, ("ctx", "mp"), scatter_dimension=0, tiled=True),
    )
    return (
        outputs.astype(jnp.bfloat16),
        input_grad.astype(jnp.bfloat16),
        small_sums[0],
        weight_grads[0],
        weight_grads[1],
        weight_grads[2],
        weight_grads[3],
        small_sums[1],
        small_sums[2],
        weight_grads[4],
        weight_grads[5],
    )


def solution(mesh):
    placed = (
        P(("ctx", "mp"), None),
        P("ctx"),
        P(("ctx", "mp"), None),
        P("ctx"),
        P("ctx", "mp"),
        P("ctx", "mp"),
        P("ctx", "mp"),
        P("mp", "ctx"),
        P("ctx"),
        P("ctx", None),
        P("mp", "ctx", None),
        P("mp", None, "ctx"),
        P(("ctx", "mp"), None),
    )
    return jax.shard_map(
        body,
        mesh=mesh,
        in_specs=placed,
        out_specs=(
            P(("ctx", "mp"), None),
            P(("ctx", "mp"), None),
            P(("ctx", "mp")),
            P("ctx", "mp"),
            P("ctx", "mp"),
            P("ctx", "mp"),
            P("mp", "ctx"),
            P(("ctx", "mp")),
            P(("ctx", "mp"), None),
            P("mp", "ctx", None),
            P("mp", None, "ctx"),
        ),
        check_vma=False,
    )
```

profile of v0, /device:TPU:65, one launch (start us, length us, event | category | flops | bytes accessed | tf_op | source)
XLA Modules:
  0.0 1734.6 jit_solution(13302306968292610431)
XLA Ops:
  10.8 27.2 %all-reduce.6 = (bf16[1024]{0:T(1024)(128)(2,1)S(1)}, bf16[1024]{0:T(1024)(128)(2,1)S(1)}) all-reduce(bf16[1024]{0:T(1024)(128)(2,1)S(1)} %dynamic-update-slice.1, bf16[1024]{0:T(1024)(128)(2,1)S(1)} %dynamic-update-slice), channel_id=1, replica_groups=mesh['ctx'=16,'mp'=8] {'ctx'}, use_global_device_ids=true, to_apply=%add.1 | all-reduce | flops 2048 | bytes 8192
  41.7 20.7 %all_gather.43 = bf16[1024,64]{1,0:T(8,128)(2,1)S(1)} all-gather(bf16[64,64]{1,0:T(8,128)(2,1)} %param.26), channel_id=1, replica_groups=mesh['ctx'=16,'mp'=8] {'ctx'}, dimensions={0}, use_global_device_ids=true | all-gather | bytes 139264 | tf_op jit(solution)/shard_map/all_gather | solution.py:83
  62.5 33.1 %all-gather.8.cloned.1.call-done = bf16[1024,1024]{1,0:T(8,128)(2,1)} async-done(((bf16[128,1024]{1,0:T(8,128)(2,1)}), bf16[1024,1024]{1,0:T(8,128)(2,1)}) %all-gather.8.cloned.1.call-update) | async-done | bytes 2097168 | tf_op jit(solution)/shard_map/all_gather | solution.py:106
  99.9 20.5 %all_gather.46 = bf16[1024,64]{1,0:T(8,128)(2,1)S(1)} all-gather(bf16[64,64]{1,0:T(8,128)(2,1)S(1)} %copy-done.42), channel_id=1, replica_groups=mesh['ctx'=16,'mp'=8] {'ctx'}, dimensions={0}, use_global_device_ids=true | all-gather | bytes 139264 | tf_op jit(solution)/shard_map/all_gather | solution.py:84
  121.9 17.0 all_gather.45
  139.0 18.5 %all_gather.48 = bf16[128,1024]{0,1:T(8,128)(2,1)S(1)} all-gather(bf16[128,64]{0,1:T(8,128)(2,1)S(1)} %copy-done.44), channel_id=1, replica_groups=mesh['ctx'=16,'mp'=8] {'ctx'}, dimensions={1}, use_global_device_ids=true | all-gather | bytes 278528 | tf_op jit(solution)/shard_map/all_gather | solution.py:85
  175.8 38.6 %while.31 = (s32[]{:T(128)}, f32[2048]{0:T(1024)S(1)}, f32[2048]{0:T(1024)S(1)}, f32[2048,64]{0,1:T(8,128)S(1)}, s32[16]{0:T(128)S(1)}, /*index=5*/s32[]{:T(128)...) while((s32[]{:T(128)}, f32[2048]{0:T(1024)S(1)}, ...), condition=%wide.region_6.7_spmd.clone, body=%wide.region_1.6_spmd.clone.sunk | while | flops 566500352 | bytes 27215120 | solution.py:162
  227.9 183.0 %reduce-scatter.10.cloned.1.call-done = bf16[128,1024]{1,0:T(8,128)(2,1)} async-done(((bf16[1024,1024]{1,0:T(8,128)(2,1)}), bf16[128,1024]{1,0:T(8,128)(2,1)}) %reduce-scatter.10.cloned.1.call-update) | async-done | bytes 262160 | tf_op jit(solution)/shard_map/reduce_scatter | solution.py:172
  430.4 68.5 %all-gather = bf16[16,64,32]{1,2,0:T(8,128)(2,1)S(1)} all-gather(bf16[1,64,32]{1,2,0:T(8,128)(2,1)S(1)} %bitcast.257), channel_id=1, replica_groups=mesh['ctx'=16,'mp'=8] {'ctx'}, dimensions={0}, use_global_device_ids=true | all-gather | bytes 69632 | tf_op jit(solution)/shard_map/all_gather | solution.py:87
  526.9 13.9 all-gather.16.cloned.1.call-done
  540.8 13.7 all-to-all-done.2
  584.1 18.0 %all-to-all-done.1 = bf16[8,4,36,1024]{3,1,2,0:T(4,128)(2,1)S(1)} async-done(((bf16[8,4,36,1024]{3,1,2,0:T(4,128)(2,1)}), bf16[8,4,36,1024]{3,1,2,0:T(4,128)(2,1)S(1)}, u32[]{:S(2)}, u32[]{:S(2)}) %all-to-all-start.1) | async-done | bytes 2359328 | tf_op jit(solution)/shard_map/all_to_all | solution.py:208
  664.0 51.4 %all-gather.18.cloned.1.call-done = bf16[1024,1024]{1,0:T(8,128)(2,1)} async-done(((bf16[128,1024]{1,0:T(8,128)(2,1)}), bf16[1024,1024]{1,0:T(8,128)(2,1)}) %all-gather.18.cloned.1.call-update) | async-done | bytes 2097168 | tf_op jit(solution)/shard_map/all_gather | solution.py:272
  718.6 57.3 %while.32 = (s32[]{:T(128)}, f32[2048,64]{0,1:T(8,128)S(1)}, bf16[16,1024,128]{1,2,0:T(8,128)(2,1)}, s32[16]{0:T(128)S(1)}, s32[]{:T(128)}, /*index=5*/bf16[16,1...) while((s32[]{:T(128)}, f32[2048,64]{0,1:T(8,128)S(1)}, ...), condition=%wide.region_23.24_spmd.clone, body=%wide.region_20.23_spmd.clone.sunk | while | flops 1368263680 | bytes 42039560 | solution.py:311
  799.1 218.0 %reduce-scatter.12.cloned.1.call-done = bf16[1024,128]{0,1:T(8,128)(2,1)} async-done(((bf16[16384,128]{0,1:T(8,128)(2,1)}), bf16[1024,128]{0,1:T(8,128)(2,1)}) %reduce-scatter.12.cloned.1.call-update) | async-done | bytes 262160 | tf_op jit(solution)/shard_map/reduce_scatter | solution.py:316
  1041.8 127.0 %all-reduce.9.cloned.1.call-done = f32[1024,32]{1,0:T(8,128)} async-done(((f32[1024,32]{1,0:T(8,128)}), f32[1024,32]{1,0:T(8,128)}) %all-reduce.9.cloned.1.call-update) | async-done | bytes 131088
  1170.1 57.1 %reduce-scatter.22.cloned.1.call-done = bf16[128,64]{0,1:T(8,128)(2,1)} async-done(((bf16[128,1024]{0,1:T(8,128)(2,1)}), bf16[128,64]{0,1:T(8,128)(2,1)}) %reduce-scatter.22.cloned.1.call-update) | async-done | bytes 16400 | tf_op jit(solution)/shard_map/reduce_scatter | solution.py:353
  1228.6 60.2 %reduce-scatter.16.cloned.1.call-done = bf16[64,128]{1,0:T(8,128)(2,1)} async-done(((bf16[1024,128]{1,0:T(8,128)(2,1)}), bf16[64,128]{1,0:T(8,128)(2,1)}) %reduce-scatter.16.cloned.1.call-update) | async-done | bytes 16400 | tf_op jit(solution)/shard_map/reduce_scatter | solution.py:344
  1290.1 67.1 %reduce-scatter.26.cloned.1.call-done = bf16[4,512,64]{1,2,0:T(8,128)(2,1)} async-done(((bf16[4,512,1024]{1,2,0:T(8,128)(2,1)}), bf16[4,512,64]{1,2,0:T(8,128)(2,1)}) %reduce-scatter.26.cloned.1.call-update) | async-done | bytes 262160 | tf_op jit(solution)/shard_map/reduce_scatter | solution.py:359
  1358.9 59.3 %reduce-scatter.18.cloned.1.call-done = bf16[64,64]{1,0:T(8,128)(2,1)} async-done(((bf16[1024,64]{1,0:T(8,128)(2,1)}), bf16[64,64]{1,0:T(8,128)(2,1)}) %reduce-scatter.18.cloned.1.call-update) | async-done | bytes 8208 | tf_op jit(solution)/shard_map/reduce_scatter | solution.py:347
  1419.6 59.5 %reduce-scatter.20.cloned.1.call-done = bf16[64,64]{1,0:T(8,128)(2,1)} async-done(((bf16[1024,64]{1,0:T(8,128)(2,1)}), bf16[64,64]{1,0:T(8,128)(2,1)}) %reduce-scatter.20.cloned.1.call-update) | async-done | bytes 8208 | tf_op jit(solution)/shard_map/reduce_scatter | solution.py:350
  1480.3 99.7 %reduce-scatter.24.cloned.1.call-done = bf16[4,64,1024]{2,1,0:T(8,128)(2,1)} async-done(((bf16[4,1024,1024]{2,1,0:T(8,128)(2,1)}), bf16[4,64,1024]{2,1,0:T(8,128)(2,1)}) %reduce-scatter.24.cloned.1.call-update) | async-done | bytes 524304 | tf_op jit(solution)/shard_map/reduce_scatter | solution.py:356
  1582.2 74.8 %reduce-scatter.14.cloned.1.call-done = bf16[128,1024]{1,0:T(8,128)(2,1)} async-done(((bf16[1024,1024]{1,0:T(8,128)(2,1)}), bf16[128,1024]{1,0:T(8,128)(2,1)}) %reduce-scatter.14.cloned.1.call-update) | async-done | bytes 262160 | tf_op jit(solution)/shard_map/reduce_scatter | solution.py:335
  1658.2 65.9 %all-reduce.5 = (f32[1024]{0:T(1024)S(1)}, f32[1024]{0:T(1024)S(1)}) all-reduce(f32[1024]{0:T(1024)S(1)} %get-tuple-element.498, f32[1024]{0:T(1024)S(1)} %get-tuple-element.496), channel_id=5, replica_groups=mesh['ctx'=16,'mp'=8] {'ctx','mp'}, use_global_device_ids=true, to_apply=%region_28.29.clone | all-reduce | flops 2048 | bytes 16384
  (472 shorter events, 365.4 us)
Async XLA Ops:
  7.2 88.5 %all-gather.8.cloned.1.call-start = ((), (), s32[]{:S(2)}) async-start(), calls=%async_computation.13 | async-start | bytes 2359296 | tf_op jit(solution)/shard_map/all_gather | solution.py:106
  41.0 117.8 %all-gather.10.cloned.1.call-start = ((), (), s32[]{:S(2)}) async-start(), calls=%async_computation.14 | async-start | bytes 2228224 | tf_op jit(solution)/shard_map/all_gather | solution.py:132
  99.8 71.1 %all-gather.12.cloned.1.call-start = ((), (), s32[]{:S(2)}) async-start(), calls=%async_computation.15 | async-start | bytes 2228224 | tf_op jit(solution)/shard_map/all_gather | solution.py:133
  121.8 289.1 %reduce-scatter.10.cloned.1.call-start = ((), (), s32[]{:S(2)}) async-start(), calls=%async_computation.16 | async-start | bytes 2359296 | tf_op jit(solution)/shard_map/reduce_scatter | solution.py:172
  216.8 300.0 %all-gather.14.cloned.1.call-start = ((), (), s32[]{:S(2)}) async-start(), calls=%async_computation.17 | async-start | bytes 8912896 | tf_op jit(solution)/shard_map/all_gather | solution.py:88
  217.4 323.3 %all-gather.16.cloned.1.call-start = ((), (), s32[]{:S(2)}) async-start(), calls=%async_computation.18 | async-start | bytes 4456448 | tf_op jit(solution)/shard_map/all_gather | solution.py:89
  424.3 85.7 %all-to-all-start = ((bf16[8,4,36,1024]{3,1,2,0:T(4,128)(2,1)}), bf16[8,4,36,1024]{3,1,2,0:T(4,128)(2,1)}, u32[]{:S(2)}, u32[]{:S(2)}) async-start(bf16[8,4,36,1024]{3,1,2,0:T(4,128)(2,1)} %copy.148), calls=%async_computation.1 | async-start | bytes 4718592 | tf_op jit(solution)/shard_map/all_to_all | solution.py:200
  510.0 44.6 %all-to-all-start.2 = ((bf16[8,4,36,1024]{3,1,2,0:T(4,128)(2,1)}), bf16[8,4,36,1024]{3,1,2,0:T(4,128)(2,1)S(1)}, u32[]{:S(2)}, u32[]{:S(2)}) async-start(bf16[8,4,36,1024]{3,1,2,0:T(4,128)(2,1)} %copy.154), calls=%async_computation.3 | async-start | bytes 4718592 | tf_op jit(solution)/shard_map/all_to_all | solution.py:228
  567.5 34.6 %all-to-all-start.1 = ((bf16[8,4,36,1024]{3,1,2,0:T(4,128)(2,1)}), bf16[8,4,36,1024]{3,1,2,0:T(4,128)(2,1)S(1)}, u32[]{:S(2)}, u32[]{:S(2)}) async-start(bf16[8,4,36,1024]{3,1,2,0:T(4,128)(2,1)} %copy.150), calls=%async_computation.2 | async-start | bytes 4718592 | tf_op jit(solution)/shard_map/all_to_all | solution.py:208
  602.1 34.2 %all-to-all-start.3 = ((bf16[8,4,36,1024]{3,1,2,0:T(4,128)(2,1)}), bf16[8,4,36,1024]{3,1,2,0:T(4,128)(2,1)}, u32[]{:S(2)}, u32[]{:S(2)}) async-start(bf16[8,4,36,1024]{3,1,2,0:T(4,128)(2,1)} %copy.156), calls=%async_computation.4 | async-start | bytes 4718592 | tf_op jit(solution)/shard_map/all_to_all | solution.py:247
  608.8 106.6 %all-gather.18.cloned.1.call-start = ((), (), s32[]{:S(2)}) async-start(), calls=%async_computation.19 | async-start | bytes 2359296 | tf_op jit(solution)/shard_map/all_gather | solution.py:272
  663.7 353.4 %reduce-scatter.12.cloned.1.call-start = ((), (), s32[]{:S(2)}) async-start(), calls=%async_computation.20 | async-start | bytes 4456448 | tf_op jit(solution)/shard_map/reduce_scatter | solution.py:316
  780.7 388.1 %all-reduce.9.cloned.1.call-start = ((), (), s32[]{:S(2)}) async-start(), calls=%async_computation.28 | async-start | bytes 1048576
  783.1 444.1 %reduce-scatter.22.cloned.1.call-start = ((), (), s32[]{:S(2)}) async-start(), calls=%async_computation.25 | async-start | bytes 278528 | tf_op jit(solution)/shard_map/reduce_scatter | solution.py:353
  789.1 499.7 %reduce-scatter.16.cloned.1.call-start = ((), (), s32[]{:S(2)}) async-start(), calls=%async_computation.22 | async-start | bytes 278528 | tf_op jit(solution)/shard_map/reduce_scatter | solution.py:344
  791.7 565.4 %reduce-scatter.26.cloned.1.call-start = ((), (), s32[]{:S(2)}) async-start(), calls=%async_computation.27 | async-start | bytes 4456448 | tf_op jit(solution)/shard_map/reduce_scatter | solution.py:359
  799.0 619.2 %reduce-scatter.18.cloned.1.call-start = ((), (), s32[]{:S(2)}) async-start(), calls=%async_computation.23 | async-start | bytes 278528 | tf_op jit(solution)/shard_map/reduce_scatter | solution.py:347
  1021.4 457.6 %reduce-scatter.20.cloned.1.call-start = ((), (), s32[]{:S(2)}) async-start(), calls=%async_computation.24 | async-start | bytes 278528 | tf_op jit(solution)/shard_map/reduce_scatter | solution.py:350
  1023.0 557.1 %reduce-scatter.24.cloned.1.call-start = ((), (), s32[]{:S(2)}) async-start(), calls=%async_computation.26 | async-start | bytes 8912896 | tf_op jit(solution)/shard_map/reduce_scatter | solution.py:356
  1034.4 622.6 %reduce-scatter.14.cloned.1.call-start = ((), (), s32[]{:S(2)}) async-start(), calls=%async_computation.21 | async-start | bytes 2359296 | tf_op jit(solution)/shard_map/reduce_scatter | solution.py:335
  1039.0 686.3 %copy-start.4 = (bf16[128,1024]{1,0:T(8,128)(2,1)S(1)}, bf16[128,1024]{1,0:T(8,128)(2,1)}, u32[]{:S(2)}) copy-start(bf16[128,1024]{1,0:T(8,128)(2,1)} %reduce-scatter.10.cloned.1.call-done) | copy-start | bytes 786436
  1039.0 686.3 %copy-start.8 = (f32[128,1024]{1,0:T(8,128)S(1)}, f32[128,1024]{1,0:T(8,128)}, u32[]{:S(2)}) copy-start(f32[128,1024]{1,0:T(8,128)} %copy-done.7) | copy-start | bytes 1572868
  1039.0 686.3 %copy-start.22 = (bf16[128,1024]{1,0:T(8,128)(2,1)S(1)}, bf16[128,1024]{1,0:T(8,128)(2,1)}, u32[]{:S(2)}) copy-start(bf16[128,1024]{1,0:T(8,128)(2,1)} %param.33) | copy-start | bytes 786436
  1039.0 686.3 %copy-start.51 = (f32[128]{0:T(128)S(1)}, f32[128]{0:T(128)}, u32[]{:S(2)}) copy-start(f32[128]{0:T(128)} %copy-done.50) | copy-start | bytes 1540
  (50 other events, 3048.3 us)
Sparse Core Ops, SparseCore 0:
  41.1 54.5 all-gather.7
  100.0 34.2 all-gather.9
  136.5 34.4 all-gather.11
  217.0 193.9 reduce-scatter.9
  412.4 80.4 all-gather.13
  494.5 46.2 all-gather.15
  663.8 51.5 all-gather.17
  780.8 236.2 reduce-scatter.11
  1022.5 146.2 all-reduce.8
  1171.1 56.0 reduce-scatter.21
  1230.1 58.5 reduce-scatter.15
  1291.1 65.9 reduce-scatter.25
  1359.6 58.5 reduce-scatter.17
  1420.4 58.5 reduce-scatter.19
  1481.4 98.6 reduce-scatter.23
  1584.1 72.7 reduce-scatter.13
where the time goes:
time: 1750 us; the launch traced here: 1730 us
  waiting for transfers between devices  1160 us (66%)
  blocking collectives  238 us (14%)
  matrix products  118 us (7%)
  local copies, waits for them, and re-layouts  103 us (6%)
  other arithmetic  51.8 us (3%)
  starting transfers between devices  27.8 us (2%)
  loops' own time  22.7 us (1%)
    reduce_scatter x1, waiting for transfers between devices, body(): lax.psum_scatter(key_terms.reshape(total_keys, 2 * head_width).astype(jnp...  218 us
    reduce_scatter x1, waiting for transfers between devices, body(): lax.psum_scatter(jnp.dot(out_rows, out_w, preferred_element_type=jnp.floa...  183 us
    unnamed x17, waiting for transfers between devices  128 us
    reduce_scatter x1, waiting for transfers between devices, body(): lax.psum_scatter(in_expert_grad.astype(jnp.bfloat16), 'ctx', scatter_dime...  99.7 us
    unnamed x2, blocking collectives  93.2 us
    reduce_scatter x1, waiting for transfers between devices, body(): lax.psum_scatter((total_term + contract(value_grad, value_w, 1, 1)).astyp...  74.8 us
    all_gather x1, blocking collectives, body(): lax.all_gather(router, 'ctx', axis=0, tiled=True)  68.5 us
    reduce_scatter x1, waiting for transfers between devices, body(): lax.psum_scatter(out_expert_grad.astype(jnp.bfloat16), 'ctx', scatter_dim...  67.1 us
  transfers between devices with their start and end apart: 20, of which 17 were waited for; matrix products, arithmetic and copies ran while one was open for 7% of the time, Pallas kernels for 0%

commit v1 on v0

v1 whole, which is shorter than its diff:
```python
import functools

import jax
import jax.numpy as jnp
from jax import lax
from jax.experimental import pallas as pl
from jax.experimental.pallas import tpu as pltpu
from jax.sharding import PartitionSpec as P

MESH = pl.DeviceIdType.MESH
epsilon = 1e-06
branch_scale = 0.22
score_scale = 0.015625
rope_base = 10000.0
highest = lax.Precision.HIGHEST
log2_e = 1.4426950408889634
bf16 = jnp.bfloat16
f32 = jnp.float32
CTX, MP = 16, 8
HEAD = 64
TOK = 128
BLOCK = 1024
HALF = 512
ANY = pl.BlockSpec(memory_space=pl.ANY)
VM = pl.BlockSpec(memory_space=pltpu.VMEM)
VMEM_LIMIT = 56 * 1024 * 1024


def contract(left, right, left_dim, right_dim):
    return lax.dot_general(
        left, right, (((left_dim,), (right_dim,)), ((), ())), preferred_element_type=f32
    )


def place():
    return lax.axis_index("ctx"), lax.axis_index("mp")


def greet(signal_to, expected):
    barrier = pltpu.get_barrier_semaphore()
    for target in signal_to:
        pl.semaphore_signal(barrier, inc=1, device_id=target, device_id_type=MESH)
    pl.semaphore_wait(barrier, expected)


def remote(src, dst, send, recv, target):
    return pltpu.make_async_remote_copy(
        src_ref=src, dst_ref=dst, send_sem=send, recv_sem=recv,
        device_id=target, device_id_type=MESH,
    )


def comm_call(kernel, number, arrays, outs, sems, cost):
    return pl.pallas_call(
        kernel,
        out_shape=outs,
        in_specs=[ANY] * len(arrays),
        out_specs=[ANY] * len(outs),
        scratch_shapes=[pltpu.SemaphoreType.DMA((n,)) for n in sems],
        compiler_params=pltpu.CompilerParams(collective_id=number, has_side_effects=True),
        cost_estimate=pl.CostEstimate(flops=0, bytes_accessed=cost, transcendentals=0),
    )(*arrays)


def shape(dims, kind=bf16):
    return jax.ShapeDtypeStruct(dims, kind)


def start_kernel(x_ref, id_ref, w_ref, xo, ido, wo, xs, xr, ids, idr, ws, wr, loc):
    c, m = place()
    upper = m >= MP // 2
    t = jnp.where(upper, CTX - 1 - c, c)
    signals = []
    for k in range(1, MP):
        sender = lax.rem(m + k, MP)
        signals.append((jnp.where(sender >= MP // 2, CTX - 1 - c, c), sender))
    for k in range(1, CTX):
        signals.append((lax.rem(c + k, CTX), m))
    barrier = pltpu.get_barrier_semaphore()
    for target in signals:
        pl.semaphore_signal(barrier, inc=1, device_id=target, device_id_type=MESH)

    @pl.when(upper)
    def _():
        pl.semaphore_signal(barrier, inc=1, device_id=(CTX - 1 - c, m), device_id_type=MESH)
        pl.semaphore_wait(barrier, MP + CTX - 1)

    @pl.when(jnp.logical_not(upper))
    def _():
        pl.semaphore_wait(barrier, MP + CTX - 2)

    own_w = pltpu.make_async_copy(w_ref, wo.at[c], loc.at[0])
    own_w.start()
    x_copies, id_copies, w_copies = [], [], []
    for k in range(MP):
        target = (t, lax.rem(m + k, MP))
        x_copies.append(remote(x_ref, xo.at[m], xs.at[k], xr.at[k], target))
        id_copies.append(remote(id_ref, ido.at[m], ids.at[k], idr.at[k], target))
    for k in range(1, CTX):
        w_copies.append(remote(w_ref, wo.at[c], ws.at[k], wr.at[k], (lax.rem(c + k, CTX), m)))
    own_x = pltpu.make_async_copy(x_ref, xo.at[m], loc.at[1])
    own_id = pltpu.make_async_copy(id_ref, ido.at[m], loc.at[2])

    @pl.when(upper)
    def _():
        x_copies[0].start()
        id_copies[0].start()

    @pl.when(jnp.logical_not(upper))
    def _():
        own_x.start()
        own_id.start()

    for k in range(1, MP):
        x_copies[k].start()
        id_copies[k].start()
    for copy in w_copies:
        copy.start()
    for k in range(1, MP):
        x_copies[k].wait()
        id_copies[k].wait()
    for copy in w_copies:
        copy.wait()
    own_w.wait()

    @pl.when(upper)
    def _():
        x_copies[0].wait()
        id_copies[0].wait()

    @pl.when(jnp.logical_not(upper))
    def _():
        own_x.wait()
        own_id.wait()


def keys_kernel(kv_ref, w_ref, kvo, wo, send, recv, send2, recv2, ws, wr, loc):
    c, m = place()
    chip, core = c // 2, lax.rem(c, 2)
    sibling = (chip * 2 + 1 - core, m)
    others = [(lax.rem(chip + k, 8) * 2 + core, m) for k in range(1, 8)]
    mates = [(c, lax.rem(m + k, MP)) for k in range(1, MP)]
    greet(others + [sibling] + mates, 7 + 1 + 7)
    own = pltpu.make_async_copy(kv_ref, kvo.at[c], loc.at[0])
    own.start()
    own_w = pltpu.make_async_copy(w_ref, wo.at[m], loc.at[1])
    own_w.start()
    far, near, rows = [], [], []
    for k in range(1, 8):
        copy = remote(kv_ref, kvo.at[c], send.at[k], recv.at[k], others[k - 1])
        copy.start()
        far.append(copy)
    first = remote(kv_ref, kvo.at[c], send.at[0], recv.at[0], sibling)
    first.start()
    for k in range(1, MP):
        copy = remote(w_ref, wo.at[m], ws.at[k], wr.at[k], mates[k - 1])
        copy.start()
        rows.append(copy)
    for k in range(1, 8):
        far[k - 1].wait_recv()
        slot = lax.rem(chip + 8 - k, 8) * 2 + core
        copy = remote(kvo.at[slot], kvo.at[slot], send2.at[k], recv2.at[k], sibling)
        copy.start()
        near.append(copy)
    first.wait()
    for k in range(1, 8):
        far[k - 1].wait_send()
        near[k - 1].wait()
        rows[k - 1].wait()
    own.wait()
    own_w.wait()


def gather_kernel(a_ref, out, send, recv, loc):
    c, m = place()
    mates = [(c, lax.rem(m + k, MP)) for k in range(1, MP)]
    greet(mates, MP - 1)
    own = pltpu.make_async_copy(a_ref, out.at[m], loc.at[0])
    own.start()
    copies = []
    for k in range(1, MP):
        copy = remote(a_ref, out.at[m], send.at[k], recv.at[k], mates[k - 1])
        copy.start()
        copies.append(copy)
    for copy in copies:
        copy.wait()
    own.wait()


def scatter_kernel(a_ref, b_ref, ao, bo, s1, r1, s2, r2, loc):
    c, m = place()
    mates = [(c, lax.rem(m + k, MP)) for k in range(1, MP)]
    greet(mates, MP - 1)
    own_a = pltpu.make_async_copy(a_ref.at[m], ao.at[m], loc.at[0])
    own_a.start()
    own_b = pltpu.make_async_copy(b_ref.at[m], bo.at[m], loc.at[1])
    own_b.start()
    copies = []
    for k in range(1, MP):
        to = lax.rem(m + k, MP)
        copies.append(remote(a_ref.at[to], ao.at[m], s1.at[k], r1.at[k], mates[k - 1]))
        copies.append(remote(b_ref.at[to], bo.at[m], s2.at[k], r2.at[k], mates[k - 1]))
    for copy in copies:
        copy.start()
    for copy in copies:
        copy.wait()
    own_a.wait()
    own_b.wait()


def sibling_kernel(a_ref, out, send, recv):
    c, m = place()
    chip, core = c // 2, lax.rem(c, 2)
    sibling = (chip * 2 + 1 - core, m)
    greet([sibling], 1)
    copy = remote(a_ref.at[:, 1 - core], out, send.at[0], recv.at[0], sibling)
    copy.start()
    copy.wait()


def chips_kernel(a_ref, out, send, recv, loc):
    c, m = place()
    chip, core = c // 2, lax.rem(c, 2)
    others = [(lax.rem(chip + k, 8) * 2 + core, m) for k in range(1, 8)]
    greet(others, 7)
    own = pltpu.make_async_copy(a_ref.at[chip], out.at[chip], loc.at[0])
    own.start()
    copies = []
    for k in range(1, 8):
        to = lax.rem(chip + k, 8)
        copy = remote(a_ref.at[to], out.at[chip], send.at[k], recv.at[k], others[k - 1])
        copy.start()
        copies.append(copy)
    for copy in copies:
        copy.wait()
    own.wait()


def finish_kernel(a_ref, g_ref, ao, go, s1, r1, s2, r2, loc):
    c, m = place()
    upper = m >= MP // 2
    t = jnp.where(upper, CTX - 1 - c, c)
    barrier = pltpu.get_barrier_semaphore()
    for k in range(1, MP):
        pl.semaphore_signal(
            barrier, inc=1, device_id=(t, lax.rem(m + k, MP)), device_id_type=MESH
        )
    for k in range(1, CTX):
        pl.semaphore_signal(
            barrier, inc=1, device_id=(lax.rem(c + k, CTX), m), device_id_type=MESH
        )

    @pl.when(upper)
    def _():
        pl.semaphore_signal(barrier, inc=1, device_id=(t, m), device_id_type=MESH)
        pl.semaphore_wait(barrier, MP + CTX - 1)

    @pl.when(jnp.logical_not(upper))
    def _():
        pl.semaphore_wait(barrier, MP + CTX - 2)

    own_g = pltpu.make_async_copy(g_ref.at[c], go.at[c], loc.at[0])
    own_g.start()
    own_a = pltpu.make_async_copy(a_ref.at[m], ao.at[m], loc.at[1])
    a_copies, g_copies = [], []
    for k in range(MP):
        to = lax.rem(m + k, MP)
        target = (jnp.where(to >= MP // 2, CTX - 1 - c, c), to)
        a_copies.append(remote(a_ref.at[to], ao.at[m], s1.at[k], r1.at[k], target))
    for k in range(1, CTX):
        to = lax.rem(c + k, CTX)
        g_copies.append(remote(g_ref.at[to], go.at[c], s2.at[k], r2.at[k], (to, m)))

    @pl.when(upper)
    def _():
        a_copies[0].start()

    @pl.when(jnp.logical_not(upper))
    def _():
        own_a.start()

    for k in range(1, MP):
        a_copies[k].start()
    for copy in g_copies:
        copy.start()
    for k in range(1, MP):
        a_copies[k].wait()
    for copy in g_copies:
        copy.wait()
    own_g.wait()

    @pl.when(upper)
    def _():
        a_copies[0].wait()

    @pl.when(jnp.logical_not(upper))
    def _():
        own_a.wait()


def sums_kernel(a_ref, out, got, part, got2, s1, r1, s2, r2):
    c, m = place()
    peers = [(lax.rem(c + k, CTX), m) for k in range(1, CTX)]
    mates = [(c, lax.rem(m + k, MP)) for k in range(1, MP)]
    greet(peers + mates, CTX - 1 + MP - 1)
    copies = []
    for k in range(1, CTX):
        to = lax.rem(c + k, CTX)
        copy = remote(a_ref.at[to], got.at[k], s1.at[k], r1.at[k], peers[k - 1])
        copy.start()
        copies.append(copy)
    total = a_ref[c]
    for copy in copies:
        copy.wait()
    for k in range(1, CTX):
        total = total + got[k]
    part[...] = total
    copies = []
    for k in range(1, MP):
        to = lax.rem(m + k, MP)
        copy = remote(part.at[to], got2.at[k], s2.at[k], r2.at[k], mates[k - 1])
        copy.start()
        copies.append(copy)
    last = part[m]
    for copy in copies:
        copy.wait()
    for k in range(1, MP):
        last = last + got2[k]
    out[...] = last


def small_sums(terms):
    dims = terms.shape[2:]
    return pl.pallas_call(
        sums_kernel,
        out_shape=shape(dims, f32),
        in_specs=[VM],
        out_specs=VM,
        scratch_shapes=[
            pltpu.VMEM((CTX, MP) + dims, f32),
            pltpu.VMEM((MP,) + dims, f32),
            pltpu.VMEM((MP,) + dims, f32),
            pltpu.SemaphoreType.DMA((CTX,)),
            pltpu.SemaphoreType.DMA((CTX,)),
            pltpu.SemaphoreType.DMA((MP,)),
            pltpu.SemaphoreType.DMA((MP,)),
        ],
        compiler_params=pltpu.CompilerParams(collective_id=9, has_side_effects=True),
    )(terms)


def unit(index, first_half):
    second = index > first_half
    part = second.astype(jnp.int32)
    key_half = jnp.where(second, index - first_half - 1, index)
    odd = lax.rem(key_half, 2) == 1
    slot = jnp.where(odd, 2 * CTX - key_half, key_half)
    diagonal = jnp.logical_or(index == first_half, index == 2 * CTX)
    return part, slot, diagonal


def visible_mask(rows):
    key_at = lax.broadcasted_iota(jnp.int32, (HALF, rows), 0)
    query_at = lax.rem(lax.broadcasted_iota(jnp.int32, (HALF, rows), 1), HALF)
    return key_at <= query_at


def forward_kernel(q_ref, kv_ref, out_ref, lse_ref, best, total, summed):
    first_half = 2 * lax.axis_index("ctx")
    best[...] = jnp.full(best.shape, -1e30, f32)
    total[...] = jnp.zeros(total.shape, f32)
    summed[...] = jnp.zeros(summed.shape, f32)

    def work(part, slot, masked):
        kv = kv_ref[slot]
        scores = contract(kv, q_ref[part], 1, 1)
        if masked:
            scores = jnp.where(visible_mask(scores.shape[1]), scores, -jnp.inf)
        old = best[part]
        new = jnp.maximum(old, jnp.max(scores, axis=0, keepdims=True))
        weights = jnp.exp2(scores * log2_e - new * log2_e)
        fading = jnp.exp2((old - new) * log2_e)
        total[part] = total[part] * fading + jnp.sum(weights, axis=0, keepdims=True)
        summed[part] = summed[part] * fading + contract(kv, weights.astype(bf16), 0, 0)
        best[part] = new

    def step(index, carry):
        part, slot, diagonal = unit(index, first_half)

        @pl.when(diagonal)
        def _():
            work(part, slot, True)

        @pl.when(jnp.logical_not(diagonal))
        def _():
            work(part, slot, False)

        return carry

    lax.fori_loop(0, 2 * CTX + 1, step, 0)
    for part in range(2):
        out_ref[part] = summed[part][HEAD:, :] / total[part]
        lse_ref[part] = best[part] + jnp.log(total[part])


def attention(q_rows, kv_all):
    rows = q_rows.shape[1]
    return pl.pallas_call(
        forward_kernel,
        out_shape=[shape((2, HEAD, rows), f32), shape((2, 1, rows), f32)],
        in_specs=[VM, VM],
        out_specs=[VM, VM],
        scratch_shapes=[
            pltpu.VMEM((2, 1, rows), f32),
            pltpu.VMEM((2, 1, rows), f32),
            pltpu.VMEM((2, 2 * HEAD, rows), f32),
        ],
        compiler_params=pltpu.CompilerParams(vmem_limit_bytes=VMEM_LIMIT),
        cost_estimate=pl.CostEstimate(
            flops=33 * 4 * HALF * rows * 256, bytes_accessed=1 << 23, transcendentals=33 * HALF * rows
        ),
    )(q_rows, kv_all)


def backward_kernel(q_ref, do_ref, lse_ref, delta_ref, kv_ref, dkv_ref, dq_ref, total):
    first_half = 2 * lax.axis_index("ctx")
    dq_ref[...] = jnp.zeros(dq_ref.shape, f32)

    def clear(index, carry):
        total[index] = jnp.zeros(total.shape[1:], f32)
        return carry

    lax.fori_loop(0, 2 * CTX, clear, 0)

    def work(part, slot, masked):
        kv = kv_ref[slot]
        queries = q_ref[part]
        grads = do_ref[part]
        scores = contract(kv, queries, 1, 1)
        probs = jnp.exp2((scores - lse_ref[part]) * log2_e)
        if masked:
            probs = jnp.where(visible_mask(scores.shape[1]), probs, 0.0)
        prob_grad = contract(kv, grads, 1, 1)
        score_grad = (probs * (prob_grad - delta_ref[part])).astype(bf16)
        total[slot] += contract(probs.astype(bf16), grads, 1, 0) + contract(
            score_grad, queries, 1, 0
        )
        dq_ref[part] += contract(kv, score_grad, 0, 0)

    def step(index, carry):
        part, slot, diagonal = unit(index, first_half)

        @pl.when(diagonal)
        def _():
            work(part, slot, True)

        @pl.when(jnp.logical_not(diagonal))
        def _():
            work(part, slot, False)

        return carry

    lax.fori_loop(0, 2 * CTX + 1, step, 0)

    def write(index, carry):
        dkv_ref[index] = total[index].astype(bf16)
        return carry

    lax.fori_loop(0, 2 * CTX, write, 0)


def attention_back(q_rows, do_rows, lse, delta, kv_all):
    rows = q_rows.shape[1]
    return pl.pallas_call(
        backward_kernel,
        out_shape=[shape(kv_all.shape, bf16), shape((2, 2 * HEAD, rows), f32)],
        in_specs=[VM] * 5,
        out_specs=[VM] * 2,
        scratch_shapes=[pltpu.VMEM(kv_all.shape, f32)],
        compiler_params=pltpu.CompilerParams(vmem_limit_bytes=VMEM_LIMIT),
        cost_estimate=pl.CostEstimate(
            flops=33 * 10 * HALF * rows * 256, bytes_accessed=1 << 24, transcendentals=33 * HALF * rows
        ),
    )(q_rows, do_rows, lse, delta, kv_all)


def phases(positions, head_width):
    steps_up = jnp.arange(head_width // 2).astype(f32)
    frequency = rope_base ** (-2.0 * steps_up / head_width)
    angles = positions.astype(f32)[:, None] * frequency[None, :]
    angles = jnp.concatenate([angles, angles], axis=1)
    return (jnp.cos(angles), jnp.sin(angles))


def rotate(values, cosine, sine):
    half_width = values.shape[-1] // 2
    turned = jnp.concatenate([-values[..., half_width:], values[..., :half_width]], axis=-1)
    return values * cosine + turned * sine


def rotate_back(grads, cosine, sine):
    half_width = grads.shape[-1] // 2
    turned = grads * sine
    turned = jnp.concatenate([turned[..., half_width:], -turned[..., :half_width]], axis=-1)
    return grads * cosine + turned


def normalize(values):
    inverse = lax.rsqrt(jnp.mean(values * values, axis=-1, keepdims=True) + epsilon)
    return (values * inverse, inverse)


def norm_back(grads, scaled, inverse, gain):
    inner = grads * gain
    return (
        inverse * (inner - scaled * jnp.mean(inner * scaled, axis=-1, keepdims=True)),
        jnp.sum(grads * scaled, axis=0),
    )


def swap_home(array):
    pairs = []
    for c in range(CTX):
        for m in range(MP):
            t = CTX - 1 - c if m >= MP // 2 else c
            pairs.append((c * MP + m, t * MP + m))
    return lax.ppermute(array, ("ctx", "mp"), pairs)


def sum_over_ctx(terms):
    c = lax.axis_index("ctx")
    chip, core = c // 2, lax.rem(c, 2)
    mine = lax.dynamic_index_in_dim(terms, core, 1, False)
    theirs = lax.dynamic_index_in_dim(terms, 1 - core, 1, False)
    got = lax.ppermute(theirs, "ctx", [(i, i ^ 1) for i in range(CTX)])
    pair = (mine.astype(f32) + got.astype(f32)).astype(bf16)
    total = lax.dynamic_index_in_dim(pair, chip, 0, False).astype(f32)
    for k in range(1, 8):
        piece = lax.dynamic_index_in_dim(pair, jnp.bitwise_xor(chip, k), 0, False)
        total = total + lax.ppermute(
            piece, "ctx", [(i, i ^ (2 * k)) for i in range(CTX)]
        ).astype(f32)
    return total


def heads_to_rows(values):
    return values.reshape(2, HALF, 2, HEAD).transpose(0, 2, 1, 3).reshape(2, 2 * HALF, HEAD)


def body(
    layer_input,
    positions,
    expert_ids,
    attn_gain,
    w_query,
    w_key,
    w_value,
    w_attn_out,
    ffn_gain,
    router,
    w_in,
    w_out,
    cotangent,
):
    c, m = place()
    in_w = lax.all_gather(w_in, "ctx", axis=1, tiled=True)
    out_expert = lax.all_gather(w_out, "ctx", axis=2, tiled=True)
    dy_all = lax.all_gather(swap_home(cotangent), "mp", axis=0, tiled=True)

    own_positions = lax.dynamic_slice_in_dim(positions, m * TOK, TOK, 0)
    id_pack = jnp.concatenate(
        [expert_ids.T, own_positions[None, :], jnp.zeros((7, TOK), jnp.int32)], axis=0
    )
    w_pack = jnp.concatenate(
        [
            w_query,
            w_key,
            w_value,
            router,
            attn_gain[:, None],
            ffn_gain[:, None],
            jnp.zeros((64, 94), bf16),
            w_attn_out.T,
        ],
        axis=1,
    )
    x_all, id_all, w_all = comm_call(
        start_kernel,
        1,
        [layer_input, id_pack, w_pack],
        [
            shape((MP, TOK, 1024)),
            shape((MP, 16, TOK), jnp.int32),
            shape((CTX, 64, 512)),
        ],
        [MP, MP, MP, MP, CTX, CTX, 3],
        4 << 20,
    )
    inputs = x_all.reshape(BLOCK, 1024).astype(f32)
    ids = id_all[:, :8, :].transpose(1, 0, 2).reshape(8, BLOCK)
    places = id_all[:, 8, :].reshape(BLOCK)
    w_all = w_all.reshape(1024, 512)
    qkv_w = w_all[:, :256]
    router_w = w_all[:, 256:288]
    gain_one = w_all[:, 288].astype(f32)
    gain_two = w_all[:, 289].astype(f32)
    out_w = w_all[:, 384:].T

    scaled_all, _ = normalize(inputs)
    normed = (scaled_all * gain_one).astype(bf16)
    qkv = jnp.dot(normed, qkv_w, preferred_element_type=f32)
    cosine, sine = phases(places, HEAD)
    cos2, sin2 = cosine[:, None, :], sine[:, None, :]
    queries = rotate(qkv[:, :128].reshape(BLOCK, 2, HEAD), cos2, sin2).astype(bf16)
    queries = queries * jnp.asarray(score_scale, bf16)
    q_rows = heads_to_rows(queries.reshape(BLOCK, 128))
    q_rows = jnp.concatenate([q_rows, jnp.zeros_like(q_rows)], axis=-1)
    keys = rotate(qkv[:, 128:192], cosine, sine).astype(bf16)
    kv_new = jnp.concatenate([keys, qkv[:, 192:].astype(bf16)], axis=-1)
    kv_all, out_w_all = comm_call(
        keys_kernel,
        2,
        [kv_new, out_w],
        [shape((CTX, BLOCK, 128)), shape((MP, 128, 1024))],
        [8, 8, 8, 8, MP, MP, 2],
        8 << 20,
    )
    kv_all = kv_all.reshape(2 * CTX, HALF, 128)
    out_cols, lse = attention(q_rows, kv_all)
    attended = (
        out_cols.reshape(2, HEAD, 2, HALF).transpose(0, 3, 2, 1).reshape(BLOCK, 128)
    )
    out_rows = attended.astype(bf16)
    (rows_all,) = comm_call(
        gather_kernel, 3, [out_rows], [shape((MP, BLOCK, 128))], [MP, MP, 1], 4 << 20
    )
    branch = lax.dot_general(
        rows_all, out_w_all, (((0, 2), (0, 1)), ((), ())), preferred_element_type=f32
    )
    hidden = inputs + branch_scale * branch
    scaled_two, inverse_two = normalize(hidden)
    routed = (scaled_two * gain_two).astype(bf16)

    logits = contract(router_w, routed, 0, 1)
    experts = lax.broadcasted_iota(jnp.int32, (32, BLOCK), 0)
    member = jnp.any(ids[:, None, :] == experts[None], axis=0)
    chosen = jnp.where(member, logits, -jnp.inf)
    top_logit = jnp.max(chosen, axis=0, keepdims=True)
    powers = jnp.exp(chosen - top_logit)
    gates = powers / jnp.sum(powers, axis=0, keepdims=True)

    here = 4 * m + lax.broadcasted_iota(jnp.int32, (4, BLOCK), 0)
    selected = jnp.any(ids[:, None, :] == here[None], axis=0)
    earlier = (
        lax.broadcasted_iota(jnp.int32, (BLOCK, BLOCK), 0)
        <= lax.broadcasted_iota(jnp.int32, (BLOCK, BLOCK), 1)
    ).astype(bf16)
    counts = jnp.dot(selected.astype(bf16), earlier, preferred_element_type=f32)
    rank = jnp.where(selected, counts.astype(jnp.int32) - 1, -1)
    capacity = 288
    place_bool = rank[:, None, :] == lax.broadcasted_iota(jnp.int32, (4, capacity, BLOCK), 1)
    placing = place_bool.astype(bf16).reshape(4 * capacity, BLOCK)
    gates_here = lax.dynamic_slice_in_dim(gates, 4 * m, 4, 0)
    slot_gate = jnp.sum(jnp.where(place_bool, gates_here[:, None, :], 0.0), axis=2)

    incoming = jnp.dot(placing, routed, preferred_element_type=f32).astype(bf16)
    incoming = incoming.reshape(4, capacity, 1024)
    dy_rows = jnp.dot(placing, dy_all, preferred_element_type=f32).reshape(4, capacity, 1024)
    gate_up = jnp.einsum("esd,edf->esf", incoming, in_w, preferred_element_type=f32)
    gate_part, up_part = gate_up[..., :512], gate_up[..., 512:]
    squashed = jax.nn.sigmoid(gate_part)
    silu_part = gate_part * squashed
    active = (silu_part * up_part).astype(bf16)
    produced = jnp.einsum(
        "esf,efd->esd", active, out_expert, preferred_element_type=f32
    ).astype(bf16)
    produced_f = produced.astype(f32)
    d_produced = (branch_scale * slot_gate[..., None] * dy_rows).astype(bf16)
    slot_share = branch_scale * jnp.sum(dy_rows * produced_f, axis=2)
    weighted = (slot_gate[..., None] * produced_f).astype(bf16).reshape(4 * capacity, 1024)
    mixed = branch_scale * contract(placing, weighted, 0, 0)
    mixed = mixed.astype(bf16).reshape(MP, TOK, 1024)

    d_active = jnp.einsum("esd,efd->esf", d_produced, out_expert, preferred_element_type=f32)
    slope = squashed * (1.0 + gate_part * (1.0 - squashed))
    d_gate_up = jnp.concatenate(
        [d_active * up_part * slope, d_active * silu_part], axis=-1
    ).astype(bf16)
    row_grads = jnp.einsum(
        "esf,edf->esd", d_gate_up, in_w, preferred_element_type=f32
    ).astype(bf16)
    routed_terms = contract(placing, row_grads.reshape(4 * capacity, 1024), 0, 0)
    routed_terms = routed_terms.astype(bf16).reshape(MP, TOK, 1024)
    share = jnp.sum(jnp.where(place_bool, slot_share[:, :, None], 0.0), axis=1)
    share = jnp.pad(share.reshape(4, MP, TOK).transpose(1, 0, 2), ((0, 0), (0, 4), (0, 0)))
    routed_got, share_got = comm_call(
        scatter_kernel,
        4,
        [routed_terms, share],
        [shape((MP, TOK, 1024)), shape((MP, 8, TOK), f32)],
        [MP, MP, MP, MP, 2],
        4 << 20,
    )

    def own_rows(array):
        return lax.dynamic_slice_in_dim(array, m * TOK, TOK, 0)

    hidden_own = own_rows(hidden)
    scaled_own, inverse_own = normalize(hidden_own)
    routed_own = (scaled_own * gain_two).astype(bf16).astype(f32)
    dy_own = own_rows(dy_all).astype(f32)
    gates_own = lax.dynamic_slice_in_dim(gates, m * TOK, TOK, 1)
    share_own = share_got[:, :4, :].reshape(32, TOK)
    logit_grad = gates_own * (
        share_own - jnp.sum(gates_own * share_own, axis=0, keepdims=True)
    )
    routed_grad = jnp.sum(routed_got.astype(f32), axis=0) + lax.dot_general(
        logit_grad,
        router_w.astype(f32),
        (((0,), (1,)), ((), ())),
        precision=highest,
        preferred_element_type=f32,
    )
    router_grad = lax.dot_general(
        routed_own,
        logit_grad,
        (((0,), (1,)), ((), ())),
        precision=highest,
        preferred_element_type=f32,
    )
    hidden_grad, gain_two_grad = norm_back(routed_grad, scaled_own, inverse_own, gain_two)
    hidden_grad = hidden_grad + dy_own
    branch_grad = (branch_scale * hidden_grad).astype(bf16)
    (branch_rows,) = comm_call(
        gather_kernel, 5, [branch_grad], [shape((MP, TOK, 1024))], [MP, MP, 1], 4 << 20
    )
    branch_rows = branch_rows.reshape(BLOCK, 1024)
    hidden_grad_home = swap_home(hidden_grad)

    out_expert_grad = jnp.einsum(
        "esf,esd->efd", active, d_produced, preferred_element_type=f32
    ).astype(bf16)
    in_expert_grad = jnp.einsum(
        "esd,esf->edf", incoming, d_gate_up, preferred_element_type=f32
    ).astype(bf16)
    in_terms = in_expert_grad.reshape(4, 8, 2, 64, 1024).transpose(1, 2, 0, 3, 4)
    out_terms = out_expert_grad.reshape(4, 512, 8, 2, 64).transpose(2, 3, 0, 1, 4)
    expert_in = sum_over_ctx(in_terms.reshape(8, 2, 4 * 64, 1024)).reshape(4, 64, 1024)
    expert_out = sum_over_ctx(out_terms.reshape(8, 2, 4 * 512, 64)).reshape(4, 512, 64)

    mixed_got = lax.all_to_all(mixed, "mp", split_axis=0, concat_axis=0, tiled=True)
    outputs = (hidden_own + jnp.sum(mixed_got.astype(f32), axis=0)).astype(bf16)
    outputs = swap_home(outputs)

    out_grad = contract(branch_rows, out_w, 1, 1).astype(bf16)
    do_rows = heads_to_rows(out_grad)
    delta = jnp.sum(do_rows.astype(f32) * heads_to_rows(attended), axis=-1)[:, None, :]
    do_rows = jnp.concatenate([jnp.zeros_like(do_rows), do_rows], axis=-1)
    dkv_terms, dq_cols = attention_back(q_rows, do_rows, lse, delta, kv_all)
    dkv_terms = dkv_terms.reshape(8, 2, BLOCK, 128)
    (theirs,) = comm_call(
        sibling_kernel, 6, [dkv_terms], [shape((8, BLOCK, 128))], [1, 1], 4 << 20
    )
    mine = lax.dynamic_index_in_dim(dkv_terms, lax.rem(c, 2), 1, False)
    pair = (mine.astype(f32) + theirs.astype(f32)).astype(bf16)
    (dkv_got,) = comm_call(
        chips_kernel, 7, [pair], [shape((8, BLOCK, 128))], [8, 8, 1], 4 << 20
    )
    dkv = jnp.sum(dkv_got.astype(f32), axis=0)
    d_key = rotate_back(dkv[:, :HEAD], cosine, sine).astype(bf16)
    d_value = dkv[:, HEAD:].astype(bf16)
    dq = score_scale * dq_cols[:, :HEAD, :]
    dq = dq.reshape(2, HEAD, 2, HALF).transpose(0, 3, 2, 1).reshape(BLOCK, 2, HEAD)
    d_query = rotate_back(dq, cos2, sin2).reshape(BLOCK, 128).astype(bf16)
    d_qkv = jnp.concatenate([d_query, d_key, d_value], axis=1)
    qkv_w_grad = contract(normed, d_qkv, 0, 0)
    out_w_grad = contract(branch_rows, out_rows, 0, 0)
    w_terms = jnp.concatenate([qkv_w_grad, out_w_grad], axis=1).astype(bf16)
    normed_terms = contract(d_qkv, qkv_w, 1, 1).astype(bf16).reshape(MP, TOK, 1024)
    normed_got, w_got = comm_call(
        finish_kernel,
        8,
        [normed_terms, w_terms.reshape(CTX, 64, 384)],
        [shape((MP, TOK, 1024)), shape((CTX, 64, 384))],
        [MP, MP, CTX, CTX, 2],
        5 << 20,
    )
    w_grad = jnp.sum(w_got.astype(f32), axis=0)
    normed_grad = jnp.sum(normed_got.astype(f32), axis=0)
    scaled_one, inverse_one = normalize(layer_input.astype(f32))
    input_grad, gain_one_grad = norm_back(normed_grad, scaled_one, inverse_one, gain_one)
    input_grad = (input_grad + hidden_grad_home).astype(bf16)

    small = jnp.concatenate(
        [
            router_grad,
            gain_one_grad[:, None],
            gain_two_grad[:, None],
            jnp.zeros((1024, 94), f32),
        ],
        axis=1,
    )
    sums = small_sums(small.reshape(CTX, MP, 8, 128))
    return (
        outputs,
        input_grad,
        sums[:, 32],
        w_grad[:, :128],
        w_grad[:, 128:192],
        w_grad[:, 192:256],
        w_grad[:, 256:].T,
        sums[:, 33],
        sums[:, :32],
        expert_in,
        expert_out,
    )


def solution(mesh):
    placed = (
        P(("ctx", "mp"), None),
        P("ctx"),
        P(("ctx", "mp"), None),
        P("ctx"),
        P("ctx", "mp"),
        P("ctx", "mp"),
        P("ctx", "mp"),
        P("mp", "ctx"),
        P("ctx"),
        P("ctx", None),
        P("mp", "ctx", None),
        P("mp", None, "ctx"),
        P(("ctx", "mp"), None),
    )
    return jax.shard_map(
        body,
        mesh=mesh,
        in_specs=placed,
        out_specs=(
            P(("ctx", "mp"), None),
            P(("ctx", "mp"), None),
            P(("ctx", "mp")),
            P("ctx", "mp"),
            P("ctx", "mp"),
            P("ctx", "mp"),
            P("mp", "ctx"),
            P(("ctx", "mp")),
            P(("ctx", "mp"), None),
            P("mp", "ctx", None),
            P("mp", None, "ctx"),
        ),
        check_vma=False,
    )
```

time: 1750 us -> 846 us (0.48)
  waiting for transfers between devices: 1160 us -> 99.1 us
  Pallas kernels: 0 us -> 454 us
  blocking collectives: 238 us -> 0 us
  matrix products: 118 us -> 82.8 us
  loops' own time: 22.7 us -> 0 us
  local copies, waits for them, and re-layouts: 103 us -> 85.5 us
    reduce_scatter x9 -> x0, waiting for transfers between devices: 879 us -> none  [the longest x1 218 us: body(): lax.psum_scatter(key_terms.reshape(total_keys, 2 * head_width).astype(jnp...]
    pallas_call x0 -> x11, Pallas kernels: none -> 454 us  [the longest x8 322 us: comm_call(): pl.pallas_call(kernel, out_shape=outs, in_specs=[ANY] * len(arrays), out_...]
    all_gather x5 -> x0, blocking collectives: 145 us -> none  [the longest x1 68.5 us: body(): lax.all_gather(router, 'ctx', axis=0, tiled=True)]
    unnamed x17 -> x3, waiting for transfers between devices: 128 us -> 1.39 us
    unnamed x2 -> x0, blocking collectives: 93.2 us -> none
    all_gather x6 -> x3, waiting for transfers between devices: 106 us -> 31.9 us  [the longest x1 31.9 us: body(): dy_all = lax.all_gather(swap_home(cotangent), 'mp', axis=0, tiled=True)]
    ppermute x0 -> x19, waiting for transfers between devices: none -> 65.8 us  [the longest x14 62.7 us: sum_over_ctx(): lax.ppermute(piece, 'ctx', [(i, i ^ 2 * k) for i in range(CTX)]).astype(f32)]
    all_to_all x4 -> x1, waiting for transfers between devices: 44.5 us -> 0.01 us  [body(): lax.all_to_all(mixed, 'mp', split_axis=0, concat_axis=0, tiled=True)]
  transfers between devices with their start and end apart: 20 -> 23, of which waited for: 17 -> 10; matrix products, arithmetic and copies ran while one was open for 7% -> 25% of each run, Pallas kernels for 0% -> 54%
where the time goes in v1:
time: 846 us; the launch traced here: 839 us
  Pallas kernels  454 us (54%)
  waiting for transfers between devices  99.1 us (12%)
  local copies, waits for them, and re-layouts  85.5 us (10%)
  matrix products  82.8 us (10%)
  other arithmetic  60.9 us (7%)
  starting transfers between devices  41.7 us (5%)
  between operations  15 us (2%)
    pallas_call x8, Pallas kernels, comm_call(): pl.pallas_call(kernel, out_shape=outs, in_specs=[ANY] * len(arrays), out_...  322 us
    ppermute x14, waiting for transfers between devices, sum_over_ctx(): lax.ppermute(piece, 'ctx', [(i, i ^ 2 * k) for i in range(CTX)]).astype(f32)  62.7 us
    pallas_call x1, Pallas kernels, attention_back(): pl.pallas_call(backward_kernel, out_shape=[shape(kv_all.shape, bf16), sha...  53.9 us
    pallas_call x1, Pallas kernels, attention(): pl.pallas_call(forward_kernel, out_shape=[shape((2, HEAD, rows), f32), sh...  39.7 us
    pallas_call x1, Pallas kernels, small_sums(): pl.pallas_call(sums_kernel, out_shape=shape(dims, f32), in_specs=[VM], ou...  38 us
    all_gather x1, waiting for transfers between devices, body(): dy_all = lax.all_gather(swap_home(cotangent), 'mp', axis=0, tiled=True)  31.9 us
    dot_general x7, matrix products, contract(): lax.dot_general(left, right, (((left_dim,), (right_dim,)), ((), ())), pre...  26.2 us
    ppermute x3, starting transfers between devices, swap_home(): return lax.ppermute(array, ('ctx', 'mp'), pairs)  18.4 us
  transfers between devices with their start and end apart: 23, of which 10 were waited for; matrix products, arithmetic and copies ran while one was open for 25% of the time, Pallas kernels for 54%

profile of v1, /device:TPU:65, one launch (start us, length us, event | category | flops | bytes accessed | tf_op | source)
XLA Modules:
  0.0 838.8 jit_solution(10891096747672315186)
XLA Ops:
  20.0 65.0 %shard_map.212 = (bf16[8,128,1024]{2,1,0:T(8,128)(2,1)}, s32[8,16,128]{2,1,0:T(8,128)}, bf16[16,64,512]{2,1,0:T(8,128)(2,1)}) custom-call(bf16[128,1024]{1,0:T(8,128)(2,1)} %x_ref.1, s32[16,128]{1,0:T(8,128)} %add_add_fusion.id_ref, bf16[64,512]{1,0:T(8,128)(2,1)} %concatenate.72.w_ref), custom_call_target="tpu_custom_call" | custom-call | bytes 4194304 | tf_op jit(solution)/shard_map/pallas_call | solution.py:54
  116.4 87.6 %shard_map.213 = (bf16[16,1024,128]{2,1,0:T(8,128)(2,1)}, bf16[8,128,1024]{2,1,0:T(8,128)(2,1)}) custom-call(bf16[1024,128]{1,0:T(8,128)(2,1)} %pad_maximum_fusion.12.kv_ref, bf16[128,1024]{1,0:T(8,128)(2,1)} %bitcast.218), custom_call_target="tpu_custom_call" | custom-call | bytes 8388608 | tf_op jit(solution)/shard_map/pallas_call | solution.py:54
  204.1 39.7 %shard_map.214 = (f32[2,64,1024]{2,1,0:T(8,128)}, f32[2,1,1024]{2,1,0:T(1,128)}) custom-call(bf16[2,1024,128]{2,1,0:T(8,128)(2,1)} %concatenate.77.q_ref, bf16[32,512,128]{2,1,0:T(8,128)(2,1)} %bitcast.232), custom_call_target="tpu_custom_call" | custom-call | flops 17716740096 | bytes 8388608 | tf_op jit(solution)/shard_map/pallas_call | solution.py:408
  246.5 27.3 %shard_map.215 = bf16[8,1024,128]{2,1,0:T(8,128)(2,1)} custom-call(bf16[1024,128]{1,0:T(8,128)(2,1)} %copy.149.a_ref), custom_call_target="tpu_custom_call" | custom-call | bytes 4194304 | tf_op jit(solution)/shard_map/pallas_call | solution.py:54
  274.3 7.2 multiply_reduce_fusion
  310.6 31.9 %all-gather.8.cloned.1.call-done = bf16[1024,1024]{1,0:T(8,128)(2,1)} async-done(((bf16[128,1024]{1,0:T(8,128)(2,1)}), bf16[1024,1024]{1,0:T(8,128)(2,1)}) %all-gather.8.cloned.1.call-update) | async-done | bytes 2097168 | tf_op jit(solution)/shard_map/all_gather | solution.py:568
  342.5 6.4 fusion.2
  362.2 7.0 convolution_convert_fusion.2
  369.2 7.3 multiply_convert_fusion.3
  376.4 10.8 %bitcast_convert_fusion = bf16[1024,1024]{1,0:T(8,128)(2,1)} fusion(s32[4,1024]{1,0:T(4,128)S(1)} %copy-done.30, bf16[4,1024,1024]{2,1,0:T(8,128)(2,1)} %all-gather.4.cloned.1.call-done, bf16[4,288,512]{2,1,0:T(8,128)(2,1)} %get-tuple-element.94, bf16[4,288,512]{2,1,0:T(8,128)(2,1)} %get-tuple-element.93), kind=kOutput, calls=%fused_computation.19 | convolution fusion | flops 4839964672 | bytes 12861440 | tf_op jit(solution)/shard_map/dot_general | solution.py:30
  387.3 30.0 %shard_map.216 = (bf16[8,128,1024]{2,1,0:T(8,128)(2,1)}, f32[8,8,128]{2,1,0:T(8,128)}) custom-call(bf16[8,128,1024]{2,1,0:T(8,128)(2,1)} %bitcast.209, f32[8,8,128]{2,1,0:T(8,128)} %pad.6.b_ref), custom_call_target="tpu_custom_call" | custom-call | bytes 4194304 | tf_op jit(solution)/shard_map/pallas_call | solution.py:54
  437.7 8.2 convolution_convert_fusion
  446.0 8.4 %copy.168 = bf16[4,8,2,64,1024]{4,3,0,2,1:T(8,128)(2,1)} copy(bf16[4,8,2,64,1024]{4,3,2,1,0:T(8,128)(2,1)} %bitcast.191) | data formatting | bytes 16777216 | tf_op jit(solution)/shard_map/reshape | solution.py:746
  464.1 29.6 %shard_map.217 = bf16[8,128,1024]{2,1,0:T(8,128)(2,1)} custom-call(bf16[128,1024]{1,0:T(8,128)(2,1)} %get-tuple-element.91.a_ref), custom_call_target="tpu_custom_call" | custom-call | bytes 4194304 | tf_op jit(solution)/shard_map/pallas_call | solution.py:54
  498.9 53.9 %shard_map.218 = (bf16[32,512,128]{2,1,0:T(8,128)(2,1)}, f32[2,128,1024]{2,1,0:T(8,128)}) custom-call(bf16[2,1024,128]{2,1,0:T(8,128)(2,1)} %concatenate.77.q_ref, bf16[2,1024,128]{2,1,0:T(8,128)(2,1)} %concatenate.82.do_ref, f32[2,1,1024]{2,1,0:T(1,128)} %get-tuple-element.32.lse_ref, f32[2,1,1024]{2,1,0:T(1,128)} %broadcast_in_dim.51.delta_ref, ...), custom_call_target="tpu_custom_call" | custom-call | flops 44291850240 | bytes 16777216 | tf_op jit(solution)/shard_map/pallas_call | solution.py:474
  561.5 31.2 %shard_map.220 = bf16[8,1024,128]{2,1,0:T(8,128)(2,1)} custom-call(bf16[8,1024,128]{2,1,0:T(8,128)(2,1)} %fusion.7.a_ref), custom_call_target="tpu_custom_call" | custom-call | bytes 4194304 | tf_op jit(solution)/shard_map/pallas_call | solution.py:54
  636.4 46.8 %shard_map.221 = (bf16[8,128,1024]{2,1,0:T(8,128)(2,1)}, bf16[16,64,384]{2,1,0:T(8,128)(2,1)}) custom-call(bf16[8,128,1024]{2,1,0:T(8,128)(2,1)} %bitcast.194, bf16[16,64,384]{2,1,0:T(8,128)(2,1)} %pad_maximum_fusion.7.g_ref), custom_call_target="tpu_custom_call" | custom-call | bytes 5242880 | tf_op jit(solution)/shard_map/pallas_call | solution.py:54
  687.1 38.0 %shard_map.222 = f32[8,128]{1,0:T(8,128)} custom-call(f32[16,8,8,128]{3,2,1,0:T(8,128)} %maximum_maximum_fusion.a_ref), custom_call_target="tpu_custom_call" | custom-call | tf_op jit(solution)/shard_map/pallas_call | solution.py:334
  745.4 6.4 collective-permute-start.2
  760.2 7.9 collective-permute-done.14
  777.2 18.4 %collective-permute-done.4 = bf16[256,1024]{1,0:T(8,128)(2,1)S(1)} collective-permute-done((bf16[256,1024]{1,0:T(8,128)(2,1)S(1)}, bf16[256,1024]{1,0:T(8,128)(2,1)S(1)}, u32[]{:S(2)}, u32[]{:S(2)}) %collective-permute-start.4) | collective-permute-done | bytes 524320 | tf_op jit(solution)/shard_map/ppermute | solution.py:540
  799.0 10.5 %collective-permute-done.10 = bf16[256,1024]{1,0:T(8,128)(2,1)S(1)} collective-permute-done((bf16[256,1024]{1,0:T(8,128)(2,1)S(1)}, bf16[256,1024]{1,0:T(8,128)(2,1)S(1)}, u32[]{:S(2)}, u32[]{:S(2)}) %collective-permute-start.10) | collective-permute-done | bytes 524320 | tf_op jit(solution)/shard_map/ppermute | solution.py:540
  812.1 6.4 collective-permute-done.9
  818.5 9.5 %collective-permute-done.5 = bf16[256,1024]{1,0:T(8,128)(2,1)S(1)} collective-permute-done((bf16[256,1024]{1,0:T(8,128)(2,1)S(1)}, bf16[256,1024]{1,0:T(8,128)(2,1)S(1)}, u32[]{:S(2)}, u32[]{:S(2)}) %collective-permute-start.5) | collective-permute-done | bytes 524320 | tf_op jit(solution)/shard_map/ppermute | solution.py:540
  (265 shorter events, 228.3 us)
Async XLA Ops:
  7.2 289.7 %all-gather.4.cloned.1.call-start = ((), (), s32[]{:S(2)}) async-start(), calls=%async_computation.1 | async-start | bytes 8912896 | tf_op jit(solution)/shard_map/all_gather | solution.py:566
  7.9 297.7 %all-gather.6.cloned.1.call-start = ((), (), s32[]{:S(2)}) async-start(), calls=%async_computation.2 | async-start | bytes 4456448 | tf_op jit(solution)/shard_map/all_gather | solution.py:567
  8.7 333.8 %all-gather.8.cloned.1.call-start = ((), (), s32[]{:S(2)}) async-start(), calls=%async_computation.3 | async-start | bytes 2359296 | tf_op jit(solution)/shard_map/all_gather | solution.py:568
  8.7 279.5 %collective-permute-start.1 = (bf16[128,1024]{1,0:T(8,128)(2,1)}, bf16[128,1024]{1,0:T(8,128)(2,1)}, u32[]{:S(2)}, u32[]{:S(2)}) collective-permute-start(bf16[128,1024]{1,0:T(8,128)(2,1)} %param.25), channel_id=1, source_target_pairs={{0,0},{1,1},{2,2},{3,3},{4,124},{5,125},{6,126},{7,127},{8,8},{9,9... | collective-permute-start | bytes 786440 | tf_op jit(solution)/shard_map/ppermute | solution.py:527
  274.3 76.6 %copy-start.29 = (s32[4,1024]{1,0:T(4,128)}, s32[4,1024]{1,0:T(4,128)S(1)}, u32[]{:S(2)}) copy-start(s32[4,1024]{1,0:T(4,128)S(1)} %fusion.29) | copy-start | bytes 49156
  355.3 106.0 %all-to-all-start = ((bf16[8,128,1024]{2,1,0:T(8,128)(2,1)}), bf16[8,128,1024]{2,1,0:T(8,128)(2,1)S(1)}, u32[]{:S(2)}, u32[]{:S(2)}) async-start(bf16[8,128,1024]{2,1,0:T(8,128)(2,1)} %bitcast.208), calls=%async_computation | async-start | bytes 4194304 | tf_op jit(solution)/shard_map/all_to_all | solution.py:751
  437.2 288.6 %collective-permute-start.11 = (bf16[8,2048,64]{1,2,0:T(8,128)(2,1)}, bf16[8,2048,64]{1,2,0:T(8,128)(2,1)}, u32[]{:S(2)}, u32[]{:S(2)}) collective-permute-start(bf16[8,2048,64]{1,2,0:T(8,128)(2,1)} %dynamic-slice_bitcast_fusion.1), channel_id=1, source_target_pairs={{0,8},{8,0},{16,24},{24,16},{32,40},{40,32},{48,56},{56,48},{64,72... | collective-permute-start | bytes 6291464 | tf_op jit(solution)/shard_map/ppermute | solution.py:535
  458.9 274.1 %collective-permute-start.3 = (bf16[8,256,1024]{2,1,0:T(8,128)(2,1)}, bf16[8,256,1024]{2,1,0:T(8,128)(2,1)}, u32[]{:S(2)}, u32[]{:S(2)}) collective-permute-start(bf16[8,256,1024]{2,1,0:T(8,128)(2,1)} %dynamic-slice_bitcast_fusion), channel_id=1, source_target_pairs={{0,8},{8,0},{16,24},{24,16},{32,40},{40,32},{48,56},{56,48},{64,72... | collective-permute-start | bytes 12582920 | tf_op jit(solution)/shard_map/ppermute | solution.py:535
  598.5 142.0 %collective-permute-start = (bf16[128,1024]{1,0:T(8,128)(2,1)}, bf16[128,1024]{1,0:T(8,128)(2,1)}, u32[]{:S(2)}, u32[]{:S(2)}) collective-permute-start(bf16[128,1024]{1,0:T(8,128)(2,1)} %get-tuple-element.102), channel_id=1, source_target_pairs={{0,0},{1,1},{2,2},{3,3},{4,124},{5,125},{6,126},{7,127},{8,8},{9,9... | collective-permute-start | bytes 786440 | tf_op jit(solution)/shard_map/ppermute | solution.py:527
  729.1 16.3 %collective-permute-start.12 = (bf16[2048,64]{0,1:T(8,128)(2,1)S(1)}, bf16[2048,64]{0,1:T(8,128)(2,1)S(1)}, u32[]{:S(2)}, u32[]{:S(2)}) collective-permute-start(bf16[2048,64]{0,1:T(8,128)(2,1)S(1)} %get-tuple-element.103), channel_id=1, source_target_pairs={{0,16},{8,24},{16,0},{24,8},{32,48},{40,56},{48,32},{56,40},{64,80... | collective-permute-start | bytes 786440 | tf_op jit(solution)/shard_map/ppermute | solution.py:540
  730.4 21.4 %collective-permute-start.18 = (bf16[2048,64]{0,1:T(8,128)(2,1)S(1)}, bf16[2048,64]{0,1:T(8,128)(2,1)S(1)}, u32[]{:S(2)}, u32[]{:S(2)}) collective-permute-start(bf16[2048,64]{0,1:T(8,128)(2,1)S(1)} %get-tuple-element.104), channel_id=1, source_target_pairs={{0,112},{8,120},{16,96},{24,104},{32,80},{40,88},{48,64},{56,72},{... | collective-permute-start | bytes 786440 | tf_op jit(solution)/shard_map/ppermute | solution.py:540
  731.4 23.5 %collective-permute-start.17 = (bf16[2048,64]{0,1:T(8,128)(2,1)S(1)}, bf16[2048,64]{0,1:T(8,128)(2,1)S(1)}, u32[]{:S(2)}, u32[]{:S(2)}) collective-permute-start(bf16[2048,64]{0,1:T(8,128)(2,1)S(1)} %get-tuple-element.105), channel_id=1, source_target_pairs={{0,96},{8,104},{16,112},{24,120},{32,64},{40,72},{48,80},{56,88},{... | collective-permute-start | bytes 786440 | tf_op jit(solution)/shard_map/ppermute | solution.py:540
  733.1 24.1 %collective-permute-start.16 = (bf16[2048,64]{0,1:T(8,128)(2,1)S(1)}, bf16[2048,64]{0,1:T(8,128)(2,1)S(1)}, u32[]{:S(2)}, u32[]{:S(2)}) collective-permute-start(bf16[2048,64]{0,1:T(8,128)(2,1)S(1)} %get-tuple-element.106), channel_id=1, source_target_pairs={{0,80},{8,88},{16,64},{24,72},{32,112},{40,120},{48,96},{56,104},{... | collective-permute-start | bytes 786440 | tf_op jit(solution)/shard_map/ppermute | solution.py:540
  740.6 16.6 %collective-permute-start.15 = (bf16[2048,64]{0,1:T(8,128)(2,1)S(1)}, bf16[2048,64]{0,1:T(8,128)(2,1)S(1)}, u32[]{:S(2)}, u32[]{:S(2)}) collective-permute-start(bf16[2048,64]{0,1:T(8,128)(2,1)S(1)} %get-tuple-element.107), channel_id=1, source_target_pairs={{0,64},{8,72},{16,80},{24,88},{32,96},{40,104},{48,112},{56,120},{... | collective-permute-start | bytes 786440 | tf_op jit(solution)/shard_map/ppermute | solution.py:540
  745.4 31.0 %collective-permute-start.2 = (f32[128,1024]{1,0:T(8,128)S(1)}, f32[128,1024]{1,0:T(8,128)S(1)}, u32[]{:S(2)}, u32[]{:S(2)}) collective-permute-start(f32[128,1024]{1,0:T(8,128)S(1)} %copy-done.26), channel_id=1, source_target_pairs={{0,0},{1,1},{2,2},{3,3},{4,124},{5,125},{6,126},{7,127},{8,8},{9,9... | collective-permute-start | bytes 1572872 | tf_op jit(solution)/shard_map/ppermute | solution.py:527
  751.8 43.8 %collective-permute-start.4 = (bf16[256,1024]{1,0:T(8,128)(2,1)S(1)}, bf16[256,1024]{1,0:T(8,128)(2,1)S(1)}, u32[]{:S(2)}, u32[]{:S(2)}) collective-permute-start(bf16[256,1024]{1,0:T(8,128)(2,1)S(1)} %get-tuple-element.95), channel_id=1, source_target_pairs={{0,16},{8,24},{16,0},{24,8},{32,48},{40,56},{48,32},{56,40},{64,80... | collective-permute-start | bytes 1572872 | tf_op jit(solution)/shard_map/ppermute | solution.py:540
  754.9 54.7 %collective-permute-start.10 = (bf16[256,1024]{1,0:T(8,128)(2,1)S(1)}, bf16[256,1024]{1,0:T(8,128)(2,1)S(1)}, u32[]{:S(2)}, u32[]{:S(2)}) collective-permute-start(bf16[256,1024]{1,0:T(8,128)(2,1)S(1)} %get-tuple-element.96), channel_id=1, source_target_pairs={{0,112},{8,120},{16,96},{24,104},{32,80},{40,88},{48,64},{56,72},{... | collective-permute-start | bytes 1572872 | tf_op jit(solution)/shard_map/ppermute | solution.py:540
  757.2 10.9 %collective-permute-start.14 = (bf16[2048,64]{0,1:T(8,128)(2,1)S(1)}, bf16[2048,64]{0,1:T(8,128)(2,1)S(1)}, u32[]{:S(2)}, u32[]{:S(2)}) collective-permute-start(bf16[2048,64]{0,1:T(8,128)(2,1)S(1)} %get-tuple-element.108), channel_id=1, source_target_pairs={{0,48},{8,56},{16,32},{24,40},{32,16},{40,24},{48,0},{56,8},{64,11... | collective-permute-start | bytes 786440 | tf_op jit(solution)/shard_map/ppermute | solution.py:540
  757.2 16.1 %collective-permute-start.13 = (bf16[2048,64]{0,1:T(8,128)(2,1)S(1)}, bf16[2048,64]{0,1:T(8,128)(2,1)S(1)}, u32[]{:S(2)}, u32[]{:S(2)}) collective-permute-start(bf16[2048,64]{0,1:T(8,128)(2,1)S(1)} %get-tuple-element.109), channel_id=1, source_target_pairs={{0,32},{8,40},{16,48},{24,56},{32,0},{40,8},{48,16},{56,24},{64,96... | collective-permute-start | bytes 786440 | tf_op jit(solution)/shard_map/ppermute | solution.py:540
  768.1 50.4 %collective-permute-start.9 = (bf16[256,1024]{1,0:T(8,128)(2,1)S(1)}, bf16[256,1024]{1,0:T(8,128)(2,1)S(1)}, u32[]{:S(2)}, u32[]{:S(2)}) collective-permute-start(bf16[256,1024]{1,0:T(8,128)(2,1)S(1)} %get-tuple-element.97), channel_id=1, source_target_pairs={{0,96},{8,104},{16,112},{24,120},{32,64},{40,72},{48,80},{56,88},{... | collective-permute-start | bytes 1572872 | tf_op jit(solution)/shard_map/ppermute | solution.py:540
  773.4 45.1 %collective-permute-start.8 = (bf16[256,1024]{1,0:T(8,128)(2,1)S(1)}, bf16[256,1024]{1,0:T(8,128)(2,1)S(1)}, u32[]{:S(2)}, u32[]{:S(2)}) collective-permute-start(bf16[256,1024]{1,0:T(8,128)(2,1)S(1)} %get-tuple-element.98), channel_id=1, source_target_pairs={{0,80},{8,88},{16,64},{24,72},{32,112},{40,120},{48,96},{56,104},{... | collective-permute-start | bytes 1572872 | tf_op jit(solution)/shard_map/ppermute | solution.py:540
  776.4 42.1 %collective-permute-start.7 = (bf16[256,1024]{1,0:T(8,128)(2,1)S(1)}, bf16[256,1024]{1,0:T(8,128)(2,1)S(1)}, u32[]{:S(2)}, u32[]{:S(2)}) collective-permute-start(bf16[256,1024]{1,0:T(8,128)(2,1)S(1)} %get-tuple-element.99), channel_id=1, source_target_pairs={{0,64},{8,72},{16,80},{24,88},{32,96},{40,104},{48,112},{56,120},{... | collective-permute-start | bytes 1572872 | tf_op jit(solution)/shard_map/ppermute | solution.py:540
  795.6 22.9 %collective-permute-start.6 = (bf16[256,1024]{1,0:T(8,128)(2,1)S(1)}, bf16[256,1024]{1,0:T(8,128)(2,1)S(1)}, u32[]{:S(2)}, u32[]{:S(2)}) collective-permute-start(bf16[256,1024]{1,0:T(8,128)(2,1)S(1)} %get-tuple-element.100), channel_id=1, source_target_pairs={{0,48},{8,56},{16,32},{24,40},{32,16},{40,24},{48,0},{56,8},{64,11... | collective-permute-start | bytes 1572872 | tf_op jit(solution)/shard_map/ppermute | solution.py:540
  809.6 18.5 %collective-permute-start.5 = (bf16[256,1024]{1,0:T(8,128)(2,1)S(1)}, bf16[256,1024]{1,0:T(8,128)(2,1)S(1)}, u32[]{:S(2)}, u32[]{:S(2)}) collective-permute-start(bf16[256,1024]{1,0:T(8,128)(2,1)S(1)} %get-tuple-element.101), channel_id=1, source_target_pairs={{0,32},{8,40},{16,48},{24,56},{32,0},{40,8},{48,16},{56,24},{64,96... | collective-permute-start | bytes 1572872 | tf_op jit(solution)/shard_map/ppermute | solution.py:540
  (39 other events, 377.4 us)
Sparse Core Ops, SparseCore 0:
  9.7 90.8 all-gather.3
  102.3 45.7 all-gather.5
  288.4 54.0 all-gather.7

commit v2 on v1

--- a/solution.py
+++ b/solution.py
@@ -56,7 +56,9 @@
         out_shape=outs,
         in_specs=[ANY] * len(arrays),
         out_specs=[ANY] * len(outs),
-        scratch_shapes=[pltpu.SemaphoreType.DMA((n,)) for n in sems],
+        scratch_shapes=[
+            pltpu.SemaphoreType.DMA((n,)) if isinstance(n, int) else n for n in sems
+        ],
         compiler_params=pltpu.CompilerParams(collective_id=number, has_side_effects=True),
         cost_estimate=pl.CostEstimate(flops=0, bytes_accessed=cost, transcendentals=0),
     )(*arrays)
@@ -64,6 +66,156 @@
 
 def shape(dims, kind=bf16):
     return jax.ShapeDtypeStruct(dims, kind)
+
+
+def flip(index, stride):
+    return index + stride - 2 * stride * lax.rem(index // stride, 2)
+
+
+class Ring:
+    def __init__(self, own, dst, index, spread, near, stride, target, sems, sibling=None):
+        send, recv, loc = sems[:3]
+        count = spread
+        plus, minus = lax.rem(index + stride, count), lax.rem(index + count - stride, count)
+        far = lax.rem(index + 2 * stride, count)
+        near_of = lambda slot: flip(slot, near)
+        me_near = near_of(index)
+
+        def copy(src, place_of, at, to):
+            return lambda: remote(src, place_of, send.at[at], recv.at[at], target(to))
+
+        def relay(slot, part, at, to):
+            return copy(dst(slot, part), dst(slot, part), at, to)
+
+        self.own = lambda: pltpu.make_async_copy(own, dst(index, None), loc)
+        self.to_near = copy(own, dst(index, None), 0, me_near)
+        self.plus_own = copy(own, dst(index, None), 1, plus)
+        self.minus_own = copy(own, dst(index, None), 2, minus)
+        self.plus_near = relay(me_near, None, 3, plus)
+        self.minus_near = relay(me_near, None, 4, minus)
+        self.plus_far = relay(minus, 0, 5, plus)
+        self.minus_far = relay(plus, 1, 6, minus)
+        self.plus_far_near = relay(near_of(minus), 0, 7, plus)
+        self.minus_far_near = relay(near_of(plus), 1, 8, minus)
+        self.over = None
+        if sibling is not None:
+            send2, recv2 = sems[3:]
+            parts = [
+                (index, None),
+                (me_near, None),
+                (minus, None),
+                (plus, None),
+                (near_of(minus), None),
+                (near_of(plus), None),
+                (far, 0),
+                (far, 1),
+                (near_of(far), 0),
+                (near_of(far), 1),
+            ]
+
+            def over(at):
+                slot, part = parts[at]
+                src = own if at == 0 else dst(slot, part)
+                return remote(src, dst(slot, part), send2.at[at], recv2.at[at], sibling)
+
+            self.over = over
+
+    def cross(self, *numbers):
+        if self.over is not None:
+            for at in numbers:
+                self.over(at).start()
+
+    def start(self):
+        self.own().start()
+        for copy in (self.to_near, self.plus_own, self.minus_own):
+            copy().start()
+        self.cross(0)
+
+    def relay_near(self):
+        self.to_near().wait_recv()
+        self.plus_near().start()
+        self.minus_near().start()
+        self.cross(1)
+
+    def relay_own(self):
+        self.plus_own().wait_recv()
+        self.plus_far().start()
+        self.minus_own().wait_recv()
+        self.minus_far().start()
+        self.cross(2, 3)
+
+    def relay_far(self):
+        self.plus_near().wait_recv()
+        self.plus_far_near().start()
+        self.minus_near().wait_recv()
+        self.minus_far_near().start()
+        self.cross(4, 5)
+
+    def finish(self):
+        last = (self.plus_far, self.minus_far, self.plus_far_near, self.minus_far_near)
+        for number, copy in enumerate(last):
+            copy().wait_recv()
+            self.cross(6 + number)
+        for copy in (
+            self.to_near,
+            self.plus_own,
+            self.minus_own,
+            self.plus_near,
+            self.minus_near,
+        ) + last:
+            copy().wait_send()
+        if self.over is not None:
+            for at in range(10):
+                self.over(at).wait()
+        self.own().wait()
+
+
+def mp_ring(own, dst, sems):
+    c, m = place()
+    return Ring(own, dst, m, MP, 1, 2, lambda slot: (c, slot), sems)
+
+
+def ctx_ring(own, dst, sems):
+    c, m = place()
+    return Ring(own, dst, c, CTX, 2, 4, lambda slot: (slot, m), sems, (flip(c, 1), m))
+
+
+def mp_neighbours():
+    c, m = place()
+    return [(c, flip(m, 1)), (c, lax.rem(m + 2, MP)), (c, lax.rem(m + 6, MP))]
+
+
+def ctx_neighbours():
+    c, m = place()
+    return [
+        (flip(c, 2), m),
+        (lax.rem(c + 4, CTX), m),
+        (lax.rem(c + 12, CTX), m),
+        (flip(c, 1), m),
+    ]
+
+
+def slots(ref):
+    half = ref.shape[1] // 2
+
+    def dst(slot, part):
+        return ref.at[slot] if part is None else ref.at[slot, pl.ds(part * half, half)]
+
+    return dst
+
+
+def row_slots(ref):
+    half = ref.shape[0] // 2
+
+    def dst(slot, part):
+        rows = pl.ds(pl.multiple_of(slot * 64, 64), 64)
+        return ref.at[:, rows] if part is None else ref.at[pl.ds(part * half, half), rows]
+
+    return dst
+
+
+MP_SEMS = [pltpu.SemaphoreType.DMA((9,)), pltpu.SemaphoreType.DMA((9,)), pltpu.SemaphoreType.DMA]
+CTX_SEMS = MP_SEMS + [pltpu.SemaphoreType.DMA((10,)), pltpu.SemaphoreType.DMA((10,))]
 
 
 def start_kernel(x_ref, id_ref, w_ref, xo, ido, wo, xs, xr, ids, idr, ws, wr, loc):
@@ -134,57 +286,45 @@
         own_id.wait()
 
 
-def keys_kernel(kv_ref, w_ref, kvo, wo, send, recv, send2, recv2, ws, wr, loc):
-    c, m = place()
-    chip, core = c // 2, lax.rem(c, 2)
-    sibling = (chip * 2 + 1 - core, m)
-    others = [(lax.rem(chip + k, 8) * 2 + core, m) for k in range(1, 8)]
+def keys_kernel(kv_ref, out, *sems):
+    greet(ctx_neighbours(), 4)
+    ring = ctx_ring(kv_ref, slots(out), sems)
+    ring.start()
+    ring.relay_near()
+    ring.relay_own()
+    ring.relay_far()
+    ring.finish()
+
+
+def gather_kernel(a_ref, out, *sems):
+    greet(mp_neighbours(), 3)
+    ring = mp_ring(a_ref, slots(out), sems)
+    ring.start()
+    ring.relay_near()
+    ring.relay_own()
+    ring.relay_far()
+    ring.finish()
+
+
+def outputs_kernel(a_ref, g_ref, h_ref, ao, go, ho, s1, r1, s2, r2, loc):
+    c, m = place()
+    core = lax.rem(c, 2)
+    sibling = (flip(c, 1), m)
     mates = [(c, lax.rem(m + k, MP)) for k in range(1, MP)]
-    greet(others + [sibling] + mates, 7 + 1 + 7)
-    own = pltpu.make_async_copy(kv_ref, kvo.at[c], loc.at[0])
-    own.start()
-    own_w = pltpu.make_async_copy(w_ref, wo.at[m], loc.at[1])
-    own_w.start()
-    far, near, rows = [], [], []
-    for k in range(1, 8):
-        copy = remote(kv_ref, kvo.at[c], send.at[k], recv.at[k], others[k - 1])
-        copy.start()
-        far.append(copy)
-    first = remote(kv_ref, kvo.at[c], send.at[0], recv.at[0], sibling)
-    first.start()
-    for k in range(1, MP):
-        copy = remote(w_ref, wo.at[m], ws.at[k], wr.at[k], mates[k - 1])
-        copy.start()
-        rows.append(copy)
-    for k in range(1, 8):
-        far[k - 1].wait_recv()
-        slot = lax.rem(chip + 8 - k, 8) * 2 + core
-        copy = remote(kvo.at[slot], kvo.at[slot], send2.at[k], recv2.at[k], sibling)
-        copy.start()
-        near.append(copy)
-    first.wait()
-    for k in range(1, 8):
-        far[k - 1].wait_send()
-        near[k - 1].wait()
-        rows[k - 1].wait()
-    own.wait()
-    own_w.wait()
-
-
-def gather_kernel(a_ref, out, send, recv, loc):
-    c, m = place()
-    mates = [(c, lax.rem(m + k, MP)) for k in range(1, MP)]
-    greet(mates, MP - 1)
-    own = pltpu.make_async_copy(a_ref, out.at[m], loc.at[0])
-    own.start()
+    greet(mates + [sibling], MP)
+    own_a = pltpu.make_async_copy(a_ref.at[m], ao.at[m], loc.at[0])
+    own_a.start()
     copies = []
     for k in range(1, MP):
-        copy = remote(a_ref, out.at[m], send.at[k], recv.at[k], mates[k - 1])
+        to = lax.rem(m + k, MP)
+        copies.append(remote(a_ref.at[to], ao.at[m], s1.at[k], r1.at[k], mates[k - 1]))
+    copies.append(remote(g_ref.at[:, :, 1 - core], go, s2.at[0], r2.at[0], sibling))
+    copies.append(remote(h_ref.at[:, :, 1 - core], ho, s2.at[1], r2.at[1], sibling))
+    for copy in copies:
         copy.start()
-        copies.append(copy)
     for copy in copies:
         copy.wait()
-    own.wait()
+    own_a.wait()
 
 
 def scatter_kernel(a_ref, b_ref, ao, bo, s1, r1, s2, r2, loc):
@@ -365,8 +505,23 @@
     return key_at <= query_at
 
 
-def forward_kernel(q_ref, kv_ref, out_ref, lse_ref, best, total, summed):
+def forward_kernel(
+    q_ref, kv_ref, in_ref, outw_ref, dy_ref, rows_ref,
+    out_ref, lse_ref, in_all, outw_all, dy_all, rows_all,
+    best, total, summed, *sems,
+):
     first_half = 2 * lax.axis_index("ctx")
+    greet(ctx_neighbours() + mp_neighbours(), 7)
+    weights_rings = [
+        ctx_ring(in_ref, row_slots(in_all), sems[0:5]),
+        ctx_ring(outw_ref, row_slots(outw_all), sems[5:10]),
+    ]
+    rows_rings = [
+        mp_ring(rows_ref, slots(rows_all), sems[10:13]),
+        mp_ring(dy_ref, slots(dy_all), sems[13:16]),
+    ]
+    for ring in weights_rings + rows_rings:
+        ring.start()
     best[...] = jnp.full(best.shape, -1e30, f32)
     total[...] = jnp.zeros(total.shape, f32)
     summed[...] = jnp.zeros(summed.shape, f32)
@@ -387,6 +542,28 @@
     def step(index, carry):
         part, slot, diagonal = unit(index, first_half)
 
+        @pl.when(index == 11)
+        def _():
+            for ring in rows_rings:
+                ring.relay_near()
+                ring.relay_own()
+
+        @pl.when(index == 16)
+        def _():
+            for ring in weights_rings:
+                ring.relay_near()
+                ring.relay_own()
+
+        @pl.when(index == 20)
+        def _():
+            for ring in rows_rings:
+                ring.relay_far()
+
+        @pl.when(index == 30)
+        def _():
+            for ring in weights_rings:
+                ring.relay_far()
+
         @pl.when(diagonal)
         def _():
             work(part, slot, True)
@@ -401,29 +578,84 @@
     for part in range(2):
         out_ref[part] = summed[part][HEAD:, :] / total[part]
         lse_ref[part] = best[part] + jnp.log(total[part])
-
-
-def attention(q_rows, kv_all):
+    for ring in rows_rings + weights_rings:
+        ring.finish()
+
+
+def attention(q_rows, kv_all, w_in, w_out_t, dy, out_rows_w):
     rows = q_rows.shape[1]
     return pl.pallas_call(
         forward_kernel,
-        out_shape=[shape((2, HEAD, rows), f32), shape((2, 1, rows), f32)],
-        in_specs=[VM, VM],
-        out_specs=[VM, VM],
+        out_shape=[
+            shape((2, HEAD, rows), f32),
+            shape((2, 1, rows), f32),
+            shape((4, 1024, 1024)),
+            shape((4, 1024, 512)),
+            shape((MP, TOK, 1024)),
+            shape((MP, TOK, 1024)),
+        ],
+        in_specs=[VM, VM, ANY, ANY, ANY, ANY],
+        out_specs=[VM, VM, ANY, ANY, ANY, ANY],
         scratch_shapes=[
             pltpu.VMEM((2, 1, rows), f32),
             pltpu.VMEM((2, 1, rows), f32),
             pltpu.VMEM((2, 2 * HEAD, rows), f32),
-        ],
-        compiler_params=pltpu.CompilerParams(vmem_limit_bytes=VMEM_LIMIT),
+        ]
+        + CTX_SEMS * 2
+        + MP_SEMS * 2,
+        compiler_params=pltpu.CompilerParams(
+            vmem_limit_bytes=VMEM_LIMIT, collective_id=10, has_side_effects=True
+        ),
         cost_estimate=pl.CostEstimate(
             flops=33 * 4 * HALF * rows * 256, bytes_accessed=1 << 23, transcendentals=33 * HALF * rows
         ),
-    )(q_rows, kv_all)
-
-
-def backward_kernel(q_ref, do_ref, lse_ref, delta_ref, kv_ref, dkv_ref, dq_ref, total):
-    first_half = 2 * lax.axis_index("ctx")
+    )(q_rows, kv_all, w_in, w_out_t, dy, out_rows_w)
+
+
+def backward_kernel(
+    q_ref, do_ref, lse_ref, delta_ref, kv_ref, pair_ref, br_ref, qw_ref,
+    dkv_ref, dq_ref, grad_ref, br_all, qw_all,
+    total, got_a, got_b, sum_a, sum_b, last_a, last_b, *sems,
+):
+    c, m = place()
+    first_half = 2 * c
+    x, y = c // 4, lax.rem(c // 2, 2)
+    peers = [(lax.rem(c + 4 * k, CTX), m) for k in range(1, 4)]
+    across = (flip(c, 2), m)
+    greet(peers + [across] + mp_neighbours(), 7)
+    sa, ra, sb, rb = sems[:4]
+    rings = [
+        mp_ring(br_ref, slots(br_all), sems[4:7]),
+        mp_ring(qw_ref, slots(qw_all), sems[7:10]),
+    ]
+
+    def first_copies():
+        copies = [
+            remote(
+                pair_ref.at[pl.ds(0, 2), lax.rem(x + k, 4)],
+                got_a.at[k - 1], sa.at[k], ra.at[k], peers[k - 1],
+            )
+            for k in range(1, 4)
+        ]
+        copies.append(
+            remote(pair_ref.at[pl.ds(2, 2), :, 1 - y], got_b, sa.at[0], ra.at[0], across)
+        )
+        return copies
+
+    def second_copies():
+        copies = [
+            remote(
+                sum_b.at[:, lax.rem(x + k, 4)], last_b.at[k - 1], sb.at[k], rb.at[k], peers[k - 1]
+            )
+            for k in range(1, 4)
+        ]
+        copies.append(remote(sum_a.at[:, 1 - y], last_a, sb.at[0], rb.at[0], across))
+        return copies
+
+    for copy in first_copies():
+        copy.start()
+    for ring in rings:
+        ring.start()
     dq_ref[...] = jnp.zeros(dq_ref.shape, f32)
 
     def clear(index, carry):
@@ -447,8 +679,38 @@
         )
         dq_ref[part] += contract(kv, score_grad, 0, 0)
 
+    def middle():
+        for copy in first_copies():
+            copy.wait()
+        for e in range(2):
+            for j in range(2):
+                term = pair_ref[e, x, j].astype(f32)
+                for k in range(3):
+                    term = term + got_a[k, e, j].astype(f32)
+                sum_a[e, j] = term.astype(bf16)
+            for j in range(4):
+                term = pair_ref[2 + e, j, y].astype(f32) + got_b[e, j].astype(f32)
+                sum_b[e, j] = term.astype(bf16)
+        for copy in second_copies():
+            copy.start()
+
     def step(index, carry):
         part, slot, diagonal = unit(index, first_half)
+
+        @pl.when(index == 11)
+        def _():
+            for ring in rings:
+                ring.relay_near()
+                ring.relay_own()
+
+        @pl.when(index == 21)
+        def _():
+            for ring in rings:
+                ring.relay_far()
+
+        @pl.when(index == 23)
+        def _():
+            middle()
 
         @pl.when(diagonal)
         def _():
@@ -467,21 +729,50 @@
         return carry
 
     lax.fori_loop(0, 2 * CTX, write, 0)
-
-
-def attention_back(q_rows, do_rows, lse, delta, kv_all):
+    for ring in rings:
+        ring.finish()
+    for copy in second_copies():
+        copy.wait()
+    for e in range(2):
+        grad_ref[e] = sum_a[e, y].astype(f32) + last_a[e].astype(f32)
+        term = sum_b[e, x].astype(f32)
+        for k in range(3):
+            term = term + last_b[k, e].astype(f32)
+        grad_ref[2 + e] = term
+
+
+def attention_back(q_rows, do_rows, lse, delta, kv_all, pair, branch_grad, qkv_w):
     rows = q_rows.shape[1]
+    wide = pair.shape[-1]
     return pl.pallas_call(
         backward_kernel,
-        out_shape=[shape(kv_all.shape, bf16), shape((2, 2 * HEAD, rows), f32)],
-        in_specs=[VM] * 5,
-        out_specs=[VM] * 2,
-        scratch_shapes=[pltpu.VMEM(kv_all.shape, f32)],
-        compiler_params=pltpu.CompilerParams(vmem_limit_bytes=VMEM_LIMIT),
+        out_shape=[
+            shape(kv_all.shape, bf16),
+            shape((2, 2 * HEAD, rows), f32),
+            shape((4, 64, wide), f32),
+            shape((MP, TOK, 1024)),
+            shape((MP,) + qkv_w.shape),
+        ],
+        in_specs=[VM] * 6 + [ANY] * 2,
+        out_specs=[VM] * 3 + [ANY] * 2,
+        scratch_shapes=[
+            pltpu.VMEM(kv_all.shape, f32),
+            pltpu.VMEM((3, 2, 2, 64, wide), bf16),
+            pltpu.VMEM((2, 4, 64, wide), bf16),
+            pltpu.VMEM((2, 2, 64, wide), bf16),
+            pltpu.VMEM((2, 4, 64, wide), bf16),
+            pltpu.VMEM((2, 64, wide), bf16),
+            pltpu.VMEM((3, 2, 64, wide), bf16),
+        ]
+        + [pltpu.SemaphoreType.DMA((4,))] * 4
+        + MP_SEMS * 2,
+        compiler_params=pltpu.CompilerParams(
+            vmem_limit_bytes=VMEM_LIMIT, collective_id=11, has_side_effects=True
+        ),
         cost_estimate=pl.CostEstimate(
             flops=33 * 10 * HALF * rows * 256, bytes_accessed=1 << 24, transcendentals=33 * HALF * rows
         ),
-    )(q_rows, do_rows, lse, delta, kv_all)
+    )(q_rows, do_rows, lse, delta, kv_all, pair, branch_grad, qkv_w)
 
 
 def phases(positions, head_width):
@@ -525,22 +816,6 @@
             t = CTX - 1 - c if m >= MP // 2 else c
             pairs.append((c * MP + m, t * MP + m))
     return lax.ppermute(array, ("ctx", "mp"), pairs)
-
-
-def sum_over_ctx(terms):
-    c = lax.axis_index("ctx")
-    chip, core = c // 2, lax.rem(c, 2)
-    mine = lax.dynamic_index_in_dim(terms, core, 1, False)
-    theirs = lax.dynamic_index_in_dim(terms, 1 - core, 1, False)
-    got = lax.ppermute(theirs, "ctx", [(i, i ^ 1) for i in range(CTX)])
-    pair = (mine.astype(f32) + got.astype(f32)).astype(bf16)
-    total = lax.dynamic_index_in_dim(pair, chip, 0, False).astype(f32)
-    for k in range(1, 8):
-        piece = lax.dynamic_index_in_dim(pair, jnp.bitwise_xor(chip, k), 0, False)
-        total = total + lax.ppermute(
-            piece, "ctx", [(i, i ^ (2 * k)) for i in range(CTX)]
-        ).astype(f32)
-    return total
 
 
 def heads_to_rows(values):
@@ -563,10 +838,7 @@
     cotangent,
 ):
     c, m = place()
-    in_w = lax.all_gather(w_in, "ctx", axis=1, tiled=True)
-    out_expert = lax.all_gather(w_out, "ctx", axis=2, tiled=True)
-    dy_all = lax.all_gather(swap_home(cotangent), "mp", axis=0, tiled=True)
-
+    dy_swapped = swap_home(cotangent)
     own_positions = lax.dynamic_slice_in_dim(positions, m * TOK, TOK, 0)
     id_pack = jnp.concatenate(
         [expert_ids.T, own_positions[None, :], jnp.zeros((7, TOK), jnp.int32)], axis=0
@@ -610,6 +882,7 @@
     normed = (scaled_all * gain_one).astype(bf16)
     qkv = jnp.dot(normed, qkv_w, preferred_element_type=f32)
     cosine, sine = phases(places, HEAD)
+    cosine, sine = lax.optimization_barrier((cosine, sine))
     cos2, sin2 = cosine[:, None, :], sine[:, None, :]
     queries = rotate(qkv[:, :128].reshape(BLOCK, 2, HEAD), cos2, sin2).astype(bf16)
     queries = queries * jnp.asarray(score_scale, bf16)
@@ -617,22 +890,20 @@
     q_rows = jnp.concatenate([q_rows, jnp.zeros_like(q_rows)], axis=-1)
     keys = rotate(qkv[:, 128:192], cosine, sine).astype(bf16)
     kv_new = jnp.concatenate([keys, qkv[:, 192:].astype(bf16)], axis=-1)
-    kv_all, out_w_all = comm_call(
-        keys_kernel,
-        2,
-        [kv_new, out_w],
-        [shape((CTX, BLOCK, 128)), shape((MP, 128, 1024))],
-        [8, 8, 8, 8, MP, MP, 2],
-        8 << 20,
+    (kv_all,) = comm_call(
+        keys_kernel, 2, [kv_new], [shape((CTX, BLOCK, 128))], CTX_SEMS, 4 << 20
     )
     kv_all = kv_all.reshape(2 * CTX, HALF, 128)
-    out_cols, lse = attention(q_rows, kv_all)
+    out_cols, lse, in_w, out_w_t, dy_all, out_w_all = attention(
+        q_rows, kv_all, w_in, w_out.transpose(0, 2, 1), dy_swapped, out_w
+    )
+    dy_all = dy_all.reshape(BLOCK, 1024)
     attended = (
         out_cols.reshape(2, HEAD, 2, HALF).transpose(0, 3, 2, 1).reshape(BLOCK, 128)
     )
     out_rows = attended.astype(bf16)
     (rows_all,) = comm_call(
-        gather_kernel, 3, [out_rows], [shape((MP, BLOCK, 128))], [MP, MP, 1], 4 << 20
+        gather_kernel, 3, [out_rows], [shape((MP, BLOCK, 128))], MP_SEMS, 4 << 20
     )
     branch = lax.dot_general(
         rows_all, out_w_all, (((0, 2), (0, 1)), ((), ())), preferred_element_type=f32
@@ -672,7 +943,7 @@
     silu_part = gate_part * squashed
     active = (silu_part * up_part).astype(bf16)
     produced = jnp.einsum(
-        "esf,efd->esd", active, out_expert, preferred_element_type=f32
+        "esf,edf->esd", active, out_w_t, preferred_element_type=f32
     ).astype(bf16)
     produced_f = produced.astype(f32)
     d_produced = (branch_scale * slot_gate[..., None] * dy_rows).astype(bf16)
@@ -681,7 +952,7 @@
     mixed = branch_scale * contract(placing, weighted, 0, 0)
     mixed = mixed.astype(bf16).reshape(MP, TOK, 1024)
 
-    d_active = jnp.einsum("esd,efd->esf", d_produced, out_expert, preferred_element_type=f32)
+    d_active = jnp.einsum("esd,edf->esf", d_produced, out_w_t, preferred_element_type=f32)
     slope = squashed * (1.0 + gate_part * (1.0 - squashed))
     d_gate_up = jnp.concatenate(
         [d_active * up_part * slope, d_active * silu_part], axis=-1
@@ -731,32 +1002,49 @@
     hidden_grad, gain_two_grad = norm_back(routed_grad, scaled_own, inverse_own, gain_two)
     hidden_grad = hidden_grad + dy_own
     branch_grad = (branch_scale * hidden_grad).astype(bf16)
-    (branch_rows,) = comm_call(
-        gather_kernel, 5, [branch_grad], [shape((MP, TOK, 1024))], [MP, MP, 1], 4 << 20
-    )
-    branch_rows = branch_rows.reshape(BLOCK, 1024)
     hidden_grad_home = swap_home(hidden_grad)
 
     out_expert_grad = jnp.einsum(
-        "esf,esd->efd", active, d_produced, preferred_element_type=f32
+        "esd,esf->edf", d_produced, active, preferred_element_type=f32
     ).astype(bf16)
     in_expert_grad = jnp.einsum(
         "esd,esf->edf", incoming, d_gate_up, preferred_element_type=f32
     ).astype(bf16)
-    in_terms = in_expert_grad.reshape(4, 8, 2, 64, 1024).transpose(1, 2, 0, 3, 4)
-    out_terms = out_expert_grad.reshape(4, 512, 8, 2, 64).transpose(2, 3, 0, 1, 4)
-    expert_in = sum_over_ctx(in_terms.reshape(8, 2, 4 * 64, 1024)).reshape(4, 64, 1024)
-    expert_out = sum_over_ctx(out_terms.reshape(8, 2, 4 * 512, 64)).reshape(4, 512, 64)
+    in_terms = in_expert_grad.reshape(4, 8, 2, 64, 1024)
+    out_terms = out_expert_grad.reshape(4, 8, 2, 64, 512)
+    out_grad_terms = jnp.einsum(
+        "td,hfd->htf", branch_grad, out_w_all, preferred_element_type=f32
+    ).astype(bf16)
+    out_grad, in_theirs, out_theirs = comm_call(
+        outputs_kernel,
+        5,
+        [out_grad_terms, in_terms, out_terms],
+        [shape((MP, TOK, 128)), shape((4, 8, 64, 1024)), shape((4, 8, 64, 512))],
+        [MP, MP, 2, 2, 1],
+        8 << 20,
+    )
+    out_grad = out_grad.reshape(BLOCK, 128)
+    core = lax.rem(c, 2)
+
+    def with_sibling(own, theirs):
+        mine = lax.dynamic_index_in_dim(own, core, 2, False)
+        return (mine.astype(f32) + theirs.astype(f32)).astype(bf16)
+
+    pair = jnp.concatenate(
+        [with_sibling(in_terms, in_theirs), with_sibling(out_terms, out_theirs)], axis=-1
+    ).reshape(4, 4, 2, 64, 1536)
 
     mixed_got = lax.all_to_all(mixed, "mp", split_axis=0, concat_axis=0, tiled=True)
     outputs = (hidden_own + jnp.sum(mixed_got.astype(f32), axis=0)).astype(bf16)
     outputs = swap_home(outputs)
 
-    out_grad = contract(branch_rows, out_w, 1, 1).astype(bf16)
     do_rows = heads_to_rows(out_grad)
     delta = jnp.sum(do_rows.astype(f32) * heads_to_rows(attended), axis=-1)[:, None, :]
     do_rows = jnp.concatenate([jnp.zeros_like(do_rows), do_rows], axis=-1)
-    dkv_terms, dq_cols = attention_back(q_rows, do_rows, lse, delta, kv_all)
+    dkv_terms, dq_cols, expert_grad, branch_rows, qkv_w_all = attention_back(
+        q_rows, do_rows, lse, delta, kv_all, pair, branch_grad, qkv_w
+    )
+    branch_rows = branch_rows.reshape(BLOCK, 1024)
     dkv_terms = dkv_terms.reshape(8, 2, BLOCK, 128)
     (theirs,) = comm_call(
         sibling_kernel, 6, [dkv_terms], [shape((8, BLOCK, 128))], [1, 1], 4 << 20
@@ -776,17 +1064,18 @@
     qkv_w_grad = contract(normed, d_qkv, 0, 0)
     out_w_grad = contract(branch_rows, out_rows, 0, 0)
     w_terms = jnp.concatenate([qkv_w_grad, out_w_grad], axis=1).astype(bf16)
-    normed_terms = contract(d_qkv, qkv_w, 1, 1).astype(bf16).reshape(MP, TOK, 1024)
-    normed_got, w_got = comm_call(
+    qkv_got, w_got = comm_call(
         finish_kernel,
         8,
-        [normed_terms, w_terms.reshape(CTX, 64, 384)],
-        [shape((MP, TOK, 1024)), shape((CTX, 64, 384))],
+        [d_qkv.reshape(MP, TOK, 256), w_terms.reshape(CTX, 64, 384)],
+        [shape((MP, TOK, 256)), shape((CTX, 64, 384))],
         [MP, MP, CTX, CTX, 2],
         5 << 20,
     )
     w_grad = jnp.sum(w_got.astype(f32), axis=0)
-    normed_grad = jnp.sum(normed_got.astype(f32), axis=0)
+    normed_grad = jnp.einsum(
+        "htf,hdf->td", qkv_got, qkv_w_all, preferred_element_type=f32
+    )
     scaled_one, inverse_one = normalize(layer_input.astype(f32))
     input_grad, gain_one_grad = norm_back(normed_grad, scaled_one, inverse_one, gain_one)
     input_grad = (input_grad + hidden_grad_home).astype(bf16)
@@ -811,8 +1100,8 @@
         w_grad[:, 256:].T,
         sums[:, 33],
         sums[:, :32],
-        expert_in,
-        expert_out,
+        expert_grad[..., :1024],
+        expert_grad[..., 1024:].transpose(0, 2, 1),
     )
 
 

time: 846 us -> 636 us (0.75)
  waiting for transfers between devices: 99.1 us -> 10.7 us
  Pallas kernels: 454 us -> 420 us
  local copies, waits for them, and re-layouts: 85.5 us -> 55.6 us
  starting transfers between devices: 41.7 us -> 18.8 us
  matrix products: 82.8 us -> 63.1 us
  between operations: 15 us -> 2.24 us
    pallas_call x8, Pallas kernels: 322 us -> 221 us  [comm_call(): pl.pallas_call(kernel, out_shape=outs, in_specs=[ANY] * len(arrays), out_...]
    ppermute x16 -> x0, waiting for transfers between devices: 62.7 us -> none  [the longest x14 62.7 us: sum_over_ctx(): lax.ppermute(piece, 'ctx', [(i, i ^ 2 * k) for i in range(CTX)]).astype(f32)]
    pallas_call x1, Pallas kernels: 53.9 us -> 98.8 us  [attention_back(): pl.pallas_call(backward_kernel, out_shape=[shape(kv_all.shape, bf16), sha...]
    pallas_call x1, Pallas kernels: 39.7 us -> 81.5 us  [attention(): pl.pallas_call(forward_kernel, out_shape=[shape((2, HEAD, rows), f32), sh...]
    all_gather x3 -> x0, waiting for transfers between devices: 31.9 us -> none  [the longest x1 31.9 us: body(): dy_all = lax.all_gather(swap_home(cotangent), 'mp', axis=0, tiled=True)]
    pallas_call x1, Pallas kernels: 38 us -> 19.1 us  [small_sums(): pl.pallas_call(sums_kernel, out_shape=shape(dims, f32), in_specs=[VM], ou...]
    ppermute x16 -> x0, starting transfers between devices: 17.6 us -> none  [the longest x14 17.1 us: sum_over_ctx(): lax.ppermute(piece, 'ctx', [(i, i ^ 2 * k) for i in range(CTX)]).astype(f32)]
    reshape x4 -> x0, local copies, waits for them, and re-layouts: 14.2 us -> none  [the longest x1 8.4 us: body(): in_expert_grad.reshape(4, 8, 2, 64, 1024).transpose(1, 2, 0, 3, 4)]
  transfers between devices with their start and end apart: 23 -> 4, of which waited for: 10 -> 1; matrix products, arithmetic and copies ran while one was open for 25% -> 12% of each run, Pallas kernels for 54% -> 15%
where the time goes in v2:
time: 636 us; the launch traced here: 626 us
  Pallas kernels  420 us (66%)
  matrix products  63.1 us (10%)
  other arithmetic  55.7 us (9%)
  local copies, waits for them, and re-layouts  55.6 us (9%)
  starting transfers between devices  18.8 us (3%)
  waiting for transfers between devices  10.7 us (2%)
    pallas_call x8, Pallas kernels, comm_call(): pl.pallas_call(kernel, out_shape=outs, in_specs=[ANY] * len(arrays), out_...  221 us
    pallas_call x1, Pallas kernels, attention_back(): pl.pallas_call(backward_kernel, out_shape=[shape(kv_all.shape, bf16), sha...  98.8 us
    pallas_call x1, Pallas kernels, attention(): pl.pallas_call(forward_kernel, out_shape=[shape((2, HEAD, rows), f32), sh...  81.5 us
    pallas_call x1, Pallas kernels, small_sums(): pl.pallas_call(sums_kernel, out_shape=shape(dims, f32), in_specs=[VM], ou...  19.1 us
    dot_general x5, matrix products, contract(): lax.dot_general(left, right, (((left_dim,), (right_dim,)), ((), ())), pre...  18.8 us
    ppermute x3, starting transfers between devices, swap_home(): return lax.ppermute(array, ('ctx', 'mp'), pairs)  13.6 us
  transfers between devices with their start and end apart: 4, of which 1 were waited for; matrix products, arithmetic and copies ran while one was open for 12% of the time, Pallas kernels for 15%

profile of v2, /device:TPU:65, one launch (start us, length us, event | category | flops | bytes accessed | tf_op | source)
XLA Modules:
  0.0 626.1 jit_solution(3732274962007680817)
XLA Ops:
  0.7 6.0 collective-permute-start
  12.0 64.4 %shard_map.212 = (bf16[8,128,1024]{2,1,0:T(8,128)(2,1)}, s32[8,16,128]{2,1,0:T(8,128)}, bf16[16,64,512]{2,1,0:T(8,128)(2,1)}) custom-call(bf16[128,1024]{1,0:T(8,128)(2,1)} %x_ref.1, s32[16,128]{1,0:T(8,128)} %add_add_fusion.id_ref, bf16[64,512]{1,0:T(8,128)(2,1)} %concatenate.63.w_ref), custom_call_target="tpu_custom_call" | custom-call | bytes 4194304 | tf_op jit(solution)/shard_map/pallas_call | solution.py:54
  106.7 26.8 %shard_map.213 = bf16[16,1024,128]{2,1,0:T(8,128)(2,1)} custom-call(bf16[1024,128]{1,0:T(8,128)(2,1)} %pad_maximum_fusion.12.kv_ref), custom_call_target="tpu_custom_call" | custom-call | bytes 4194304 | tf_op jit(solution)/shard_map/pallas_call | solution.py:54
  142.3 81.5 %shard_map.214 = (f32[2,64,1024]{2,1,0:T(8,128)}, f32[2,1,1024]{2,1,0:T(1,128)}, bf16[4,1024,1024]{2,1,0:T(8,128)(2,1)}, bf16[4,1024,512]{2,1,0:T(8,128)(2,1)}, ...) custom-call(bf16[2,1024,128]{2,1,0:T(8,128)(2,1)} %concatenate.68.q_ref, bf16[32,512,128]{2,1,0:T(8,128)(2,1)} %bitcast.172, ...), custom_call_target="tpu_custom_call" | custom-call | flops 17716740096 | bytes 8388608 | tf_op jit(solution)/shard_map/pallas_call | solution.py:587
  226.6 21.8 %shard_map.215 = bf16[8,1024,128]{2,1,0:T(8,128)(2,1)} custom-call(bf16[1024,128]{1,0:T(8,128)(2,1)} %copy.119.a_ref), custom_call_target="tpu_custom_call" | custom-call | bytes 4194304 | tf_op jit(solution)/shard_map/pallas_call | solution.py:54
  248.4 4.8 multiply_reduce_fusion
  269.8 4.4 fusion.10
  279.3 10.8 %bitcast_convert_fusion = bf16[1024,1024]{1,0:T(8,128)(2,1)} fusion(s32[4,1024]{1,0:T(4,128)S(1)} %fusion.31, bf16[4,1024,1024]{2,1,0:T(8,128)(2,1)} %get-tuple-element.41, bf16[4,288,512]{2,1,0:T(8,128)(2,1)} %get-tuple-element.70, bf16[4,288,512]{2,1,0:T(8,128)(2,1)S(1)} %get-tuple-element.69), kind=kOutput, calls=%fused_computation.22 | convolution fusion | flops 4839964672 | bytes 12861440 | tf_op jit(solution)/shard_map/dot_general | solution.py:30
  290.1 28.1 %shard_map.216 = (bf16[8,128,1024]{2,1,0:T(8,128)(2,1)}, f32[8,8,128]{2,1,0:T(8,128)}) custom-call(bf16[8,128,1024]{2,1,0:T(8,128)(2,1)} %bitcast.179, f32[8,8,128]{2,1,0:T(8,128)} %pad.6.b_ref), custom_call_target="tpu_custom_call" | custom-call | bytes 4194304 | tf_op jit(solution)/shard_map/pallas_call | solution.py:54
  320.1 5.2 all-to-all-start
  337.8 7.0 %convolution_convert_fusion.2 = bf16[4,1024,512]{2,1,0:T(8,128)(2,1)} fusion(bf16[4,288,512]{2,1,0:T(8,128)(2,1)S(1)} %multiply_convert_fusion.4, f32[4,288,1024]{2,1,0:T(8,128)} %copy-done.13, f32[4,288]{1,0:T(4,128)S(1)} %broadcast_multiply_fusion.3), kind=kOutput, calls=%fused_computation.40 | convolution fusion | flops 1212416000 | bytes 10097152 | tf_op jit(solution)/shard_map/esd,esf->edf/dot_general | solution.py:1007
  344.8 7.0 %convolution_convert_fusion = bf16[4,1024,1024]{2,1,0:T(8,128)(2,1)} fusion(bf16[4,288,1024]{2,1,0:T(8,128)(2,1)S(1)} %bitcast.203, bf16[4,288,512]{2,1,0:T(8,128)(2,1)S(1)} %copy-done.53, bf16[4,288,512]{2,1,0:T(8,128)(2,1)S(1)} %copy-done.52), kind=kOutput, calls=%fused_computation.2 | convolution fusion | flops 2424832000 | bytes 13107200 | tf_op jit(solution)/shard_map/esd,esf->edf/dot_general | solution.py:1010
  356.7 17.3 %shard_map.217 = (bf16[8,128,128]{2,1,0:T(8,128)(2,1)}, bf16[4,8,64,1024]{3,2,1,0:T(8,128)(2,1)}, bf16[4,8,64,512]{3,2,1,0:T(8,128)(2,1)}) custom-call(bf16[8,128,128]{2,1,0:T(8,128)(2,1)} %fusion.28.a_ref, bf16[4,8,2,64,1024]{4,3,2,1,0:T(8,128)(2,1)} %bitcast.155, bf16[4,8,2,64,512]{4,3,2,1,0:T(8,128)(2,1)} %bitcast.152), custom_call_target="tpu_custom_call" | custom-call | bytes 8388608 | tf_op jit(solution)/shard_map/pallas_call | solution.py:54
  374.0 8.0 %fusion = bf16[4,8,64,1024]{3,2,1,0:T(8,128)(2,1)} fusion(bf16[4,8,64,1024]{3,2,1,0:T(8,128)(2,1)} %get-tuple-element.48, bf16[4,8,2,64,1024]{4,3,2,1,0:T(8,128)(2,1)} %bitcast.156, s32[]{:T(128)S(6)} %select_n.39), kind=kLoop, calls=%fused_computation.1 | loop fusion | flops 8388608 | bytes 12582916 | tf_op jit(solution)/shard_map/convert_element_type | solution.py:1031
  385.7 5.6 pad_maximum_fusion
  391.3 98.8 %shard_map.218 = (bf16[32,512,128]{2,1,0:T(8,128)(2,1)}, f32[2,128,1024]{2,1,0:T(8,128)}, f32[4,64,1536]{2,1,0:T(8,128)}, bf16[8,128,1024]{2,1,0:T(8,128)(2,1)}, bf16[8,1024,256]{2,1,0:T(8,128)(2,1)}) custom-call(bf16[2,1024,128]{2,1,0:T(8,128)(2,1)} %concatenate.68.q_ref, bf16[2,1024,128]{2,1,0:T(8,128)(2,1)} %concatenate.72.do_ref, ...), custom_call_target="tpu_custom_call" | custom-call | flops 44291850240 | bytes 16777216 | tf_op jit(solution)/shard_map/pallas_call | solution.py:747
  490.1 5.8 shard_map.219
  495.9 4.1 fusion.8.a_ref
  500.0 30.7 %shard_map.220 = bf16[8,1024,128]{2,1,0:T(8,128)(2,1)} custom-call(bf16[8,1024,128]{2,1,0:T(8,128)(2,1)} %fusion.8.a_ref), custom_call_target="tpu_custom_call" | custom-call | bytes 4194304 | tf_op jit(solution)/shard_map/pallas_call | solution.py:54
  546.3 25.8 %shard_map.221 = (bf16[8,128,256]{2,1,0:T(8,128)(2,1)}, bf16[16,64,384]{2,1,0:T(8,128)(2,1)}) custom-call(bf16[8,128,256]{2,1,0:T(8,128)(2,1)} %bitcast.180, bf16[16,64,384]{2,1,0:T(8,128)(2,1)} %pad_maximum_fusion.8.g_ref), custom_call_target="tpu_custom_call" | custom-call | bytes 5242880 | tf_op jit(solution)/shard_map/pallas_call | solution.py:54
  574.7 4.0 fusion.42
  580.3 19.1 %shard_map.222 = f32[8,128]{1,0:T(8,128)} custom-call(f32[16,8,8,128]{3,2,1,0:T(8,128)} %maximum_maximum_fusion.a_ref), custom_call_target="tpu_custom_call" | custom-call | tf_op jit(solution)/shard_map/pallas_call | solution.py:474
  599.3 4.8 collective-permute-start.2
  612.7 10.7 %collective-permute-done.1 = bf16[128,1024]{1,0:T(8,128)(2,1)S(1)} collective-permute-done((bf16[128,1024]{1,0:T(8,128)(2,1)S(1)}, bf16[128,1024]{1,0:T(8,128)(2,1)S(1)}, u32[]{:S(2)}, u32[]{:S(2)}) %collective-permute-start.1) | collective-permute-done | bytes 262176 | tf_op jit(solution)/shard_map/ppermute | solution.py:818
  (249 shorter events, 121.5 us)
Async XLA Ops:
  0.6 8.4 %copy-start = (s32[1024]{0:T(1024)S(1)}, s32[1024]{0:T(1024)}, u32[]{:S(2)}) copy-start(s32[1024]{0:T(1024)} %param.14) | copy-start | bytes 12292
  0.7 141.6 %collective-permute-start = (bf16[128,1024]{1,0:T(8,128)(2,1)}, bf16[128,1024]{1,0:T(8,128)(2,1)}, u32[]{:S(2)}, u32[]{:S(2)}) collective-permute-start(bf16[128,1024]{1,0:T(8,128)(2,1)} %param.25), channel_id=1, source_target_pairs={{0,0},{1,1},{2,2},{3,3},{4,124},{5,125},{6,126},{7,127},{8,8},{9,9... | collective-permute-start | bytes 786440 | tf_op jit(solution)/shard_map/ppermute | solution.py:818
  89.3 16.2 %copy-start.3 = (f32[1024,64]{1,0:T(8,128)}, f32[1024,64]{1,0:T(8,128)S(1)}, u32[]{:S(2)}) copy-start(f32[1024,64]{1,0:T(8,128)S(1)} %get-tuple-element.38) | copy-start | bytes 786436
  89.3 17.1 %copy-start.5 = (f32[1024,64]{1,0:T(8,128)}, f32[1024,64]{1,0:T(8,128)S(1)}, u32[]{:S(2)}) copy-start(f32[1024,64]{1,0:T(8,128)S(1)} %get-tuple-element.37) | copy-start | bytes 786436
  106.6 28.0 %copy-start.34 = (bf16[128,1024]{0,1:T(8,128)(2,1)S(1)}, bf16[128,1024]{0,1:T(8,128)(2,1)}, u32[]{:S(2)}) copy-start(bf16[128,1024]{0,1:T(8,128)(2,1)} %slice_bitcast_fusion.1) | copy-start | bytes 786436
  225.3 48.9 %copy-start.10 = (f32[2,64,2,512]{3,2,1,0:T(2,128)}, f32[2,64,2,512]{3,2,1,0:T(2,128)S(1)}, u32[]{:S(2)}) copy-start(f32[2,64,2,512]{3,2,1,0:T(2,128)S(1)} %reshape.244) | copy-start | bytes 1572868
  225.3 23.1 %copy-start.9 = (bf16[8,128,1024]{2,1,0:T(8,128)(2,1)S(1)}, bf16[8,128,1024]{2,1,0:T(8,128)(2,1)}, u32[]{:S(2)}) copy-start(bf16[8,128,1024]{2,1,0:T(8,128)(2,1)} %get-tuple-element.34) | copy-start | bytes 6291460
  255.8 12.4 %copy-start.36 = (f32[32,1024]{1,0:T(8,128)}, f32[32,1024]{1,0:T(8,128)S(1)}, u32[]{:S(2)}) copy-start(f32[32,1024]{1,0:T(8,128)S(1)} %fusion.59) | copy-start | bytes 393220
  268.2 7.7 %copy-start.13 = (f32[4,288,1024]{2,1,0:T(8,128)}, f32[4,288,1024]{2,1,0:T(8,128)S(1)}, u32[]{:S(2)}) copy-start(f32[4,288,1024]{2,1,0:T(8,128)S(1)} %get-tuple-element.91) | copy-start | bytes 14155780
  279.3 10.8 %copy-start.51 = (bf16[4,288,512]{2,1,0:T(8,128)(2,1)}, bf16[4,288,512]{2,1,0:T(8,128)(2,1)S(1)}, u32[]{:S(2)}) copy-start(bf16[4,288,512]{2,1,0:T(8,128)(2,1)S(1)} %get-tuple-element.69) | copy-start | bytes 3538948
  320.1 31.8 %all-to-all-start = ((bf16[8,128,1024]{2,1,0:T(8,128)(2,1)}), bf16[8,128,1024]{2,1,0:T(8,128)(2,1)S(1)}, u32[]{:S(2)}, u32[]{:S(2)}) async-start(bf16[8,128,1024]{2,1,0:T(8,128)(2,1)} %bitcast.177), calls=%async_computation | async-start | bytes 4194304 | tf_op jit(solution)/shard_map/all_to_all | solution.py:1037
  355.1 18.8 %copy-start.30 = (bf16[128,1024]{1,0:T(8,128)(2,1)}, bf16[128,1024]{1,0:T(8,128)(2,1)S(1)}, u32[]{:S(2)}) copy-start(bf16[128,1024]{1,0:T(8,128)(2,1)S(1)} %get-tuple-element.67.br_ref) | copy-start | bytes 786436
  374.0 8.0 %copy-start.2 = (bf16[4,1024,512]{2,1,0:T(8,128)(2,1)S(1)}, bf16[4,1024,512]{2,1,0:T(8,128)(2,1)}, u32[]{:S(2)}) copy-start(bf16[4,1024,512]{2,1,0:T(8,128)(2,1)} %convolution_convert_fusion.2) | copy-start | bytes 12582916
  374.0 8.0 %copy-start.17 = (bf16[4,8,64,512]{3,2,1,0:T(8,128)(2,1)S(1)}, bf16[4,8,64,512]{3,2,1,0:T(8,128)(2,1)}, u32[]{:S(2)}) copy-start(bf16[4,8,64,512]{3,2,1,0:T(8,128)(2,1)} %get-tuple-element.49) | copy-start | bytes 6291460
  500.0 32.8 %copy-start.4 = (f32[1024,64]{1,0:T(8,128)S(1)}, f32[1024,64]{1,0:T(8,128)}, u32[]{:S(2)}) copy-start(f32[1024,64]{1,0:T(8,128)} %copy-done.3) | copy-start | bytes 786436
  545.3 29.4 %copy-start.15 = (bf16[128,1024]{1,0:T(8,128)(2,1)S(1)}, bf16[128,1024]{1,0:T(8,128)(2,1)}, u32[]{:S(2)}) copy-start(bf16[128,1024]{1,0:T(8,128)(2,1)} %x_ref.1) | copy-start | bytes 786436
  545.3 29.4 %copy-start.42 = (f32[1024]{0:T(1024)S(1)}, f32[1024]{0:T(1024)}, u32[]{:S(2)}) copy-start(f32[1024]{0:T(1024)} %copy-done.41) | copy-start | bytes 12292
  545.3 29.4 %copy-start.47 = (f32[128]{0:T(128)S(1)}, f32[128]{0:T(128)}, u32[]{:S(2)}) copy-start(f32[128]{0:T(128)} %add_rsqrt_fusion.2) | copy-start | bytes 1540
  578.7 20.6 %copy-start.35 = (f32[128,1024]{1,0:T(8,128)S(1)}, f32[128,1024]{1,0:T(8,128)}, u32[]{:S(2)}) copy-start(f32[128,1024]{1,0:T(8,128)} %get-tuple-element.68) | copy-start | bytes 1572868
  578.7 25.4 %copy-start.37 = (bf16[128,1024]{1,0:T(8,128)(2,1)S(1)}, bf16[128,1024]{1,0:T(8,128)(2,1)}, u32[]{:S(2)}) copy-start(bf16[128,1024]{1,0:T(8,128)(2,1)} %get-tuple-element.71) | copy-start | bytes 786436
  599.3 24.1 %collective-permute-start.2 = (f32[128,1024]{1,0:T(8,128)S(1)}, f32[128,1024]{1,0:T(8,128)S(1)}, u32[]{:S(2)}, u32[]{:S(2)}) collective-permute-start(f32[128,1024]{1,0:T(8,128)S(1)} %copy-done.35), channel_id=1, source_target_pairs={{0,0},{1,1},{2,2},{3,3},{4,124},{5,125},{6,126},{7,127},{8,8},{9,9... | collective-permute-start | bytes 1572872 | tf_op jit(solution)/shard_map/ppermute | solution.py:818
  604.2 19.2 %collective-permute-start.1 = (bf16[128,1024]{1,0:T(8,128)(2,1)S(1)}, bf16[128,1024]{1,0:T(8,128)(2,1)S(1)}, u32[]{:S(2)}, u32[]{:S(2)}) collective-permute-start(bf16[128,1024]{1,0:T(8,128)(2,1)S(1)} %copy-done.37), channel_id=1, source_target_pairs={{0,0},{1,1},{2,2},{3,3},{4,124},{5,125},{6,126},{7,127},{8,8},{9,9... | collective-permute-start | bytes 786440 | tf_op jit(solution)/shard_map/ppermute | solution.py:818
  608.5 17.2 %copy-start.1 = (s32[1024]{0:T(1024)S(1)}, s32[1024]{0:T(1024)}, u32[]{:S(2)}) copy-start(s32[1024]{0:T(1024)} %param.14) | copy-start | bytes 12292
  608.5 16.6 %copy-start.40 = (f32[8,128]{1,0:T(8,128)S(1)}, f32[8,128]{1,0:T(8,128)}, u32[]{:S(2)}) copy-start(f32[8,128]{1,0:T(8,128)} %shard_map.222) | copy-start | bytes 12292
  (36 other events, 99.8 us)

commit v3 on v2

--- a/solution.py
+++ b/solution.py
@@ -218,7 +218,7 @@
 CTX_SEMS = MP_SEMS + [pltpu.SemaphoreType.DMA((10,)), pltpu.SemaphoreType.DMA((10,))]
 
 
-def start_kernel(x_ref, id_ref, w_ref, xo, ido, wo, xs, xr, ids, idr, ws, wr, loc):
+def start_kernel(x_ref, id_ref, w_ref, xo, ido, wo, xs, xr, ids, idr, loc, *sems):
     c, m = place()
     upper = m >= MP // 2
     t = jnp.where(upper, CTX - 1 - c, c)
@@ -226,8 +226,7 @@
     for k in range(1, MP):
         sender = lax.rem(m + k, MP)
         signals.append((jnp.where(sender >= MP // 2, CTX - 1 - c, c), sender))
-    for k in range(1, CTX):
-        signals.append((lax.rem(c + k, CTX), m))
+    signals += ctx_neighbours()
     barrier = pltpu.get_barrier_semaphore()
     for target in signals:
         pl.semaphore_signal(barrier, inc=1, device_id=target, device_id_type=MESH)
@@ -235,23 +234,21 @@
     @pl.when(upper)
     def _():
         pl.semaphore_signal(barrier, inc=1, device_id=(CTX - 1 - c, m), device_id_type=MESH)
-        pl.semaphore_wait(barrier, MP + CTX - 1)
+        pl.semaphore_wait(barrier, MP + 4)
 
     @pl.when(jnp.logical_not(upper))
     def _():
-        pl.semaphore_wait(barrier, MP + CTX - 2)
-
-    own_w = pltpu.make_async_copy(w_ref, wo.at[c], loc.at[0])
-    own_w.start()
-    x_copies, id_copies, w_copies = [], [], []
+        pl.semaphore_wait(barrier, MP + 3)
+
+    ring = ctx_ring(w_ref, slots(wo), sems)
+    ring.start()
+    x_copies, id_copies = [], []
     for k in range(MP):
         target = (t, lax.rem(m + k, MP))
         x_copies.append(remote(x_ref, xo.at[m], xs.at[k], xr.at[k], target))
         id_copies.append(remote(id_ref, ido.at[m], ids.at[k], idr.at[k], target))
-    for k in range(1, CTX):
-        w_copies.append(remote(w_ref, wo.at[c], ws.at[k], wr.at[k], (lax.rem(c + k, CTX), m)))
-    own_x = pltpu.make_async_copy(x_ref, xo.at[m], loc.at[1])
-    own_id = pltpu.make_async_copy(id_ref, ido.at[m], loc.at[2])
+    own_x = pltpu.make_async_copy(x_ref, xo.at[m], loc.at[0])
+    own_id = pltpu.make_async_copy(id_ref, ido.at[m], loc.at[1])
 
     @pl.when(upper)
     def _():
@@ -266,14 +263,13 @@
     for k in range(1, MP):
         x_copies[k].start()
         id_copies[k].start()
-    for copy in w_copies:
-        copy.start()
+    ring.relay_near()
+    ring.relay_own()
+    ring.relay_far()
+    ring.finish()
     for k in range(1, MP):
         x_copies[k].wait()
         id_copies[k].wait()
-    for copy in w_copies:
-        copy.wait()
-    own_w.wait()
 
     @pl.when(upper)
     def _():
@@ -286,14 +282,20 @@
         own_id.wait()
 
 
-def keys_kernel(kv_ref, out, *sems):
-    greet(ctx_neighbours(), 4)
-    ring = ctx_ring(kv_ref, slots(out), sems)
+def keys_kernel(kv_ref, dy_ref, out, dy_out, *sems):
+    greet(ctx_neighbours() + mp_neighbours(), 7)
+    ring = ctx_ring(kv_ref, slots(out), sems[:5])
+    rows = mp_ring(dy_ref, slots(dy_out), sems[5:])
     ring.start()
+    rows.start()
     ring.relay_near()
     ring.relay_own()
+    rows.relay_near()
+    rows.relay_own()
     ring.relay_far()
+    rows.relay_far()
     ring.finish()
+    rows.finish()
 
 
 def gather_kernel(a_ref, out, *sems):
@@ -327,10 +329,16 @@
     own_a.wait()
 
 
-def scatter_kernel(a_ref, b_ref, ao, bo, s1, r1, s2, r2, loc):
+def scatter_kernel(
+    a_ref, b_ref, dp_ref, act_ref, in_ref, dgu_ref,
+    ao, bo, pair_ref,
+    terms, theirs, s1, r1, s2, r2, s3, r3, loc,
+):
     c, m = place()
+    core = lax.rem(c, 2)
+    sibling = (flip(c, 1), m)
     mates = [(c, lax.rem(m + k, MP)) for k in range(1, MP)]
-    greet(mates, MP - 1)
+    greet(mates + [sibling], MP)
     own_a = pltpu.make_async_copy(a_ref.at[m], ao.at[m], loc.at[0])
     own_a.start()
     own_b = pltpu.make_async_copy(b_ref.at[m], bo.at[m], loc.at[1])
@@ -342,38 +350,169 @@
         copies.append(remote(b_ref.at[to], bo.at[m], s2.at[k], r2.at[k], mates[k - 1]))
     for copy in copies:
         copy.start()
+    crossing = [
+        remote(terms.at[1 - core, e], theirs.at[e], s3.at[e], r3.at[e], sibling)
+        for e in range(4)
+    ]
+    for e in range(4):
+        gate_up_grads = dgu_ref[e]
+        active = act_ref[e]
+
+        def chunk(at, carry):
+            columns = pl.ds(pl.multiple_of(at * 256, 256), 256)
+            in_part = contract(in_ref[e, :, columns], gate_up_grads, 0, 0).astype(bf16)
+            out_part = contract(dp_ref[e, :, columns], active, 0, 0).astype(bf16)
+            for j in range(4):
+                rows = slice(64 * j, 64 * j + 64)
+                terms[j % 2, e, 2 * at + j // 2, :, 0:1024] = in_part[rows]
+                terms[j % 2, e, 2 * at + j // 2, :, 1024:1536] = out_part[rows]
+            return carry
+
+        lax.fori_loop(0, 4, chunk, 0)
+        crossing[e].start()
+    for e in range(4):
+        crossing[e].wait()
+
+        def add(chip, carry):
+            pair_ref[e, chip] = (
+                terms[core, e, chip].astype(f32) + theirs[e, chip].astype(f32)
+            ).astype(bf16)
+            return carry
+
+        lax.fori_loop(0, 8, add, 0)
     for copy in copies:
         copy.wait()
     own_a.wait()
     own_b.wait()
 
 
-def sibling_kernel(a_ref, out, send, recv):
+def scatter_rows(routed_terms, share, d_produced, active, incoming, d_gate_up):
+    return pl.pallas_call(
+        scatter_kernel,
+        out_shape=[
+            shape((MP, TOK, 1024)),
+            shape((MP, 8, TOK), f32),
+            shape((4, 8, 64, 1536)),
+        ],
+        in_specs=[ANY, ANY, VM, VM, VM, VM],
+        out_specs=[ANY, ANY, VM],
+        scratch_shapes=[
+            pltpu.VMEM((2, 4, 8, 64, 1536), bf16),
+            pltpu.VMEM((4, 8, 64, 1536), bf16),
+        ]
+        + [pltpu.SemaphoreType.DMA((MP,))] * 4
+        + [pltpu.SemaphoreType.DMA((4,))] * 2
+        + [pltpu.SemaphoreType.DMA((2,))],
+        compiler_params=pltpu.CompilerParams(
+            vmem_limit_bytes=VMEM_LIMIT, collective_id=4, has_side_effects=True
+        ),
+    )(routed_terms, share, d_produced, active, incoming, d_gate_up)
+
+
+def outputs_kernel(a_ref, ao, s1, r1, loc):
     c, m = place()
-    chip, core = c // 2, lax.rem(c, 2)
-    sibling = (chip * 2 + 1 - core, m)
-    greet([sibling], 1)
-    copy = remote(a_ref.at[:, 1 - core], out, send.at[0], recv.at[0], sibling)
-    copy.start()
-    copy.wait()
-
-
-def chips_kernel(a_ref, out, send, recv, loc):
-    c, m = place()
-    chip, core = c // 2, lax.rem(c, 2)
-    others = [(lax.rem(chip + k, 8) * 2 + core, m) for k in range(1, 8)]
-    greet(others, 7)
-    own = pltpu.make_async_copy(a_ref.at[chip], out.at[chip], loc.at[0])
-    own.start()
+    mates = [(c, lax.rem(m + k, MP)) for k in range(1, MP)]
+    greet(mates, MP - 1)
+    own_a = pltpu.make_async_copy(a_ref.at[m], ao.at[m], loc.at[0])
+    own_a.start()
     copies = []
-    for k in range(1, 8):
-        to = lax.rem(chip + k, 8)
-        copy = remote(a_ref.at[to], out.at[chip], send.at[k], recv.at[k], others[k - 1])
+    for k in range(1, MP):
+        to = lax.rem(m + k, MP)
+        copies.append(remote(a_ref.at[to], ao.at[m], s1.at[k], r1.at[k], mates[k - 1]))
+    for copy in copies:
         copy.start()
-        copies.append(copy)
     for copy in copies:
         copy.wait()
-    own.wait()
+    own_a.wait()
+
+
+def keys_grad_kernel(
+    a_ref, out, theirs, pair_a, pair_b, got_a, got_b, sum_a, sum_b, last_a, last_b,
+    s0, r0, s1, r1, s2, r2,
+):
+    c, m = place()
+    core = lax.rem(c, 2)
+    x, y = c // 4, lax.rem(c // 2, 2)
+    sibling = (flip(c, 1), m)
+    across = (flip(c, 2), m)
+    peers = [(lax.rem(c + 4 * k, CTX), m) for k in range(1, 4)]
+    greet(peers + [across, sibling], 5)
+    low, high = pl.ds(0, HALF), pl.ds(HALF, HALF)
+    crossing = [
+        remote(
+            a_ref.at[:, :, 1 - core, rows], theirs.at[:, :, rows], s0.at[at], r0.at[at], sibling
+        )
+        for at, rows in enumerate((high, low))
+    ]
+    for copy in crossing:
+        copy.start()
+
+    def add(a, b):
+        return a.astype(f32) + b.astype(f32)
+
+    crossing[0].wait()
+    for i in range(4):
+        for j in range(2):
+            pair_b[i, j] = add(a_ref[i, j, core, high], theirs[i, j, high]).astype(bf16)
+    first = [remote(pair_b.at[:, 1 - y], got_b, s1.at[0], r1.at[0], across)]
+    first[0].start()
+    crossing[1].wait()
+    for i in range(4):
+        for j in range(2):
+            pair_a[i, j] = add(a_ref[i, j, core, low], theirs[i, j, low]).astype(bf16)
+    for k in range(1, 4):
+        copy = remote(
+            pair_a.at[lax.rem(x + k, 4)], got_a.at[k - 1], s1.at[k], r1.at[k], peers[k - 1]
+        )
+        copy.start()
+        first.append(copy)
+    first[0].wait()
+    for i in range(4):
+        sum_b[i] = add(pair_b[i, y], got_b[i]).astype(bf16)
+    second = []
+    for k in range(1, 4):
+        copy = remote(
+            sum_b.at[lax.rem(x + k, 4)], last_b.at[k - 1], s2.at[k], r2.at[k], peers[k - 1]
+        )
+        copy.start()
+        second.append(copy)
+    for copy in first[1:]:
+        copy.wait()
+    for j in range(2):
+        sum_a[j] = (add(pair_a[x, j], got_a[0, j]) + add(got_a[1, j], got_a[2, j])).astype(bf16)
+    copy = remote(sum_a.at[1 - y], last_a, s2.at[0], r2.at[0], across)
+    copy.start()
+    second.append(copy)
+    for copy in second:
+        copy.wait()
+    out[low] = add(sum_a[y], last_a[...])
+    out[high] = add(sum_b[x], last_b[0]) + add(last_b[1], last_b[2])
+
+
+def keys_grad(terms):
+    piece = (HALF, 128)
+    return pl.pallas_call(
+        keys_grad_kernel,
+        out_shape=shape((BLOCK, 128), f32),
+        in_specs=[VM],
+        out_specs=VM,
+        scratch_shapes=[
+            pltpu.VMEM((4, 2, BLOCK, 128), bf16),
+            pltpu.VMEM((4, 2) + piece, bf16),
+            pltpu.VMEM((4, 2) + piece, bf16),
+            pltpu.VMEM((3, 2) + piece, bf16),
+            pltpu.VMEM((4,) + piece, bf16),
+            pltpu.VMEM((2,) + piece, bf16),
+            pltpu.VMEM((4,) + piece, bf16),
+            pltpu.VMEM(piece, bf16),
+            pltpu.VMEM((3,) + piece, bf16),
+        ]
+        + [pltpu.SemaphoreType.DMA((2,))] * 2
+        + [pltpu.SemaphoreType.DMA((4,))] * 4,
+        compiler_params=pltpu.CompilerParams(
+            vmem_limit_bytes=VMEM_LIMIT, collective_id=6, has_side_effects=True
+        ),
+    )(terms)
 
 
 def finish_kernel(a_ref, g_ref, ao, go, s1, r1, s2, r2, loc):
@@ -506,8 +645,8 @@
 
 
 def forward_kernel(
-    q_ref, kv_ref, in_ref, outw_ref, dy_ref, rows_ref,
-    out_ref, lse_ref, in_all, outw_all, dy_all, rows_all,
+    q_ref, kv_ref, in_ref, outw_ref, qw_ref, rows_ref,
+    out_ref, lse_ref, in_all, outw_all, qw_all, rows_all,
     best, total, summed, *sems,
 ):
     first_half = 2 * lax.axis_index("ctx")
@@ -518,7 +657,7 @@
     ]
     rows_rings = [
         mp_ring(rows_ref, slots(rows_all), sems[10:13]),
-        mp_ring(dy_ref, slots(dy_all), sems[13:16]),
+        mp_ring(qw_ref, slots(qw_all), sems[13:16]),
     ]
     for ring in weights_rings + rows_rings:
         ring.start()
@@ -542,26 +681,22 @@
     def step(index, carry):
         part, slot, diagonal = unit(index, first_half)
 
-        @pl.when(index == 11)
+        @pl.when(index == 12)
         def _():
+            for ring in weights_rings:
+                ring.relay_own()
+
+        @pl.when(index == 15)
+        def _():
+            for ring in weights_rings:
+                ring.relay_near()
             for ring in rows_rings:
                 ring.relay_near()
                 ring.relay_own()
 
-        @pl.when(index == 16)
+        @pl.when(index == 25)
         def _():
-            for ring in weights_rings:
-                ring.relay_near()
-                ring.relay_own()
-
-        @pl.when(index == 20)
-        def _():
-            for ring in rows_rings:
-                ring.relay_far()
-
-        @pl.when(index == 30)
-        def _():
-            for ring in weights_rings:
+            for ring in rows_rings + weights_rings:
                 ring.relay_far()
 
         @pl.when(diagonal)
@@ -582,7 +717,7 @@
         ring.finish()
 
 
-def attention(q_rows, kv_all, w_in, w_out_t, dy, out_rows_w):
+def attention(q_rows, kv_all, w_in, w_out_t, qkv_w, out_rows_w):
     rows = q_rows.shape[1]
     return pl.pallas_call(
         forward_kernel,
@@ -591,7 +726,7 @@
             shape((2, 1, rows), f32),
             shape((4, 1024, 1024)),
             shape((4, 1024, 512)),
-            shape((MP, TOK, 1024)),
+            shape((MP,) + qkv_w.shape),
             shape((MP, TOK, 1024)),
         ],
         in_specs=[VM, VM, ANY, ANY, ANY, ANY],
@@ -609,12 +744,12 @@
         cost_estimate=pl.CostEstimate(
             flops=33 * 4 * HALF * rows * 256, bytes_accessed=1 << 23, transcendentals=33 * HALF * rows
         ),
-    )(q_rows, kv_all, w_in, w_out_t, dy, out_rows_w)
+    )(q_rows, kv_all, w_in, w_out_t, qkv_w, out_rows_w)
 
 
 def backward_kernel(
-    q_ref, do_ref, lse_ref, delta_ref, kv_ref, pair_ref, br_ref, qw_ref,
-    dkv_ref, dq_ref, grad_ref, br_all, qw_all,
+    q_ref, do_ref, lse_ref, delta_ref, kv_ref, pair_ref, br_ref,
+    dkv_ref, dq_ref, in_grad, out_grad, br_all,
     total, got_a, got_b, sum_a, sum_b, last_a, last_b, *sems,
 ):
     c, m = place()
@@ -624,10 +759,7 @@
     across = (flip(c, 2), m)
     greet(peers + [across] + mp_neighbours(), 7)
     sa, ra, sb, rb = sems[:4]
-    rings = [
-        mp_ring(br_ref, slots(br_all), sems[4:7]),
-        mp_ring(qw_ref, slots(qw_all), sems[7:10]),
-    ]
+    ring = mp_ring(br_ref, slots(br_all), sems[4:7])
 
     def first_copies():
         copies = [
@@ -654,8 +786,7 @@
 
     for copy in first_copies():
         copy.start()
-    for ring in rings:
-        ring.start()
+    ring.start()
     dq_ref[...] = jnp.zeros(dq_ref.shape, f32)
 
     def clear(index, carry):
@@ -697,18 +828,16 @@
     def step(index, carry):
         part, slot, diagonal = unit(index, first_half)
 
-        @pl.when(index == 11)
+        @pl.when(index == 7)
         def _():
-            for ring in rings:
-                ring.relay_near()
-                ring.relay_own()
+            ring.relay_near()
+            ring.relay_own()
+
+        @pl.when(index == 14)
+        def _():
+            ring.relay_far()
 
         @pl.when(index == 21)
-        def _():
-            for ring in rings:
-                ring.relay_far()
-
-        @pl.when(index == 23)
         def _():
             middle()
 
@@ -729,19 +858,25 @@
         return carry
 
     lax.fori_loop(0, 2 * CTX, write, 0)
-    for ring in rings:
-        ring.finish()
+    ring.finish()
     for copy in second_copies():
         copy.wait()
     for e in range(2):
-        grad_ref[e] = sum_a[e, y].astype(f32) + last_a[e].astype(f32)
-        term = sum_b[e, x].astype(f32)
-        for k in range(3):
-            term = term + last_b[k, e].astype(f32)
-        grad_ref[2 + e] = term
-
-
-def attention_back(q_rows, do_rows, lse, delta, kv_all, pair, branch_grad, qkv_w):
+        for at, term in (
+            (e, sum_a[e, y].astype(f32) + last_a[e].astype(f32)),
+            (
+                2 + e,
+                sum_b[e, x].astype(f32)
+                + last_b[0, e].astype(f32)
+                + last_b[1, e].astype(f32)
+                + last_b[2, e].astype(f32),
+            ),
+        ):
+            in_grad[at] = term[:, :1024]
+            out_grad[at] = term[:, 1024:]
+
+
+def attention_back(q_rows, do_rows, lse, delta, kv_all, pair, branch_grad):
     rows = q_rows.shape[1]
     wide = pair.shape[-1]
     return pl.pallas_call(
@@ -749,12 +884,12 @@
         out_shape=[
             shape(kv_all.shape, bf16),
             shape((2, 2 * HEAD, rows), f32),
-            shape((4, 64, wide), f32),
+            shape((4, 64, 1024), f32),
+            shape((4, 64, 512), f32),
             shape((MP, TOK, 1024)),
-            shape((MP,) + qkv_w.shape),
         ],
-        in_specs=[VM] * 6 + [ANY] * 2,
-        out_specs=[VM] * 3 + [ANY] * 2,
+        in_specs=[VM] * 6 + [ANY],
+        out_specs=[VM] * 4 + [ANY],
         scratch_shapes=[
             pltpu.VMEM(kv_all.shape, f32),
             pltpu.VMEM((3, 2, 2, 64, wide), bf16),
@@ -765,14 +900,14 @@
             pltpu.VMEM((3, 2, 64, wide), bf16),
         ]
         + [pltpu.SemaphoreType.DMA((4,))] * 4
-        + MP_SEMS * 2,
+        + MP_SEMS,
         compiler_params=pltpu.CompilerParams(
             vmem_limit_bytes=VMEM_LIMIT, collective_id=11, has_side_effects=True
         ),
         cost_estimate=pl.CostEstimate(
             flops=33 * 10 * HALF * rows * 256, bytes_accessed=1 << 24, transcendentals=33 * HALF * rows
         ),
-    )(q_rows, do_rows, lse, delta, kv_all, pair, branch_grad, qkv_w)
+    )(q_rows, do_rows, lse, delta, kv_all, pair, branch_grad)
 
 
 def phases(positions, head_width):
@@ -865,7 +1000,7 @@
             shape((MP, 16, TOK), jnp.int32),
             shape((CTX, 64, 512)),
         ],
-        [MP, MP, MP, MP, CTX, CTX, 3],
+        [MP, MP, MP, MP, 2] + CTX_SEMS,
         4 << 20,
     )
     inputs = x_all.reshape(BLOCK, 1024).astype(f32)
@@ -890,12 +1025,17 @@
     q_rows = jnp.concatenate([q_rows, jnp.zeros_like(q_rows)], axis=-1)
     keys = rotate(qkv[:, 128:192], cosine, sine).astype(bf16)
     kv_new = jnp.concatenate([keys, qkv[:, 192:].astype(bf16)], axis=-1)
-    (kv_all,) = comm_call(
-        keys_kernel, 2, [kv_new], [shape((CTX, BLOCK, 128))], CTX_SEMS, 4 << 20
+    kv_all, dy_all = comm_call(
+        keys_kernel,
+        2,
+        [kv_new, dy_swapped],
+        [shape((CTX, BLOCK, 128)), shape((MP, TOK, 1024))],
+        CTX_SEMS + MP_SEMS,
+        6 << 20,
     )
     kv_all = kv_all.reshape(2 * CTX, HALF, 128)
-    out_cols, lse, in_w, out_w_t, dy_all, out_w_all = attention(
-        q_rows, kv_all, w_in, w_out.transpose(0, 2, 1), dy_swapped, out_w
+    out_cols, lse, in_w, out_w_t, qkv_w_all, out_w_all = attention(
+        q_rows, kv_all, w_in, w_out.transpose(0, 2, 1), qkv_w, out_w
     )
     dy_all = dy_all.reshape(BLOCK, 1024)
     attended = (
@@ -964,13 +1104,8 @@
     routed_terms = routed_terms.astype(bf16).reshape(MP, TOK, 1024)
     share = jnp.sum(jnp.where(place_bool, slot_share[:, :, None], 0.0), axis=1)
     share = jnp.pad(share.reshape(4, MP, TOK).transpose(1, 0, 2), ((0, 0), (0, 4), (0, 0)))
-    routed_got, share_got = comm_call(
-        scatter_kernel,
-        4,
-        [routed_terms, share],
-        [shape((MP, TOK, 1024)), shape((MP, 8, TOK), f32)],
-        [MP, MP, MP, MP, 2],
-        4 << 20,
+    routed_got, share_got, pair = scatter_rows(
+        routed_terms, share, d_produced, active, incoming, d_gate_up
     )
 
     def own_rows(array):
@@ -1004,35 +1139,14 @@
     branch_grad = (branch_scale * hidden_grad).astype(bf16)
     hidden_grad_home = swap_home(hidden_grad)
 
-    out_expert_grad = jnp.einsum(
-        "esd,esf->edf", d_produced, active, preferred_element_type=f32
-    ).astype(bf16)
-    in_expert_grad = jnp.einsum(
-        "esd,esf->edf", incoming, d_gate_up, preferred_element_type=f32
-    ).astype(bf16)
-    in_terms = in_expert_grad.reshape(4, 8, 2, 64, 1024)
-    out_terms = out_expert_grad.reshape(4, 8, 2, 64, 512)
     out_grad_terms = jnp.einsum(
         "td,hfd->htf", branch_grad, out_w_all, preferred_element_type=f32
     ).astype(bf16)
-    out_grad, in_theirs, out_theirs = comm_call(
-        outputs_kernel,
-        5,
-        [out_grad_terms, in_terms, out_terms],
-        [shape((MP, TOK, 128)), shape((4, 8, 64, 1024)), shape((4, 8, 64, 512))],
-        [MP, MP, 2, 2, 1],
-        8 << 20,
+    (out_grad,) = comm_call(
+        outputs_kernel, 5, [out_grad_terms], [shape((MP, TOK, 128))], [MP, MP, 1], 1 << 20
     )
     out_grad = out_grad.reshape(BLOCK, 128)
-    core = lax.rem(c, 2)
-
-    def with_sibling(own, theirs):
-        mine = lax.dynamic_index_in_dim(own, core, 2, False)
-        return (mine.astype(f32) + theirs.astype(f32)).astype(bf16)
-
-    pair = jnp.concatenate(
-        [with_sibling(in_terms, in_theirs), with_sibling(out_terms, out_theirs)], axis=-1
-    ).reshape(4, 4, 2, 64, 1536)
+    pair = pair.reshape(4, 4, 2, 64, 1536)
 
     mixed_got = lax.all_to_all(mixed, "mp", split_axis=0, concat_axis=0, tiled=True)
     outputs = (hidden_own + jnp.sum(mixed_got.astype(f32), axis=0)).astype(bf16)
@@ -1041,20 +1155,11 @@
     do_rows = heads_to_rows(out_grad)
     delta = jnp.sum(do_rows.astype(f32) * heads_to_rows(attended), axis=-1)[:, None, :]
     do_rows = jnp.concatenate([jnp.zeros_like(do_rows), do_rows], axis=-1)
-    dkv_terms, dq_cols, expert_grad, branch_rows, qkv_w_all = attention_back(
-        q_rows, do_rows, lse, delta, kv_all, pair, branch_grad, qkv_w
+    dkv_terms, dq_cols, in_w_grad, out_w_grad_t, branch_rows = attention_back(
+        q_rows, do_rows, lse, delta, kv_all, pair, branch_grad
     )
     branch_rows = branch_rows.reshape(BLOCK, 1024)
-    dkv_terms = dkv_terms.reshape(8, 2, BLOCK, 128)
-    (theirs,) = comm_call(
-        sibling_kernel, 6, [dkv_terms], [shape((8, BLOCK, 128))], [1, 1], 4 << 20
-    )
-    mine = lax.dynamic_index_in_dim(dkv_terms, lax.rem(c, 2), 1, False)
-    pair = (mine.astype(f32) + theirs.astype(f32)).astype(bf16)
-    (dkv_got,) = comm_call(
-        chips_kernel, 7, [pair], [shape((8, BLOCK, 128))], [8, 8, 1], 4 << 20
-    )
-    dkv = jnp.sum(dkv_got.astype(f32), axis=0)
+    dkv = keys_grad(dkv_terms.reshape(4, 2, 2, BLOCK, 128))
     d_key = rotate_back(dkv[:, :HEAD], cosine, sine).astype(bf16)
     d_value = dkv[:, HEAD:].astype(bf16)
     dq = score_scale * dq_cols[:, :HEAD, :]
@@ -1100,8 +1205,8 @@
         w_grad[:, 256:].T,
         sums[:, 33],
         sums[:, :32],
-        expert_grad[..., :1024],
-        expert_grad[..., 1024:].transpose(0, 2, 1),
+        in_w_grad,
+        out_w_grad_t.transpose(0, 2, 1),
     )
 
 

time: 636 us -> 593 us (0.932)
  Pallas kernels: 420 us -> 389 us
  other arithmetic: 55.7 us -> 39.3 us
  matrix products: 63.1 us -> 49.1 us
  local copies, waits for them, and re-layouts: 55.6 us -> 69.3 us
    pallas_call x8 -> x5, Pallas kernels: 221 us -> 141 us  [comm_call(): pl.pallas_call(kernel, out_shape=outs, in_specs=[ANY] * len(arrays), out_...]
    pallas_call x0 -> x2, Pallas kernels: none -> 68.1 us  [the longest x1 35.9 us: scatter_rows(): pl.pallas_call(scatter_kernel, out_shape=[shape((MP, TOK, 1024)), shape((...]
    dot_general x2 -> x0, matrix products: 14 us -> none  [the longest x1 6.99 us: body(): jnp.einsum('esd,esf->edf', d_produced, active, preferred_element_type=f32)]
    convert_element_type x3 -> x1, other arithmetic: 12.9 us -> 0.31 us  [body(): d_produced = (branch_scale * slot_gate[..., None] * dy_rows).astype(bf16)]
    pallas_call x1, Pallas kernels: 98.8 us -> 87.6 us  [attention_back(): pl.pallas_call(backward_kernel, out_shape=[shape(kv_all.shape, bf16), sha...]
    unnamed x121 -> x124, local copies, waits for them, and re-layouts: 9.82 us -> 17.9 us
    pallas_call x1, Pallas kernels: 81.5 us -> 74 us  [attention(): pl.pallas_call(forward_kernel, out_shape=[shape((2, HEAD, rows), f32), sh...]
  transfers between devices with their start and end apart: 4 -> 4, of which waited for: 1 -> 1; matrix products, arithmetic and copies ran while one was open for 12% -> 15% of each run, Pallas kernels for 15% -> 16%
where the time goes in v3:
time: 593 us; the launch traced here: 583 us
  Pallas kernels  389 us (66%)
  local copies, waits for them, and re-layouts  69.3 us (12%)
  matrix products  49.1 us (8%)
  other arithmetic  39.3 us (7%)
  starting transfers between devices  19.6 us (3%)
  waiting for transfers between devices  13.7 us (2%)
    pallas_call x5, Pallas kernels, comm_call(): pl.pallas_call(kernel, out_shape=outs, in_specs=[ANY] * len(arrays), out_...  141 us
    pallas_call x1, Pallas kernels, attention_back(): pl.pallas_call(backward_kernel, out_shape=[shape(kv_all.shape, bf16), sha...  87.6 us
    pallas_call x1, Pallas kernels, attention(): pl.pallas_call(forward_kernel, out_shape=[shape((2, HEAD, rows), f32), sh...  74 us
    pallas_call x1, Pallas kernels, scatter_rows(): pl.pallas_call(scatter_kernel, out_shape=[shape((MP, TOK, 1024)), shape((...  35.9 us
    pallas_call x1, Pallas kernels, keys_grad(): pl.pallas_call(keys_grad_kernel, out_shape=shape((BLOCK, 128), f32), in_s...  32.2 us
    pallas_call x1, Pallas kernels, small_sums(): pl.pallas_call(sums_kernel, out_shape=shape(dims, f32), in_specs=[VM], ou...  18.9 us
    dot_general x5, matrix products, contract(): lax.dot_general(left, right, (((left_dim,), (right_dim,)), ((), ())), pre...  18.8 us
    unnamed x124, local copies, waits for them, and re-layouts  17.9 us
  transfers between devices with their start and end apart: 4, of which 1 were waited for; matrix products, arithmetic and copies ran while one was open for 15% of the time, Pallas kernels for 16%

profile of v3, /device:TPU:65, one launch (start us, length us, event | category | flops | bytes accessed | tf_op | source)
XLA Modules:
  0.0 582.7 jit_solution(7970849655439933014)
XLA Ops:
  0.7 6.0 %collective-permute-start = (bf16[128,1024]{1,0:T(8,128)(2,1)}, bf16[128,1024]{1,0:T(8,128)(2,1)}, u32[]{:S(2)}, u32[]{:S(2)}) collective-permute-start(bf16[128,1024]{1,0:T(8,128)(2,1)} %param.25), channel_id=1, source_target_pairs={{0,0},{1,1},{2,2},{3,3},{4,124},{5,125},{6,126},{7,127},{8,8},{9,9... | collective-permute-start | bytes 786440 | tf_op jit(solution)/shard_map/ppermute | solution.py:953
  12.0 60.0 %shard_map.212 = (bf16[8,128,1024]{2,1,0:T(8,128)(2,1)}, s32[8,16,128]{2,1,0:T(8,128)}, bf16[16,64,512]{2,1,0:T(8,128)(2,1)}) custom-call(bf16[128,1024]{1,0:T(8,128)(2,1)} %x_ref.1, s32[16,128]{1,0:T(8,128)} %add_add_fusion.id_ref, bf16[64,512]{1,0:T(8,128)(2,1)} %concatenate.60.w_ref), custom_call_target="tpu_custom_call" | custom-call | bytes 4194304 | tf_op jit(solution)/shard_map/pallas_call | solution.py:54
  118.4 30.3 %shard_map.213 = (bf16[16,1024,128]{2,1,0:T(8,128)(2,1)}, bf16[8,128,1024]{2,1,0:T(8,128)(2,1)}) custom-call(bf16[1024,128]{1,0:T(8,128)(2,1)} %pad_maximum_fusion.5.kv_ref, bf16[128,1024]{1,0:T(8,128)(2,1)} %collective-permute-done.dy_ref), custom_call_target="tpu_custom_call" | custom-call | bytes 6291456 | tf_op jit(solution)/shard_map/pallas_call | solution.py:54
  148.6 74.0 %shard_map.214 = (f32[2,64,1024]{2,1,0:T(8,128)}, f32[2,1,1024]{2,1,0:T(1,128)}, bf16[4,1024,1024]{2,1,0:T(8,128)(2,1)}, bf16[4,1024,512]{2,1,0:T(8,128)(2,1)}, ...) custom-call(bf16[2,1024,128]{2,1,0:T(8,128)(2,1)} %concatenate.65.q_ref, bf16[32,512,128]{2,1,0:T(8,128)(2,1)} %bitcast.182, ...), custom_call_target="tpu_custom_call" | custom-call | flops 17716740096 | bytes 8388608 | tf_op jit(solution)/shard_map/pallas_call | solution.py:722
  229.0 22.6 %shard_map.215 = bf16[8,1024,128]{2,1,0:T(8,128)(2,1)} custom-call(bf16[1024,128]{1,0:T(8,128)(2,1)} %copy.147.a_ref), custom_call_target="tpu_custom_call" | custom-call | bytes 4194304 | tf_op jit(solution)/shard_map/pallas_call | solution.py:54
  251.6 4.8 multiply_reduce_fusion
  258.9 3.1 convolution_convert_fusion
  275.2 4.4 fusion.7
  279.9 3.4 multiply_convert_fusion.3
  283.4 6.0 %all-to-all-start = ((bf16[8,128,1024]{2,1,0:T(8,128)(2,1)}), bf16[8,128,1024]{2,1,0:T(8,128)(2,1)S(1)}, u32[]{:S(2)}, u32[]{:S(2)}) async-start(bf16[8,128,1024]{2,1,0:T(8,128)(2,1)} %bitcast.156), calls=%async_computation | async-start | bytes 4194304 | tf_op jit(solution)/shard_map/all_to_all | solution.py:1151
  289.4 10.8 %bitcast_convert_fusion = bf16[1024,1024]{1,0:T(8,128)(2,1)} fusion(s32[4,1024]{1,0:T(4,128)S(1)} %copy-done.42, bf16[4,1024,1024]{2,1,0:T(8,128)(2,1)} %get-tuple-element.42, bf16[4,288,512]{2,1,0:T(8,128)(2,1)} %get-tuple-element.70, bf16[4,288,512]{2,1,0:T(8,128)(2,1)} %get-tuple-element.69), kind=kOutput, calls=%fused_computation.14 | convolution fusion | flops 4839964672 | bytes 12861440 | tf_op jit(solution)/shard_map/dot_general | solution.py:30
  303.7 3.4 pad_maximum_fusion.dgu_ref
  307.1 35.9 %shard_map.216 = (bf16[8,128,1024]{2,1,0:T(8,128)(2,1)}, f32[8,8,128]{2,1,0:T(8,128)}, bf16[4,8,64,1536]{3,2,1,0:T(8,128)(2,1)}) custom-call(bf16[8,128,1024]{2,1,0:T(8,128)(2,1)} %bitcast.153, f32[8,8,128]{2,1,0:T(8,128)} %pad.6.b_ref, bf16[4,288,1024]{2,1,0:T(8,128)(2,1)} %copy-done.3, bf16[4,288,512]{2,1,0:T(8,128)(2,1)} %copy-done.2, ...), custom_call_target="tpu_custom_call" | custom-call | tf_op jit(solution)/shard_map/pallas_call | solution.py:390
  348.8 3.1 multiply_reduce_fusion.1
  362.2 7.6 %shard_map.217 = bf16[8,128,128]{2,1,0:T(8,128)(2,1)} custom-call(bf16[8,128,128]{2,1,0:T(8,128)(2,1)} %fusion.24.a_ref), custom_call_target="tpu_custom_call" | custom-call | bytes 1048576 | tf_op jit(solution)/shard_map/pallas_call | solution.py:54
  373.5 87.6 %shard_map.218 = (bf16[32,512,128]{2,1,0:T(8,128)(2,1)}, f32[2,128,1024]{2,1,0:T(8,128)}, f32[4,64,1024]{2,1,0:T(8,128)}, f32[4,64,512]{2,1,0:T(8,128)}, bf16[8,128,1024]{2,1,0:T(8,128)(2,1)}) custom-call(bf16[2,1024,128]{2,1,0:T(8,128)(2,1)} %concatenate.65.q_ref, bf16[2,1024,128]{2,1,0:T(8,128)(2,1)} %concatenate.69.do_ref, ...), custom_call_target="tpu_custom_call" | custom-call | flops 44291850240 | bytes 16777216 | tf_op jit(solution)/shard_map/pallas_call | solution.py:882
  461.1 32.2 %shard_map.219 = f32[1024,128]{1,0:T(8,128)} custom-call(bf16[4,2,2,1024,128]{4,3,2,1,0:T(8,128)(2,1)} %bitcast.149), custom_call_target="tpu_custom_call" | custom-call | tf_op jit(solution)/shard_map/pallas_call | solution.py:494
  501.1 2.9 copy.162
  509.0 20.4 %shard_map.220 = (bf16[8,128,256]{2,1,0:T(8,128)(2,1)}, bf16[16,64,384]{2,1,0:T(8,128)(2,1)}) custom-call(bf16[8,128,256]{2,1,0:T(8,128)(2,1)} %bitcast.158, bf16[16,64,384]{2,1,0:T(8,128)(2,1)} %pad_maximum_fusion.1.g_ref), custom_call_target="tpu_custom_call" | custom-call | bytes 5242880 | tf_op jit(solution)/shard_map/pallas_call | solution.py:54
  529.5 4.0 fusion.39
  535.0 18.9 %shard_map.221 = f32[8,128]{1,0:T(8,128)} custom-call(f32[16,8,8,128]{3,2,1,0:T(8,128)} %maximum_maximum_fusion.a_ref), custom_call_target="tpu_custom_call" | custom-call | tf_op jit(solution)/shard_map/pallas_call | solution.py:613
  553.9 4.0 collective-permute-start.2
  558.8 3.6 collective-permute-start.1
  564.6 13.7 %collective-permute-done.1 = bf16[128,1024]{1,0:T(8,128)(2,1)S(1)} collective-permute-done((bf16[128,1024]{1,0:T(8,128)(2,1)}, bf16[128,1024]{1,0:T(8,128)(2,1)S(1)}, u32[]{:S(2)}, u32[]{:S(2)}) %collective-permute-start.1) | collective-permute-done | bytes 262176 | tf_op jit(solution)/shard_map/ppermute | solution.py:953
  (244 shorter events, 117.8 us)
Async XLA Ops:
  0.6 8.4 %copy-start = (s32[1024]{0:T(1024)S(1)}, s32[1024]{0:T(1024)}, u32[]{:S(2)}) copy-start(s32[1024]{0:T(1024)} %param.14) | copy-start | bytes 12292
  0.7 117.7 %collective-permute-start = (bf16[128,1024]{1,0:T(8,128)(2,1)}, bf16[128,1024]{1,0:T(8,128)(2,1)}, u32[]{:S(2)}, u32[]{:S(2)}) collective-permute-start(bf16[128,1024]{1,0:T(8,128)(2,1)} %param.25), channel_id=1, source_target_pairs={{0,0},{1,1},{2,2},{3,3},{4,124},{5,125},{6,126},{7,127},{8,8},{9,9... | collective-permute-start | bytes 786440 | tf_op jit(solution)/shard_map/ppermute | solution.py:953
  73.6 185.1 %copy-start.39 = (f32[1024]{0:T(1024)}, f32[1024]{0:T(1024)S(1)}, u32[]{:S(2)}) copy-start(f32[1024]{0:T(1024)S(1)} %get-tuple-element.59) | copy-start | bytes 12292
  85.1 7.5 %slice-start = ((f32[1024,256]{0,1:T(8,128)}), f32[1024,64]{0,1:T(8,128)S(1)}, s32[]{:S(2)}) async-start(f32[1024,256]{0,1:T(8,128)} %copy-done.11), calls=%async_computation.1 | async-start | bytes 524288 | tf_op jit(solution)/shard_map/slice | solution.py:1026
  93.6 4.8 copy-start.28
  96.7 18.7 %copy-start.41 = (s32[4,1024]{1,0:T(4,128)}, s32[4,1024]{1,0:T(4,128)S(1)}, u32[]{:S(2)}) copy-start(s32[4,1024]{1,0:T(4,128)S(1)} %fusion.29) | copy-start | bytes 49156
  224.9 26.7 %copy-start.6 = (bf16[8,128,1024]{2,1,0:T(8,128)(2,1)S(1)}, bf16[8,128,1024]{2,1,0:T(8,128)(2,1)}, u32[]{:S(2)}) copy-start(bf16[8,128,1024]{2,1,0:T(8,128)(2,1)} %get-tuple-element.34) | copy-start | bytes 6291460
  256.4 7.0 %slice-start.1 = ((s8[8388608]{0:T(1024)(128)(4,1)}), s8[4194304]{0:T(1024)(128)(4,1)S(1)}, s32[]{:S(2)}) async-start(s8[8388608]{0:T(1024)(128)(4,1)} %bitcast.185), calls=%async_computation.2 | async-start | bytes 8388608
  258.9 4.6 slice-start.2
  283.4 73.9 %all-to-all-start = ((bf16[8,128,1024]{2,1,0:T(8,128)(2,1)}), bf16[8,128,1024]{2,1,0:T(8,128)(2,1)S(1)}, u32[]{:S(2)}, u32[]{:S(2)}) async-start(bf16[8,128,1024]{2,1,0:T(8,128)(2,1)} %bitcast.156), calls=%async_computation | async-start | bytes 4194304 | tf_op jit(solution)/shard_map/all_to_all | solution.py:1151
  346.8 5.2 copy-start.50
  360.6 10.9 %copy-start.27 = (bf16[128,1024]{1,0:T(8,128)(2,1)}, bf16[128,1024]{1,0:T(8,128)(2,1)S(1)}, u32[]{:S(2)}) copy-start(bf16[128,1024]{1,0:T(8,128)(2,1)S(1)} %get-tuple-element.67.br_ref) | copy-start | bytes 786436
  360.6 10.4 %copy-start.7 = (f32[2,64,2,512]{3,2,1,0:T(2,128)S(1)}, f32[2,64,2,512]{3,2,1,0:T(2,128)}, u32[]{:S(2)}) copy-start(f32[2,64,2,512]{3,2,1,0:T(2,128)} %reshape.232) | copy-start | bytes 1572868
  461.1 35.2 %copy-start.38 = (f32[2,128,1024]{2,1,0:T(8,128)S(1)}, f32[2,128,1024]{2,1,0:T(8,128)}, u32[]{:S(2)}) copy-start(f32[2,128,1024]{2,1,0:T(8,128)} %get-tuple-element.49) | copy-start | bytes 3145732
  507.3 22.2 %copy-start.13 = (bf16[128,1024]{1,0:T(8,128)(2,1)S(1)}, bf16[128,1024]{1,0:T(8,128)(2,1)}, u32[]{:S(2)}) copy-start(bf16[128,1024]{1,0:T(8,128)(2,1)} %x_ref.1) | copy-start | bytes 786436
  507.3 22.2 %copy-start.45 = (f32[1024]{0:T(1024)S(1)}, f32[1024]{0:T(1024)}, u32[]{:S(2)}) copy-start(f32[1024]{0:T(1024)} %copy-done.44) | copy-start | bytes 12292
  507.3 22.2 %copy-start.51 = (f32[128]{0:T(128)S(1)}, f32[128]{0:T(128)}, u32[]{:S(2)}) copy-start(f32[128]{0:T(128)} %add_rsqrt_fusion.2) | copy-start | bytes 1540
  529.5 4.4 copy-start.18
  533.5 24.5 %copy-start.36 = (bf16[16,64,384]{2,1,0:T(8,128)(2,1)S(1)}, bf16[16,64,384]{2,1,0:T(8,128)(2,1)}, u32[]{:S(2)}) copy-start(bf16[16,64,384]{2,1,0:T(8,128)(2,1)} %get-tuple-element.54) | copy-start | bytes 2359300
  535.0 45.5 %copy-start.35 = (f32[4,64,1024]{2,1,0:T(8,128)S(1)}, f32[4,64,1024]{2,1,0:T(8,128)}, u32[]{:S(2)}) copy-start(f32[4,64,1024]{2,1,0:T(8,128)} %get-tuple-element.116) | copy-start | bytes 3145732
  553.9 26.0 %copy-start.43 = (f32[8,128]{1,0:T(8,128)S(1)}, f32[8,128]{1,0:T(8,128)}, u32[]{:S(2)}) copy-start(f32[8,128]{1,0:T(8,128)} %shard_map.221) | copy-start | bytes 12292
  553.9 24.3 %collective-permute-start.2 = (f32[128,1024]{1,0:T(8,128)}, f32[128,1024]{1,0:T(8,128)S(1)}, u32[]{:S(2)}, u32[]{:S(2)}) collective-permute-start(f32[128,1024]{1,0:T(8,128)} %get-tuple-element.68), channel_id=1, source_target_pairs={{0,0},{1,1},{2,2},{3,3},{4,124},{5,125},{6,126},{7,127},{8,8},{9,9... | collective-permute-start | bytes 1572872 | tf_op jit(solution)/shard_map/ppermute | solution.py:953
  558.1 23.4 %copy-start.37 = (f32[4,64,512]{2,1,0:T(8,128)S(1)}, f32[4,64,512]{2,1,0:T(8,128)}, u32[]{:S(2)}) copy-start(f32[4,64,512]{2,1,0:T(8,128)} %get-tuple-element.56) | copy-start | bytes 1572868
  558.8 19.4 %collective-permute-start.1 = (bf16[128,1024]{1,0:T(8,128)(2,1)}, bf16[128,1024]{1,0:T(8,128)(2,1)S(1)}, u32[]{:S(2)}, u32[]{:S(2)}) collective-permute-start(bf16[128,1024]{1,0:T(8,128)(2,1)} %get-tuple-element.71), channel_id=1, source_target_pairs={{0,0},{1,1},{2,2},{3,3},{4,124},{5,125},{6,126},{7,127},{8,8},{9,9... | collective-permute-start | bytes 786440 | tf_op jit(solution)/shard_map/ppermute | solution.py:953
  (37 other events, 90.9 us)

commit v4 on v3

--- a/solution.py
+++ b/solution.py
@@ -282,51 +282,99 @@
         own_id.wait()
 
 
-def keys_kernel(kv_ref, dy_ref, out, dy_out, *sems):
+def lanes(rows):
+    return lax.broadcasted_iota(jnp.int32, (rows, 128), 1)
+
+
+def phase_rows(ref, at, rows):
+    part = ref[:, at : at + rows]
+    return jnp.concatenate([part] * 4, axis=0).T
+
+
+def turn(values, cosine, sine):
+    first = lax.rem(lanes(values.shape[0]), HEAD) < HEAD // 2
+    turned = jnp.where(first, -pltpu.roll(values, 96, 1), pltpu.roll(values, 32, 1))
+    return values * cosine + turned * sine
+
+
+def turn_back(grads, cosine, sine):
+    first = lax.rem(lanes(grads.shape[0]), HEAD) < HEAD // 2
+    scaled = grads * sine
+    turned = jnp.where(first, pltpu.roll(scaled, 96, 1), -pltpu.roll(scaled, 32, 1))
+    return grads * cosine + turned
+
+
+def keys_kernel(
+    x_ref, gain_ref, w_ref, cos_ref, sin_ref, dy_ref,
+    normed_ref, q_ref, kv_out, dy_out,
+    kv_own, *sems,
+):
     greet(ctx_neighbours() + mp_neighbours(), 7)
-    ring = ctx_ring(kv_ref, slots(out), sems[:5])
+    ring = ctx_ring(kv_own, slots(kv_out), sems[:5])
     rows = mp_ring(dy_ref, slots(dy_out), sems[5:])
+    rows.start()
+    size = 256
+    low = lanes(size) < HEAD
+    for part in range(4):
+        at = part * size
+        block = slice(at, at + size)
+        x = x_ref[block].astype(f32)
+        inverse = lax.rsqrt(jnp.mean(x * x, axis=1, keepdims=True) + epsilon)
+        normed = (x * inverse * gain_ref[...]).astype(bf16)
+        normed_ref[block] = normed
+        qkv = jnp.dot(normed, w_ref[...], preferred_element_type=f32)
+        cosine, sine = phase_rows(cos_ref, at, size), phase_rows(sin_ref, at, size)
+        queries = turn(qkv[:, :128], cosine, sine).astype(bf16).astype(f32) * score_scale
+        half, place_in = part // 2, at % HALF
+        q_ref[half, place_in : place_in + size] = jnp.where(low, queries, 0.0).astype(bf16)
+        q_ref[half, HALF + place_in : HALF + place_in + size] = jnp.where(
+            low, pltpu.roll(queries, HEAD, 1), 0.0
+        ).astype(bf16)
+        kv = qkv[:, 128:]
+        kv_own[block] = jnp.where(low, turn(kv, cosine, sine), kv).astype(bf16)
     ring.start()
-    rows.start()
+    rows.relay_near()
+    rows.relay_own()
     ring.relay_near()
     ring.relay_own()
-    rows.relay_near()
-    rows.relay_own()
+    rows.relay_far()
     ring.relay_far()
-    rows.relay_far()
+    rows.finish()
     ring.finish()
-    rows.finish()
-
-
-def gather_kernel(a_ref, out, *sems):
-    greet(mp_neighbours(), 3)
-    ring = mp_ring(a_ref, slots(out), sems)
+
+
+def keys_and_values(x_all, gain, qkv_w, cosine, sine, dy):
+    return pl.pallas_call(
+        keys_kernel,
+        out_shape=[
+            shape((BLOCK, 1024)),
+            shape((2, 2 * HALF, 128)),
+            shape((CTX, BLOCK, 128)),
+            shape((MP, TOK, 1024)),
+        ],
+        in_specs=[VM] * 5 + [ANY],
+        out_specs=[VM] * 2 + [ANY] * 2,
+        scratch_shapes=[pltpu.VMEM((BLOCK, 128), bf16)] + CTX_SEMS + MP_SEMS,
+        compiler_params=pltpu.CompilerParams(
+            vmem_limit_bytes=VMEM_LIMIT, collective_id=2, has_side_effects=True
+        ),
+    )(x_all, gain, qkv_w, cosine, sine, dy)
+
+
+def gather_kernel(a_ref, w_ref, out, w_out, *sems):
+    greet(ctx_neighbours() + mp_neighbours(), 7)
+    ring = mp_ring(a_ref, slots(out), sems[:3])
+    weights = ctx_ring(w_ref, row_slots(w_out), sems[3:])
     ring.start()
+    weights.start()
     ring.relay_near()
     ring.relay_own()
+    weights.relay_near()
+    weights.relay_own()
     ring.relay_far()
+    weights.relay_far()
     ring.finish()
-
-
-def outputs_kernel(a_ref, g_ref, h_ref, ao, go, ho, s1, r1, s2, r2, loc):
-    c, m = place()
-    core = lax.rem(c, 2)
-    sibling = (flip(c, 1), m)
-    mates = [(c, lax.rem(m + k, MP)) for k in range(1, MP)]
-    greet(mates + [sibling], MP)
-    own_a = pltpu.make_async_copy(a_ref.at[m], ao.at[m], loc.at[0])
-    own_a.start()
-    copies = []
-    for k in range(1, MP):
-        to = lax.rem(m + k, MP)
-        copies.append(remote(a_ref.at[to], ao.at[m], s1.at[k], r1.at[k], mates[k - 1]))
-    copies.append(remote(g_ref.at[:, :, 1 - core], go, s2.at[0], r2.at[0], sibling))
-    copies.append(remote(h_ref.at[:, :, 1 - core], ho, s2.at[1], r2.at[1], sibling))
-    for copy in copies:
-        copy.start()
-    for copy in copies:
-        copy.wait()
-    own_a.wait()
+    weights.finish()
 
 
 def scatter_kernel(
@@ -515,7 +563,11 @@
     )(terms)
 
 
-def finish_kernel(a_ref, g_ref, ao, go, s1, r1, s2, r2, loc):
+def finish_kernel(
+    dq_ref, dkv_ref, cos_ref, sin_ref, normed_ref, br_ref, rows_ref, hid_ref, y_ref,
+    ao, go, hid_out, y_out,
+    d_qkv, terms, s1, r1, s2, r2, s3, r3, loc,
+):
     c, m = place()
     upper = m >= MP // 2
     t = jnp.where(upper, CTX - 1 - c, c)
@@ -538,17 +590,48 @@
     def _():
         pl.semaphore_wait(barrier, MP + CTX - 2)
 
-    own_g = pltpu.make_async_copy(g_ref.at[c], go.at[c], loc.at[0])
-    own_g.start()
-    own_a = pltpu.make_async_copy(a_ref.at[m], ao.at[m], loc.at[1])
+    home = [
+        remote(hid_ref, hid_out, s3.at[0], r3.at[0], (t, m)),
+        remote(y_ref, y_out, s3.at[1], r3.at[1], (t, m)),
+    ]
+    stay = [
+        pltpu.make_async_copy(hid_ref, hid_out, loc.at[2]),
+        pltpu.make_async_copy(y_ref, y_out, loc.at[3]),
+    ]
+
+    @pl.when(upper)
+    def _():
+        for copy in home:
+            copy.start()
+
+    @pl.when(jnp.logical_not(upper))
+    def _():
+        for copy in stay:
+            copy.start()
+
+    low = lanes(TOK) < HEAD
+    for i in range(MP):
+        at = i * TOK
+        part, inside = at // HALF, at % HALF
+        columns = dq_ref[part]
+        heads = jnp.concatenate(
+            [
+                columns[:HEAD, inside : inside + TOK],
+                columns[:HEAD, HALF + inside : HALF + inside + TOK],
+            ],
+            axis=0,
+        ).T
+        cosine, sine = phase_rows(cos_ref, at, TOK), phase_rows(sin_ref, at, TOK)
+        d_qkv[i, :, 0:128] = turn_back(heads * score_scale, cosine, sine).astype(bf16)
+        dkv = dkv_ref[at : at + TOK]
+        d_qkv[i, :, 128:256] = jnp.where(low, turn_back(dkv, cosine, sine), dkv).astype(bf16)
+
+    own_a = pltpu.make_async_copy(d_qkv.at[m], ao.at[m], loc.at[1])
     a_copies, g_copies = [], []
     for k in range(MP):
         to = lax.rem(m + k, MP)
         target = (jnp.where(to >= MP // 2, CTX - 1 - c, c), to)
-        a_copies.append(remote(a_ref.at[to], ao.at[m], s1.at[k], r1.at[k], target))
-    for k in range(1, CTX):
-        to = lax.rem(c + k, CTX)
-        g_copies.append(remote(g_ref.at[to], go.at[c], s2.at[k], r2.at[k], (to, m)))
+        a_copies.append(remote(d_qkv.at[to], ao.at[m], s1.at[k], r1.at[k], target))
 
     @pl.when(upper)
     def _():
@@ -560,8 +643,22 @@
 
     for k in range(1, MP):
         a_copies[k].start()
-    for copy in g_copies:
+    grads = d_qkv[...].reshape(BLOCK, 256)
+    columns = jnp.concatenate(
+        [
+            contract(grads, normed_ref[...], 0, 0),
+            contract(rows_ref[...], br_ref[...], 0, 0),
+        ],
+        axis=0,
+    )
+    terms[...] = columns.T.astype(bf16).reshape(terms.shape)
+    own_g = pltpu.make_async_copy(terms.at[c], go.at[c], loc.at[0])
+    own_g.start()
+    for k in range(1, CTX):
+        to = lax.rem(c + k, CTX)
+        copy = remote(terms.at[to], go.at[c], s2.at[k], r2.at[k], (to, m))
         copy.start()
+        g_copies.append(copy)
     for k in range(1, MP):
         a_copies[k].wait()
     for copy in g_copies:
@@ -571,14 +668,44 @@
     @pl.when(upper)
     def _():
         a_copies[0].wait()
+        for copy in home:
+            copy.wait()
 
     @pl.when(jnp.logical_not(upper))
     def _():
         own_a.wait()
-
-
-def sums_kernel(a_ref, out, got, part, got2, s1, r1, s2, r2):
+        for copy in stay:
+            copy.wait()
+
+
+def finish(dq, dkv, cosine, sine, normed, branch_rows, out_rows, hidden_grad, outputs):
+    return pl.pallas_call(
+        finish_kernel,
+        out_shape=[
+            shape((MP, TOK, 256)),
+            shape((CTX, 64, 384)),
+            shape((TOK, 1024)),
+            shape((TOK, 1024)),
+        ],
+        in_specs=[VM] * 7 + [ANY] * 2,
+        out_specs=[ANY] * 4,
+        scratch_shapes=[
+            pltpu.VMEM((MP, TOK, 256), bf16),
+            pltpu.VMEM((CTX, 64, 384), bf16),
+        ]
+        + [pltpu.SemaphoreType.DMA((n,)) for n in (MP, MP, CTX, CTX, 2, 2, 4)],
+        compiler_params=pltpu.CompilerParams(
+            vmem_limit_bytes=VMEM_LIMIT, collective_id=8, has_side_effects=True
+        ),
+    )(dq, dkv, cosine, sine, normed, branch_rows, out_rows, hidden_grad, outputs)
+
+
+def sums_kernel(
+    a_ref, sum_a, sum_b, out, in_grad, out_grad,
+    got, part, got2, last_a, last_b, s1, r1, s2, r2, s3, r3,
+):
     c, m = place()
+    x, y = c // 4, lax.rem(c // 2, 2)
     peers = [(lax.rem(c + k, CTX), m) for k in range(1, CTX)]
     mates = [(c, lax.rem(m + k, MP)) for k in range(1, MP)]
     greet(peers + mates, CTX - 1 + MP - 1)
@@ -588,6 +715,16 @@
         copy = remote(a_ref.at[to], got.at[k], s1.at[k], r1.at[k], peers[k - 1])
         copy.start()
         copies.append(copy)
+    experts = [
+        remote(
+            sum_b.at[:, lax.rem(x + k, 4)],
+            last_b.at[k - 1], s3.at[k], r3.at[k], (lax.rem(c + 4 * k, CTX), m),
+        )
+        for k in range(1, 4)
+    ]
+    experts.append(remote(sum_a.at[:, 1 - y], last_a, s3.at[0], r3.at[0], (flip(c, 2), m)))
+    for copy in experts:
+        copy.start()
     total = a_ref[c]
     for copy in copies:
         copy.wait()
@@ -600,6 +737,20 @@
         copy = remote(part.at[to], got2.at[k], s2.at[k], r2.at[k], mates[k - 1])
         copy.start()
         copies.append(copy)
+    for copy in experts:
+        copy.wait()
+
+    def put(at, term):
+        in_grad[at] = term[:, :1024]
+        out_grad[at] = term[:, 1024:].T
+
+    for e in range(FIRST):
+        put(e, sum_a[e, y].astype(f32) + last_a[e].astype(f32))
+    for e in range(4 - FIRST):
+        term = sum_b[e, x].astype(f32)
+        for k in range(3):
+            term = term + last_b[k, e].astype(f32)
+        put(FIRST + e, term)
     last = part[m]
     for copy in copies:
         copy.wait()
@@ -608,24 +759,31 @@
     out[...] = last
 
 
-def small_sums(terms):
+def small_sums(terms, sum_a, sum_b):
     dims = terms.shape[2:]
+    wide = sum_a.shape[-1]
     return pl.pallas_call(
         sums_kernel,
-        out_shape=shape(dims, f32),
-        in_specs=[VM],
-        out_specs=VM,
+        out_shape=[shape(dims, f32), shape((4, 64, 1024), f32), shape((4, 512, 64), f32)],
+        in_specs=[VM] * 3,
+        out_specs=[VM] * 3,
         scratch_shapes=[
             pltpu.VMEM((CTX, MP) + dims, f32),
             pltpu.VMEM((MP,) + dims, f32),
             pltpu.VMEM((MP,) + dims, f32),
+            pltpu.VMEM((FIRST, 64, wide), bf16),
+            pltpu.VMEM((3, 4 - FIRST, 64, wide), bf16),
             pltpu.SemaphoreType.DMA((CTX,)),
             pltpu.SemaphoreType.DMA((CTX,)),
             pltpu.SemaphoreType.DMA((MP,)),
             pltpu.SemaphoreType.DMA((MP,)),
+            pltpu.SemaphoreType.DMA((4,)),
+            pltpu.SemaphoreType.DMA((4,)),
         ],
-        compiler_params=pltpu.CompilerParams(collective_id=9, has_side_effects=True),
-    )(terms)
+        compiler_params=pltpu.CompilerParams(
+            vmem_limit_bytes=VMEM_LIMIT, collective_id=9, has_side_effects=True
+        ),
+    )(terms, sum_a, sum_b)
 
 
 def unit(index, first_half):
@@ -645,19 +803,16 @@
 
 
 def forward_kernel(
-    q_ref, kv_ref, in_ref, outw_ref, qw_ref, rows_ref,
-    out_ref, lse_ref, in_all, outw_all, qw_all, rows_all,
+    q_ref, kv_ref, in_ref, qw_ref, rows_ref,
+    out_ref, rows_out, lse_ref, in_all, qw_all, rows_all,
     best, total, summed, *sems,
 ):
     first_half = 2 * lax.axis_index("ctx")
     greet(ctx_neighbours() + mp_neighbours(), 7)
-    weights_rings = [
-        ctx_ring(in_ref, row_slots(in_all), sems[0:5]),
-        ctx_ring(outw_ref, row_slots(outw_all), sems[5:10]),
-    ]
+    weights_rings = [ctx_ring(in_ref, row_slots(in_all), sems[0:5])]
     rows_rings = [
-        mp_ring(rows_ref, slots(rows_all), sems[10:13]),
-        mp_ring(qw_ref, slots(qw_all), sems[13:16]),
+        mp_ring(rows_ref, slots(rows_all), sems[5:8]),
+        mp_ring(qw_ref, slots(qw_all), sems[8:11]),
     ]
     for ring in weights_rings + rows_rings:
         ring.start()
@@ -681,22 +836,26 @@
     def step(index, carry):
         part, slot, diagonal = unit(index, first_half)
 
-        @pl.when(index == 12)
+        @pl.when(index == 10)
         def _():
             for ring in weights_rings:
                 ring.relay_own()
-
-        @pl.when(index == 15)
+                ring.relay_near()
+
+        @pl.when(index == 14)
         def _():
-            for ring in weights_rings:
-                ring.relay_near()
             for ring in rows_rings:
                 ring.relay_near()
                 ring.relay_own()
 
-        @pl.when(index == 25)
+        @pl.when(index == 21)
         def _():
-            for ring in rows_rings + weights_rings:
+            for ring in weights_rings:
+                ring.relay_far()
+
+        @pl.when(index == 26)
+        def _():
+            for ring in rows_rings:
                 ring.relay_far()
 
         @pl.when(diagonal)
@@ -711,32 +870,35 @@
 
     lax.fori_loop(0, 2 * CTX + 1, step, 0)
     for part in range(2):
-        out_ref[part] = summed[part][HEAD:, :] / total[part]
+        columns = summed[part][HEAD:, :] / total[part]
+        heads = jnp.concatenate([columns[:, :HALF], columns[:, HALF:]], axis=0).T
+        out_ref[part * HALF : part * HALF + HALF] = heads
+        rows_out[part * HALF : part * HALF + HALF] = heads.astype(bf16)
         lse_ref[part] = best[part] + jnp.log(total[part])
-    for ring in rows_rings + weights_rings:
+    for ring in weights_rings + rows_rings:
         ring.finish()
 
 
-def attention(q_rows, kv_all, w_in, w_out_t, qkv_w, out_rows_w):
+def attention(q_rows, kv_all, w_in, qkv_w, out_rows_w):
     rows = q_rows.shape[1]
     return pl.pallas_call(
         forward_kernel,
         out_shape=[
-            shape((2, HEAD, rows), f32),
+            shape((BLOCK, 128), f32),
+            shape((BLOCK, 128)),
             shape((2, 1, rows), f32),
             shape((4, 1024, 1024)),
-            shape((4, 1024, 512)),
             shape((MP,) + qkv_w.shape),
             shape((MP, TOK, 1024)),
         ],
-        in_specs=[VM, VM, ANY, ANY, ANY, ANY],
-        out_specs=[VM, VM, ANY, ANY, ANY, ANY],
+        in_specs=[VM, VM, ANY, ANY, ANY],
+        out_specs=[VM, VM, VM, ANY, ANY, ANY],
         scratch_shapes=[
             pltpu.VMEM((2, 1, rows), f32),
             pltpu.VMEM((2, 1, rows), f32),
             pltpu.VMEM((2, 2 * HEAD, rows), f32),
         ]
-        + CTX_SEMS * 2
+        + CTX_SEMS
         + MP_SEMS * 2,
         compiler_params=pltpu.CompilerParams(
             vmem_limit_bytes=VMEM_LIMIT, collective_id=10, has_side_effects=True
@@ -744,49 +906,66 @@
         cost_estimate=pl.CostEstimate(
             flops=33 * 4 * HALF * rows * 256, bytes_accessed=1 << 23, transcendentals=33 * HALF * rows
         ),
-    )(q_rows, kv_all, w_in, w_out_t, qkv_w, out_rows_w)
+    )(q_rows, kv_all, w_in, qkv_w, out_rows_w)
+
+
+FIRST = 3
 
 
 def backward_kernel(
-    q_ref, do_ref, lse_ref, delta_ref, kv_ref, pair_ref, br_ref,
-    dkv_ref, dq_ref, in_grad, out_grad, br_all,
-    total, got_a, got_b, sum_a, sum_b, last_a, last_b, *sems,
+    q_ref, og_ref, att_ref, lse_ref, kv_ref, pair_ref, br_ref, mixed_ref,
+    dkv_ref, dq_ref, sum_a, sum_b, br_all, mixed_out,
+    total, do_ref, delta_ref, got_a, got_b, *sems,
 ):
     c, m = place()
     first_half = 2 * c
     x, y = c // 4, lax.rem(c // 2, 2)
     peers = [(lax.rem(c + 4 * k, CTX), m) for k in range(1, 4)]
     across = (flip(c, 2), m)
-    greet(peers + [across] + mp_neighbours(), 7)
-    sa, ra, sb, rb = sems[:4]
-    ring = mp_ring(br_ref, slots(br_all), sems[4:7])
+    mates = [(c, lax.rem(m + k, MP)) for k in range(1, MP)]
+    greet(peers + [across] + mates, 4 + MP - 1)
+    sa, ra, sm, rm, loc = sems[:5]
+    ring = mp_ring(br_ref, slots(br_all), sems[5:8])
 
     def first_copies():
         copies = [
             remote(
-                pair_ref.at[pl.ds(0, 2), lax.rem(x + k, 4)],
+                pair_ref.at[pl.ds(0, FIRST), lax.rem(x + k, 4)],
                 got_a.at[k - 1], sa.at[k], ra.at[k], peers[k - 1],
             )
             for k in range(1, 4)
         ]
         copies.append(
-            remote(pair_ref.at[pl.ds(2, 2), :, 1 - y], got_b, sa.at[0], ra.at[0], across)
+            remote(
+                pair_ref.at[pl.ds(FIRST, 4 - FIRST), :, 1 - y], got_b, sa.at[0], ra.at[0], across
+            )
         )
         return copies
 
-    def second_copies():
-        copies = [
-            remote(
-                sum_b.at[:, lax.rem(x + k, 4)], last_b.at[k - 1], sb.at[k], rb.at[k], peers[k - 1]
+    def mixed_copies():
+        copies = []
+        for k in range(1, MP):
+            to = lax.rem(m + k, MP)
+            copies.append(
+                remote(mixed_ref.at[to], mixed_out.at[m], sm.at[k], rm.at[k], mates[k - 1])
             )
-            for k in range(1, 4)
-        ]
-        copies.append(remote(sum_a.at[:, 1 - y], last_a, sb.at[0], rb.at[0], across))
         return copies
+
+    def own_mixed():
+        return pltpu.make_async_copy(mixed_ref.at[m], mixed_out.at[m], loc)
 
     for copy in first_copies():
         copy.start()
     ring.start()
+    low = lanes(HALF) < HEAD
+    for part in range(2):
+        rows = slice(part * HALF, part * HALF + HALF)
+        grads = og_ref[rows].astype(f32)
+        product = (grads * att_ref[rows]).T
+        delta_ref[part, :, 0:HALF] = jnp.sum(product[:HEAD], axis=0, keepdims=True)
+        delta_ref[part, :, HALF:] = jnp.sum(product[HEAD:], axis=0, keepdims=True)
+        do_ref[part, 0:HALF] = jnp.where(low, 0.0, pltpu.roll(grads, HEAD, 1)).astype(bf16)
+        do_ref[part, HALF:] = jnp.where(low, 0.0, grads).astype(bf16)
     dq_ref[...] = jnp.zeros(dq_ref.shape, f32)
 
     def clear(index, carry):
@@ -810,36 +989,20 @@
         )
         dq_ref[part] += contract(kv, score_grad, 0, 0)
 
-    def middle():
-        for copy in first_copies():
-            copy.wait()
-        for e in range(2):
-            for j in range(2):
-                term = pair_ref[e, x, j].astype(f32)
-                for k in range(3):
-                    term = term + got_a[k, e, j].astype(f32)
-                sum_a[e, j] = term.astype(bf16)
-            for j in range(4):
-                term = pair_ref[2 + e, j, y].astype(f32) + got_b[e, j].astype(f32)
-                sum_b[e, j] = term.astype(bf16)
-        for copy in second_copies():
-            copy.start()
-
     def step(index, carry):
         part, slot, diagonal = unit(index, first_half)
 
-        @pl.when(index == 7)
+        @pl.when(index == 5)
         def _():
             ring.relay_near()
             ring.relay_own()
 
-        @pl.when(index == 14)
+        @pl.when(index == 10)
         def _():
             ring.relay_far()
-
-        @pl.when(index == 21)
-        def _():
-            middle()
+            own_mixed().start()
+            for copy in mixed_copies():
+                copy.start()
 
         @pl.when(diagonal)
         def _():
@@ -859,24 +1022,24 @@
 
     lax.fori_loop(0, 2 * CTX, write, 0)
     ring.finish()
-    for copy in second_copies():
+    for copy in first_copies():
         copy.wait()
-    for e in range(2):
-        for at, term in (
-            (e, sum_a[e, y].astype(f32) + last_a[e].astype(f32)),
-            (
-                2 + e,
-                sum_b[e, x].astype(f32)
-                + last_b[0, e].astype(f32)
-                + last_b[1, e].astype(f32)
-                + last_b[2, e].astype(f32),
-            ),
-        ):
-            in_grad[at] = term[:, :1024]
-            out_grad[at] = term[:, 1024:]
-
-
-def attention_back(q_rows, do_rows, lse, delta, kv_all, pair, branch_grad):
+    for e in range(FIRST):
+        for j in range(2):
+            term = pair_ref[e, x, j].astype(f32)
+            for k in range(3):
+                term = term + got_a[k, e, j].astype(f32)
+            sum_a[e, j] = term.astype(bf16)
+    for e in range(4 - FIRST):
+        for j in range(4):
+            term = pair_ref[FIRST + e, j, y].astype(f32) + got_b[e, j].astype(f32)
+            sum_b[e, j] = term.astype(bf16)
+    for copy in mixed_copies():
+        copy.wait()
+    own_mixed().wait()
+
+
+def attention_back(q_rows, out_grad, attended, lse, kv_all, pair, branch_grad, mixed):
     rows = q_rows.shape[1]
     wide = pair.shape[-1]
     return pl.pallas_call(
@@ -884,22 +1047,23 @@
         out_shape=[
             shape(kv_all.shape, bf16),
             shape((2, 2 * HEAD, rows), f32),
-            shape((4, 64, 1024), f32),
-            shape((4, 64, 512), f32),
+            shape((FIRST, 2, 64, wide)),
+            shape((4 - FIRST, 4, 64, wide)),
+            shape((MP, TOK, 1024)),
             shape((MP, TOK, 1024)),
         ],
-        in_specs=[VM] * 6 + [ANY],
-        out_specs=[VM] * 4 + [ANY],
+        in_specs=[VM] * 6 + [ANY] * 2,
+        out_specs=[VM] * 4 + [ANY] * 2,
         scratch_shapes=[
             pltpu.VMEM(kv_all.shape, f32),
-            pltpu.VMEM((3, 2, 2, 64, wide), bf16),
-            pltpu.VMEM((2, 4, 64, wide), bf16),
-            pltpu.VMEM((2, 2, 64, wide), bf16),
-            pltpu.VMEM((2, 4, 64, wide), bf16),
-            pltpu.VMEM((2, 64, wide), bf16),
-            pltpu.VMEM((3, 2, 64, wide), bf16),
+            pltpu.VMEM(q_rows.shape, bf16),
+            pltpu.VMEM((2, 1, rows), f32),
+            pltpu.VMEM((3, FIRST, 2, 64, wide), bf16),
+            pltpu.VMEM((4 - FIRST, 4, 64, wide), bf16),
         ]
-        + [pltpu.SemaphoreType.DMA((4,))] * 4
+        + [pltpu.SemaphoreType.DMA((4,))] * 2
+        + [pltpu.SemaphoreType.DMA((MP,))] * 2
+        + [pltpu.SemaphoreType.DMA]
         + MP_SEMS,
         compiler_params=pltpu.CompilerParams(
             vmem_limit_bytes=VMEM_LIMIT, collective_id=11, has_side_effects=True
@@ -907,28 +1071,14 @@
         cost_estimate=pl.CostEstimate(
             flops=33 * 10 * HALF * rows * 256, bytes_accessed=1 << 24, transcendentals=33 * HALF * rows
         ),
-    )(q_rows, do_rows, lse, delta, kv_all, pair, branch_grad)
+    )(q_rows, out_grad, attended, lse, kv_all, pair, branch_grad, mixed)
 
 
 def phases(positions, head_width):
     steps_up = jnp.arange(head_width // 2).astype(f32)
     frequency = rope_base ** (-2.0 * steps_up / head_width)
-    angles = positions.astype(f32)[:, None] * frequency[None, :]
-    angles = jnp.concatenate([angles, angles], axis=1)
+    angles = frequency[:, None] * positions.astype(f32)[None, :]
     return (jnp.cos(angles), jnp.sin(angles))
-
-
-def rotate(values, cosine, sine):
-    half_width = values.shape[-1] // 2
-    turned = jnp.concatenate([-values[..., half_width:], values[..., :half_width]], axis=-1)
-    return values * cosine + turned * sine
-
-
-def rotate_back(grads, cosine, sine):
-    half_width = grads.shape[-1] // 2
-    turned = grads * sine
-    turned = jnp.concatenate([turned[..., half_width:], -turned[..., :half_width]], axis=-1)
-    return grads * cosine + turned
 
 
 def normalize(values):
@@ -951,10 +1101,6 @@
             t = CTX - 1 - c if m >= MP // 2 else c
             pairs.append((c * MP + m, t * MP + m))
     return lax.ppermute(array, ("ctx", "mp"), pairs)
-
-
-def heads_to_rows(values):
-    return values.reshape(2, HALF, 2, HEAD).transpose(0, 2, 1, 3).reshape(2, 2 * HALF, HEAD)
 
 
 def body(
@@ -1013,37 +1159,22 @@
     gain_two = w_all[:, 289].astype(f32)
     out_w = w_all[:, 384:].T
 
-    scaled_all, _ = normalize(inputs)
-    normed = (scaled_all * gain_one).astype(bf16)
-    qkv = jnp.dot(normed, qkv_w, preferred_element_type=f32)
-    cosine, sine = phases(places, HEAD)
-    cosine, sine = lax.optimization_barrier((cosine, sine))
-    cos2, sin2 = cosine[:, None, :], sine[:, None, :]
-    queries = rotate(qkv[:, :128].reshape(BLOCK, 2, HEAD), cos2, sin2).astype(bf16)
-    queries = queries * jnp.asarray(score_scale, bf16)
-    q_rows = heads_to_rows(queries.reshape(BLOCK, 128))
-    q_rows = jnp.concatenate([q_rows, jnp.zeros_like(q_rows)], axis=-1)
-    keys = rotate(qkv[:, 128:192], cosine, sine).astype(bf16)
-    kv_new = jnp.concatenate([keys, qkv[:, 192:].astype(bf16)], axis=-1)
-    kv_all, dy_all = comm_call(
-        keys_kernel,
-        2,
-        [kv_new, dy_swapped],
-        [shape((CTX, BLOCK, 128)), shape((MP, TOK, 1024))],
-        CTX_SEMS + MP_SEMS,
-        6 << 20,
+    cosine, sine = lax.optimization_barrier(phases(places, HEAD))
+    normed, q_rows, kv_all, dy_all = keys_and_values(
+        x_all.reshape(BLOCK, 1024), gain_one[None, :], qkv_w, cosine, sine, dy_swapped
     )
     kv_all = kv_all.reshape(2 * CTX, HALF, 128)
-    out_cols, lse, in_w, out_w_t, qkv_w_all, out_w_all = attention(
-        q_rows, kv_all, w_in, w_out.transpose(0, 2, 1), qkv_w, out_w
+    attended, out_rows, lse, in_w, qkv_w_all, out_w_all = attention(
+        q_rows, kv_all, w_in, qkv_w, out_w
     )
     dy_all = dy_all.reshape(BLOCK, 1024)
-    attended = (
-        out_cols.reshape(2, HEAD, 2, HALF).transpose(0, 3, 2, 1).reshape(BLOCK, 128)
-    )
-    out_rows = attended.astype(bf16)
-    (rows_all,) = comm_call(
-        gather_kernel, 3, [out_rows], [shape((MP, BLOCK, 128))], MP_SEMS, 4 << 20
+    rows_all, out_w_t = comm_call(
+        gather_kernel,
+        3,
+        [out_rows, w_out.transpose(0, 2, 1)],
+        [shape((MP, BLOCK, 128)), shape((4, 1024, 512))],
+        MP_SEMS + CTX_SEMS,
+        8 << 20,
     )
     branch = lax.dot_general(
         rows_all, out_w_all, (((0, 2), (0, 1)), ((), ())), preferred_element_type=f32
@@ -1137,7 +1268,6 @@
     hidden_grad, gain_two_grad = norm_back(routed_grad, scaled_own, inverse_own, gain_two)
     hidden_grad = hidden_grad + dy_own
     branch_grad = (branch_scale * hidden_grad).astype(bf16)
-    hidden_grad_home = swap_home(hidden_grad)
 
     out_grad_terms = jnp.einsum(
         "td,hfd->htf", branch_grad, out_w_all, preferred_element_type=f32
@@ -1148,34 +1278,21 @@
     out_grad = out_grad.reshape(BLOCK, 128)
     pair = pair.reshape(4, 4, 2, 64, 1536)
 
-    mixed_got = lax.all_to_all(mixed, "mp", split_axis=0, concat_axis=0, tiled=True)
+    dkv_terms, dq_cols, sum_a, sum_b, branch_rows, mixed_got = attention_back(
+        q_rows, out_grad, attended, lse, kv_all, pair, branch_grad, mixed
+    )
     outputs = (hidden_own + jnp.sum(mixed_got.astype(f32), axis=0)).astype(bf16)
-    outputs = swap_home(outputs)
-
-    do_rows = heads_to_rows(out_grad)
-    delta = jnp.sum(do_rows.astype(f32) * heads_to_rows(attended), axis=-1)[:, None, :]
-    do_rows = jnp.concatenate([jnp.zeros_like(do_rows), do_rows], axis=-1)
-    dkv_terms, dq_cols, in_w_grad, out_w_grad_t, branch_rows = attention_back(
-        q_rows, do_rows, lse, delta, kv_all, pair, branch_grad
-    )
-    branch_rows = branch_rows.reshape(BLOCK, 1024)
     dkv = keys_grad(dkv_terms.reshape(4, 2, 2, BLOCK, 128))
-    d_key = rotate_back(dkv[:, :HEAD], cosine, sine).astype(bf16)
-    d_value = dkv[:, HEAD:].astype(bf16)
-    dq = score_scale * dq_cols[:, :HEAD, :]
-    dq = dq.reshape(2, HEAD, 2, HALF).transpose(0, 3, 2, 1).reshape(BLOCK, 2, HEAD)
-    d_query = rotate_back(dq, cos2, sin2).reshape(BLOCK, 128).astype(bf16)
-    d_qkv = jnp.concatenate([d_query, d_key, d_value], axis=1)
-    qkv_w_grad = contract(normed, d_qkv, 0, 0)
-    out_w_grad = contract(branch_rows, out_rows, 0, 0)
-    w_terms = jnp.concatenate([qkv_w_grad, out_w_grad], axis=1).astype(bf16)
-    qkv_got, w_got = comm_call(
-        finish_kernel,
-        8,
-        [d_qkv.reshape(MP, TOK, 256), w_terms.reshape(CTX, 64, 384)],
-        [shape((MP, TOK, 256)), shape((CTX, 64, 384))],
-        [MP, MP, CTX, CTX, 2],
-        5 << 20,
+    qkv_got, w_got, hidden_grad_home, outputs = finish(
+        dq_cols,
+        dkv,
+        cosine,
+        sine,
+        normed,
+        branch_rows.reshape(BLOCK, 1024),
+        out_rows,
+        hidden_grad.astype(bf16),
+        outputs,
     )
     w_grad = jnp.sum(w_got.astype(f32), axis=0)
     normed_grad = jnp.einsum(
@@ -1183,7 +1300,7 @@
     )
     scaled_one, inverse_one = normalize(layer_input.astype(f32))
     input_grad, gain_one_grad = norm_back(normed_grad, scaled_one, inverse_one, gain_one)
-    input_grad = (input_grad + hidden_grad_home).astype(bf16)
+    input_grad = (input_grad + hidden_grad_home.astype(f32)).astype(bf16)
 
     small = jnp.concatenate(
         [
@@ -1194,7 +1311,7 @@
         ],
         axis=1,
     )
-    sums = small_sums(small.reshape(CTX, MP, 8, 128))
+    sums, expert_in, expert_out = small_sums(small.reshape(CTX, MP, 8, 128), sum_a, sum_b)
     return (
         outputs,
         input_grad,
@@ -1205,8 +1322,8 @@
         w_grad[:, 256:].T,
         sums[:, 33],
         sums[:, :32],
-        in_w_grad,
-        out_w_grad_t.transpose(0, 2, 1),
+        expert_in,
+        expert_out,
     )
 
 

time: 593 us -> 508 us (0.86)
  local copies, waits for them, and re-layouts: 69.3 us -> 20.3 us
  Pallas kernels: 389 us -> 407 us
  other arithmetic: 39.3 us -> 23.4 us
  waiting for transfers between devices: 13.7 us -> 0.01 us
  starting transfers between devices: 19.6 us -> 5.96 us
  matrix products: 49.1 us -> 40.7 us
    pallas_call x2 -> x4, Pallas kernels: 92.8 us -> 164 us  [the longest x1 64.1 us: attention(): pl.pallas_call(forward_kernel, out_shape=[shape((BLOCK, 128), f32), shape...]
    pallas_call x5 -> x3, Pallas kernels: 141 us -> 98.6 us  [comm_call(): pl.pallas_call(kernel, out_shape=outs, in_specs=[ANY] * len(arrays), out_...]
    ppermute x3 -> x1, waiting for transfers between devices: 13.7 us -> 0.01 us  [swap_home(): return lax.ppermute(array, ('ctx', 'mp'), pairs)]
    pallas_call x1, Pallas kernels: 87.6 us -> 77.9 us  [attention_back(): pl.pallas_call(backward_kernel, out_shape=[shape(kv_all.shape, bf16), sha...]
    reshape x8 -> x0, local copies, waits for them, and re-layouts: 9.57 us -> none  [the longest x3 6.02 us: body(): out_cols.reshape(2, HEAD, 2, HALF).transpose(0, 3, 2, 1).reshape(BLOCK, 128)]
    unnamed x124 -> x60, local copies, waits for them, and re-layouts: 17.9 us -> 10.2 us
    ppermute x3 -> x1, starting transfers between devices: 13.6 us -> 5.96 us  [swap_home(): return lax.ppermute(array, ('ctx', 'mp'), pairs)]
    all_to_all x1 -> x0, starting transfers between devices: 6.01 us -> none  [body(): lax.all_to_all(mixed, 'mp', split_axis=0, concat_axis=0, tiled=True)]
  transfers between devices with their start and end apart: 4 -> 1, of which waited for: 1 -> 0; matrix products, arithmetic and copies ran while one was open for 15% -> 3% of each run, Pallas kernels for 16% -> 12%
where the time goes in v4:
time: 508 us; the launch traced here: 499 us
  Pallas kernels  407 us (80%)
  matrix products  40.7 us (8%)
  other arithmetic  23.4 us (5%)
  local copies, waits for them, and re-layouts  20.3 us (4%)
  starting transfers between devices  5.96 us (1%)
    pallas_call x3, Pallas kernels, comm_call(): pl.pallas_call(kernel, out_shape=outs, in_specs=[ANY] * len(arrays), out_...  98.6 us
    pallas_call x1, Pallas kernels, attention_back(): pl.pallas_call(backward_kernel, out_shape=[shape(kv_all.shape, bf16), sha...  77.9 us
    pallas_call x1, Pallas kernels, attention(): pl.pallas_call(forward_kernel, out_shape=[shape((BLOCK, 128), f32), shape...  64.1 us
    pallas_call x1, Pallas kernels, keys_and_values(): pl.pallas_call(keys_kernel, out_shape=[shape((BLOCK, 1024)), shape((2, 2...  36.5 us
    pallas_call x1, Pallas kernels, finish(): pl.pallas_call(finish_kernel, out_shape=[shape((MP, TOK, 256)), shape((CT...  35.4 us
    pallas_call x1, Pallas kernels, scatter_rows(): pl.pallas_call(scatter_kernel, out_shape=[shape((MP, TOK, 1024)), shape((...  35.3 us
    pallas_call x1, Pallas kernels, keys_grad(): pl.pallas_call(keys_grad_kernel, out_shape=shape((BLOCK, 128), f32), in_s...  31.7 us
    pallas_call x1, Pallas kernels, small_sums(): pl.pallas_call(sums_kernel, out_shape=[shape(dims, f32), shape((4, 64, 10...  28 us
  transfers between devices with their start and end apart: 1, of which 0 were waited for; matrix products, arithmetic and copies ran while one was open for 3% of the time, Pallas kernels for 12%

profile of v4, /device:TPU:65, one launch (start us, length us, event | category | flops | bytes accessed | tf_op | source)
XLA Modules:
  0.0 499.2 jit_solution(15603162815984564068)
XLA Ops:
  0.7 6.0 %collective-permute-start = (bf16[128,1024]{1,0:T(8,128)(2,1)}, bf16[128,1024]{1,0:T(8,128)(2,1)S(1)}, u32[]{:S(2)}, u32[]{:S(2)}) collective-permute-start(bf16[128,1024]{1,0:T(8,128)(2,1)} %param.25), channel_id=1, source_target_pairs={{0,0},{1,1},{2,2},{3,3},{4,124},{5,125},{6,126},{7,127},{8,8},{9,9... | collective-permute-start | bytes 786440 | tf_op jit(solution)/shard_map/ppermute | solution.py:1103
  13.1 60.0 %shard_map.212 = (bf16[8,128,1024]{2,1,0:T(8,128)(2,1)}, s32[8,16,128]{2,1,0:T(8,128)}, bf16[16,64,512]{2,1,0:T(8,128)(2,1)}) custom-call(bf16[128,1024]{1,0:T(8,128)(2,1)} %x_ref.1, s32[16,128]{1,0:T(8,128)} %add_add_fusion.id_ref, bf16[64,512]{1,0:T(8,128)(2,1)} %concatenate.21.w_ref), custom_call_target="tpu_custom_call" | custom-call | bytes 4194304 | tf_op jit(solution)/shard_map/pallas_call | solution.py:54
  74.7 2.1 convert_reduce_fusion.3
  83.9 36.5 %shard_map.213 = (bf16[1024,1024]{1,0:T(8,128)(2,1)}, bf16[2,1024,128]{2,1,0:T(8,128)(2,1)}, bf16[16,1024,128]{2,1,0:T(8,128)(2,1)}, bf16[8,128,1024]{2,1,0:T(8,128)(2,1)}) custom-call(bf16[1024,1024]{1,0:T(8,128)(2,1)} %bitcast.84, f32[1,1024]{1,0:T(1,128)} %bitcast.93, bf16[1024,256]{1,0:T(8,128)(2,1)} %slice.69.w_ref.qw_ref, ...), custom_call_target="tpu_custom_call" | custom-call | tf_op jit(solution)/shard_map/pallas_call | solution.py:347
  120.5 64.1 %shard_map.214 = (f32[1024,128]{1,0:T(8,128)}, bf16[1024,128]{1,0:T(8,128)(2,1)}, f32[2,1,1024]{2,1,0:T(1,128)}, bf16[4,1024,1024]{2,1,0:T(8,128)(2,1)}, bf16[8,...) custom-call(bf16[2,1024,128]{2,1,0:T(8,128)(2,1)} %get-tuple-element.49.q_ref, bf16[32,512,128]{2,1,0:T(8,128)(2,1)} %bitcast.104, ...), custom_call_target="tpu_custom_call" | custom-call | flops 17716740096 | bytes 8388608 | tf_op jit(solution)/shard_map/pallas_call | solution.py:884
  184.6 29.9 %shard_map.215 = (bf16[8,1024,128]{2,1,0:T(8,128)(2,1)}, bf16[4,1024,512]{2,1,0:T(8,128)(2,1)}) custom-call(bf16[1024,128]{1,0:T(8,128)(2,1)} %get-tuple-element.52.a_ref.rows_ref, bf16[4,64,512]{2,1,0:T(8,128)(2,1)} %bitcast.90), custom_call_target="tpu_custom_call" | custom-call | bytes 8388608 | tf_op jit(solution)/shard_map/pallas_call | solution.py:54
  214.5 4.8 multiply_reduce_fusion
  221.6 3.4 convolution_convert_fusion
  225.1 2.7 fusion.51
  232.0 2.9 fusion
  234.9 2.0 select_reduce_fusion
  236.9 4.4 fusion.7
  241.7 2.1 multiply_convert_fusion.4
  243.8 9.0 %bitcast_convert_fusion = bf16[1024,1024]{1,0:T(8,128)(2,1)} fusion(s32[4,1024]{1,0:T(4,128)} %copy-done.19, bf16[4,1024,1024]{2,1,0:T(8,128)(2,1)} %get-tuple-element.56, bf16[4,288,512]{2,1,0:T(8,128)(2,1)S(1)} %get-tuple-element.134, bf16[4,288,512]{2,1,0:T(8,128)(2,1)S(1)} %get-tuple-element.133), kind=kOutput, calls=%fused_computation.16 | convolution fusion | flops 4839964672 | bytes 12861440 | tf_op jit(solution)/shard_map/dot_general | solution.py:30
  255.2 35.3 %shard_map.216 = (bf16[8,128,1024]{2,1,0:T(8,128)(2,1)}, f32[8,8,128]{2,1,0:T(8,128)}, bf16[4,8,64,1536]{3,2,1,0:T(8,128)(2,1)}) custom-call(bf16[8,128,1024]{2,1,0:T(8,128)(2,1)} %bitcast.82, f32[8,8,128]{2,1,0:T(8,128)} %pad.4.b_ref, bf16[4,288,1024]{2,1,0:T(8,128)(2,1)} %copy-done.4, bf16[4,288,512]{2,1,0:T(8,128)(2,1)} %copy-done.3, ...), custom_call_target="tpu_custom_call" | custom-call | tf_op jit(solution)/shard_map/pallas_call | solution.py:438
  290.5 2.0 convert_reduce_fusion.1
  295.9 2.0 fusion.48
  299.6 8.7 %shard_map.217 = bf16[8,128,128]{2,1,0:T(8,128)(2,1)} custom-call(bf16[8,128,128]{2,1,0:T(8,128)(2,1)} %fusion.21.a_ref), custom_call_target="tpu_custom_call" | custom-call | bytes 1048576 | tf_op jit(solution)/shard_map/pallas_call | solution.py:54
  308.2 77.9 %shard_map.218 = (bf16[32,512,128]{2,1,0:T(8,128)(2,1)}, f32[2,128,1024]{2,1,0:T(8,128)}, bf16[3,2,64,1536]{3,2,1,0:T(8,128)(2,1)}, bf16[1,4,64,1536]{3,2,1,0:T(...) custom-call(bf16[2,1024,128]{2,1,0:T(8,128)(2,1)} %get-tuple-element.49.q_ref, ...), custom_call_target="tpu_custom_call" | custom-call | flops 44291850240 | bytes 16777216 | tf_op jit(solution)/shard_map/pallas_call | solution.py:1045
  386.1 31.7 %shard_map.219.dkv_ref = f32[1024,128]{1,0:T(8,128)} custom-call(bf16[4,2,2,1024,128]{4,3,2,1,0:T(8,128)(2,1)} %bitcast.74), custom_call_target="tpu_custom_call" | custom-call | tf_op jit(solution)/shard_map/pallas_call | solution.py:542
  420.1 35.4 %shard_map.220 = (bf16[8,128,256]{2,1,0:T(8,128)(2,1)}, bf16[16,64,384]{2,1,0:T(8,128)(2,1)}, bf16[128,1024]{1,0:T(8,128)(2,1)}, bf16[128,1024]{1,0:T(8,128)(2,1)}) custom-call(f32[2,128,1024]{2,1,0:T(8,128)} %get-tuple-element.62.dq_ref, f32[1024,128]{1,0:T(8,128)} %shard_map.219.dkv_ref, f32[32,1024]{1,0:T(8,128)} %get-tuple-element.47.cos_ref, ...), custom_call_target="tpu_custom_call" | custom-call | tf_op jit(solution)/shard_map/pallas_call | solution.py:682
  458.4 3.9 fusion.36
  463.8 28.0 %shard_map.221 = (f32[8,128]{1,0:T(8,128)}, f32[4,64,1024]{2,1,0:T(8,128)}, f32[4,512,64]{2,1,0:T(8,128)}) custom-call(f32[16,8,8,128]{3,2,1,0:T(8,128)} %maximum_maximum_fusion.a_ref, bf16[3,2,64,1536]{3,2,1,0:T(8,128)(2,1)} %get-tuple-element.71.sum_a, bf16[1,4,64,1536]{3,2,1,0:T(8,128)(2,1)} %get-tuple-element.72.sum_b), custom_call_target="tpu_custom_call" | custom-call | tf_op jit(solution)/shard_map/pallas_call | solution.py:765
  493.4 2.3 copy.67
  (118 shorter events, 40.6 us)
Async XLA Ops:
  0.6 9.5 %copy-start = (s32[1024]{0:T(1024)S(1)}, s32[1024]{0:T(1024)}, u32[]{:S(2)}) copy-start(s32[1024]{0:T(1024)} %param.14) | copy-start | bytes 12292
  0.7 82.5 %collective-permute-start = (bf16[128,1024]{1,0:T(8,128)(2,1)}, bf16[128,1024]{1,0:T(8,128)(2,1)S(1)}, u32[]{:S(2)}, u32[]{:S(2)}) collective-permute-start(bf16[128,1024]{1,0:T(8,128)(2,1)} %param.25), channel_id=1, source_target_pairs={{0,0},{1,1},{2,2},{3,3},{4,124},{5,125},{6,126},{7,127},{8,8},{9,9... | collective-permute-start | bytes 786440 | tf_op jit(solution)/shard_map/ppermute | solution.py:1103
  73.0 6.5 %copy-start.7 = (bf16[16,64,512]{2,1,0:T(8,128)(2,1)S(1)}, bf16[16,64,512]{2,1,0:T(8,128)(2,1)}, u32[]{:S(2)}) copy-start(bf16[16,64,512]{2,1,0:T(8,128)(2,1)} %get-tuple-element.45) | copy-start | bytes 3145732
  77.2 43.2 %copy-start.19 = (s32[4,1024]{1,0:T(4,128)}, s32[4,1024]{1,0:T(4,128)S(1)}, u32[]{:S(2)}) copy-start(s32[4,1024]{1,0:T(4,128)S(1)} %fusion.26) | copy-start | bytes 49156
  120.5 94.1 %copy-start.11 = (bf16[8,128,1024]{2,1,0:T(8,128)(2,1)S(1)}, bf16[8,128,1024]{2,1,0:T(8,128)(2,1)}, u32[]{:S(2)}) copy-start(bf16[8,128,1024]{2,1,0:T(8,128)(2,1)} %get-tuple-element.44) | copy-start | bytes 6291460
  219.3 2.1 copy-start.2
  219.4 2.2 copy-start.12
  219.5 5.6 %slice-start = ((s8[8388608]{0:T(1024)(128)(4,1)}), s8[4194304]{0:T(1024)(128)(4,1)S(1)}, s32[]{:S(2)}) async-start(s8[8388608]{0:T(1024)(128)(4,1)} %bitcast.107), calls=%async_computation | async-start | bytes 8388608
  221.6 3.4 slice-start.1
  225.0 2.7 copy-start.8
  227.7 2.6 copy-start.6
  228.6 3.2 copy-start.3
  241.6 2.1 copy-start.4
  290.4 2.0 copy-start.24
  294.1 3.9 copy-start.9
  298.0 10.2 %copy-start.13 = (bf16[128,1024]{1,0:T(8,128)(2,1)}, bf16[128,1024]{1,0:T(8,128)(2,1)S(1)}, u32[]{:S(2)}) copy-start(bf16[128,1024]{1,0:T(8,128)(2,1)S(1)} %multiply_convert_fusion.6.br_ref) | copy-start | bytes 786436
  386.1 31.7 %copy-start.10 = (bf16[8,128,1024]{2,1,0:T(8,128)(2,1)S(1)}, bf16[8,128,1024]{2,1,0:T(8,128)(2,1)}, u32[]{:S(2)}) copy-start(bf16[8,128,1024]{2,1,0:T(8,128)(2,1)} %get-tuple-element.66) | copy-start | bytes 6291460
  420.0 38.3 %copy-start.5 = (bf16[128,1024]{1,0:T(8,128)(2,1)S(1)}, bf16[128,1024]{1,0:T(8,128)(2,1)}, u32[]{:S(2)}) copy-start(bf16[128,1024]{1,0:T(8,128)(2,1)} %x_ref.1) | copy-start | bytes 786436
  420.0 38.3 %copy-start.18 = (f32[1024]{0:T(1024)S(1)}, f32[1024]{0:T(1024)}, u32[]{:S(2)}) copy-start(f32[1024]{0:T(1024)} %get-tuple-element.124) | copy-start | bytes 12292
  463.8 32.0 %copy-start.17 = (bf16[128,1024]{1,0:T(8,128)(2,1)S(1)}, bf16[128,1024]{1,0:T(8,128)(2,1)}, u32[]{:S(2)}) copy-start(bf16[128,1024]{1,0:T(8,128)(2,1)} %get-tuple-element.70) | copy-start | bytes 786436
  463.8 32.9 %copy-start.16 = (bf16[128,1024]{1,0:T(8,128)(2,1)S(1)}, bf16[128,1024]{1,0:T(8,128)(2,1)}, u32[]{:S(2)}) copy-start(bf16[128,1024]{1,0:T(8,128)(2,1)} %get-tuple-element.160) | copy-start | bytes 786436
  491.8 5.6 %copy-start.22 = (f32[8,128]{1,0:T(8,128)S(1)}, f32[8,128]{1,0:T(8,128)}, u32[]{:S(2)}) copy-start(f32[8,128]{1,0:T(8,128)} %get-tuple-element.73) | copy-start | bytes 12292
  491.9 6.2 %copy-start.14 = (f32[4,64,1024]{2,1,0:T(8,128)S(1)}, f32[4,64,1024]{2,1,0:T(8,128)}, u32[]{:S(2)}) copy-start(f32[4,64,1024]{2,1,0:T(8,128)} %get-tuple-element.169) | copy-start | bytes 3145732
  493.4 5.6 %copy-start.1 = (s32[1024]{0:T(1024)S(1)}, s32[1024]{0:T(1024)}, u32[]{:S(2)}) copy-start(s32[1024]{0:T(1024)} %param.14) | copy-start | bytes 12292
  (4 other events, 5.5 us)

commit v5 on v4

--- a/solution.py
+++ b/solution.py
@@ -173,6 +173,20 @@
 def mp_ring(own, dst, sems):
     c, m = place()
     return Ring(own, dst, m, MP, 1, 2, lambda slot: (c, slot), sems)
+
+
+def shared_ring(own, out, sems):
+    c, m = place()
+    half = own.shape[0] // 2
+    first = pl.multiple_of(lax.rem(c, 2) * half, half)
+
+    def dst(slot, part):
+        if part is None:
+            return out.at[slot, pl.ds(first, half)]
+        return out.at[slot, pl.ds(first + part * (half // 2), half // 2)]
+
+    mine = own.at[pl.ds(first, half)]
+    return Ring(mine, dst, m, MP, 1, 2, lambda slot: (c, slot), sems, (flip(c, 1), m))
 
 
 def ctx_ring(own, dst, sems):
@@ -379,14 +393,16 @@
 
 def scatter_kernel(
     a_ref, b_ref, dp_ref, act_ref, in_ref, dgu_ref,
-    ao, bo, pair_ref,
-    terms, theirs, s1, r1, s2, r2, s3, r3, loc,
+    ao, bo, pair_ref, sum_ref,
+    terms, theirs, got, own, s1, r1, s2, r2, s3, r3, s4, r4, loc,
 ):
     c, m = place()
     core = lax.rem(c, 2)
+    x = c // 4
     sibling = (flip(c, 1), m)
     mates = [(c, lax.rem(m + k, MP)) for k in range(1, MP)]
-    greet(mates + [sibling], MP)
+    peers = [(lax.rem(c + 4 * k, CTX), m) for k in range(1, 4)]
+    greet(mates + [sibling] + peers, MP + 3)
     own_a = pltpu.make_async_copy(a_ref.at[m], ao.at[m], loc.at[0])
     own_a.start()
     own_b = pltpu.make_async_copy(b_ref.at[m], bo.at[m], loc.at[1])
@@ -402,6 +418,32 @@
         remote(terms.at[1 - core, e], theirs.at[e], s3.at[e], r3.at[e], sibling)
         for e in range(4)
     ]
+    first = [
+        remote(own.at[lax.rem(x + k, 4)], got.at[k - 1], s4.at[k], r4.at[k], peers[k - 1])
+        for k in range(1, 4)
+    ]
+
+    def join(e, put):
+        crossing[e].wait()
+
+        def add(chip, carry):
+            put(
+                chip,
+                (terms[core, e, chip].astype(f32) + theirs[e, chip].astype(f32)).astype(bf16),
+            )
+            return carry
+
+        lax.fori_loop(0, 8, add, 0)
+
+    def put_own(chip, value):
+        own[chip // 2, lax.rem(chip, 2)] = value
+
+    def put_pair(e):
+        def put(chip, value):
+            pair_ref[e, chip // 2, lax.rem(chip, 2)] = value
+
+        return put
+
     for e in range(4):
         gate_up_grads = dgu_ref[e]
         active = act_ref[e]
@@ -418,16 +460,19 @@
 
         lax.fori_loop(0, 4, chunk, 0)
         crossing[e].start()
-    for e in range(4):
-        crossing[e].wait()
-
-        def add(chip, carry):
-            pair_ref[e, chip] = (
-                terms[core, e, chip].astype(f32) + theirs[e, chip].astype(f32)
-            ).astype(bf16)
-            return carry
-
-        lax.fori_loop(0, 8, add, 0)
+        if e == 1:
+            join(0, put_own)
+            for copy in first:
+                copy.start()
+    for e in range(1, 4):
+        join(e, put_pair(e - 1))
+    for copy in first:
+        copy.wait()
+    for j in range(2):
+        term = own[x, j].astype(f32)
+        for k in range(3):
+            term = term + got[k, j].astype(f32)
+        sum_ref[j] = term.astype(bf16)
     for copy in copies:
         copy.wait()
     own_a.wait()
@@ -440,16 +485,19 @@
         out_shape=[
             shape((MP, TOK, 1024)),
             shape((MP, 8, TOK), f32),
-            shape((4, 8, 64, 1536)),
+            shape((3, 4, 2, 64, 1536)),
+            shape((2, 64, 1536)),
         ],
         in_specs=[ANY, ANY, VM, VM, VM, VM],
-        out_specs=[ANY, ANY, VM],
+        out_specs=[ANY, ANY, VM, VM],
         scratch_shapes=[
             pltpu.VMEM((2, 4, 8, 64, 1536), bf16),
             pltpu.VMEM((4, 8, 64, 1536), bf16),
+            pltpu.VMEM((3, 2, 64, 1536), bf16),
+            pltpu.VMEM((4, 2, 64, 1536), bf16),
         ]
         + [pltpu.SemaphoreType.DMA((MP,))] * 4
-        + [pltpu.SemaphoreType.DMA((4,))] * 2
+        + [pltpu.SemaphoreType.DMA((4,))] * 4
         + [pltpu.SemaphoreType.DMA((2,))],
         compiler_params=pltpu.CompilerParams(
             vmem_limit_bytes=VMEM_LIMIT, collective_id=4, has_side_effects=True
@@ -700,12 +748,8 @@
     )(dq, dkv, cosine, sine, normed, branch_rows, out_rows, hidden_grad, outputs)
 
 
-def sums_kernel(
-    a_ref, sum_a, sum_b, out, in_grad, out_grad,
-    got, part, got2, last_a, last_b, s1, r1, s2, r2, s3, r3,
-):
+def sums_kernel(a_ref, out, got, part, got2, s1, r1, s2, r2):
     c, m = place()
-    x, y = c // 4, lax.rem(c // 2, 2)
     peers = [(lax.rem(c + k, CTX), m) for k in range(1, CTX)]
     mates = [(c, lax.rem(m + k, MP)) for k in range(1, MP)]
     greet(peers + mates, CTX - 1 + MP - 1)
@@ -715,16 +759,6 @@
         copy = remote(a_ref.at[to], got.at[k], s1.at[k], r1.at[k], peers[k - 1])
         copy.start()
         copies.append(copy)
-    experts = [
-        remote(
-            sum_b.at[:, lax.rem(x + k, 4)],
-            last_b.at[k - 1], s3.at[k], r3.at[k], (lax.rem(c + 4 * k, CTX), m),
-        )
-        for k in range(1, 4)
-    ]
-    experts.append(remote(sum_a.at[:, 1 - y], last_a, s3.at[0], r3.at[0], (flip(c, 2), m)))
-    for copy in experts:
-        copy.start()
     total = a_ref[c]
     for copy in copies:
         copy.wait()
@@ -737,20 +771,6 @@
         copy = remote(part.at[to], got2.at[k], s2.at[k], r2.at[k], mates[k - 1])
         copy.start()
         copies.append(copy)
-    for copy in experts:
-        copy.wait()
-
-    def put(at, term):
-        in_grad[at] = term[:, :1024]
-        out_grad[at] = term[:, 1024:].T
-
-    for e in range(FIRST):
-        put(e, sum_a[e, y].astype(f32) + last_a[e].astype(f32))
-    for e in range(4 - FIRST):
-        term = sum_b[e, x].astype(f32)
-        for k in range(3):
-            term = term + last_b[k, e].astype(f32)
-        put(FIRST + e, term)
     last = part[m]
     for copy in copies:
         copy.wait()
@@ -759,31 +779,24 @@
     out[...] = last
 
 
-def small_sums(terms, sum_a, sum_b):
+def small_sums(terms):
     dims = terms.shape[2:]
-    wide = sum_a.shape[-1]
     return pl.pallas_call(
         sums_kernel,
-        out_shape=[shape(dims, f32), shape((4, 64, 1024), f32), shape((4, 512, 64), f32)],
-        in_specs=[VM] * 3,
-        out_specs=[VM] * 3,
+        out_shape=shape(dims, f32),
+        in_specs=[VM],
+        out_specs=VM,
         scratch_shapes=[
             pltpu.VMEM((CTX, MP) + dims, f32),
             pltpu.VMEM((MP,) + dims, f32),
             pltpu.VMEM((MP,) + dims, f32),
-            pltpu.VMEM((FIRST, 64, wide), bf16),
-            pltpu.VMEM((3, 4 - FIRST, 64, wide), bf16),
             pltpu.SemaphoreType.DMA((CTX,)),
             pltpu.SemaphoreType.DMA((CTX,)),
             pltpu.SemaphoreType.DMA((MP,)),
             pltpu.SemaphoreType.DMA((MP,)),
-            pltpu.SemaphoreType.DMA((4,)),
-            pltpu.SemaphoreType.DMA((4,)),
         ],
-        compiler_params=pltpu.CompilerParams(
-            vmem_limit_bytes=VMEM_LIMIT, collective_id=9, has_side_effects=True
-        ),
-    )(terms, sum_a, sum_b)
+        compiler_params=pltpu.CompilerParams(collective_id=9, has_side_effects=True),
+    )(terms)
 
 
 def unit(index, first_half):
@@ -811,8 +824,8 @@
     greet(ctx_neighbours() + mp_neighbours(), 7)
     weights_rings = [ctx_ring(in_ref, row_slots(in_all), sems[0:5])]
     rows_rings = [
-        mp_ring(rows_ref, slots(rows_all), sems[5:8]),
-        mp_ring(qw_ref, slots(qw_all), sems[8:11]),
+        shared_ring(rows_ref, rows_all, sems[5:10]),
+        shared_ring(qw_ref, qw_all, sems[10:15]),
     ]
     for ring in weights_rings + rows_rings:
         ring.start()
@@ -836,7 +849,13 @@
     def step(index, carry):
         part, slot, diagonal = unit(index, first_half)
 
-        @pl.when(index == 10)
+        @pl.when(index == 7)
+        def _():
+            for ring in rows_rings:
+                ring.relay_near()
+                ring.relay_own()
+
+        @pl.when(index == 9)
         def _():
             for ring in weights_rings:
                 ring.relay_own()
@@ -845,17 +864,11 @@
         @pl.when(index == 14)
         def _():
             for ring in rows_rings:
-                ring.relay_near()
-                ring.relay_own()
+                ring.relay_far()
 
         @pl.when(index == 21)
         def _():
             for ring in weights_rings:
-                ring.relay_far()
-
-        @pl.when(index == 26)
-        def _():
-            for ring in rows_rings:
                 ring.relay_far()
 
         @pl.when(diagonal)
@@ -898,8 +911,7 @@
             pltpu.VMEM((2, 1, rows), f32),
             pltpu.VMEM((2, 2 * HEAD, rows), f32),
         ]
-        + CTX_SEMS
-        + MP_SEMS * 2,
+        + CTX_SEMS * 3,
         compiler_params=pltpu.CompilerParams(
             vmem_limit_bytes=VMEM_LIMIT, collective_id=10, has_side_effects=True
         ),
@@ -909,13 +921,11 @@
     )(q_rows, kv_all, w_in, qkv_w, out_rows_w)
 
 
-FIRST = 3
-
-
 def backward_kernel(
-    q_ref, og_ref, att_ref, lse_ref, kv_ref, pair_ref, br_ref, mixed_ref,
-    dkv_ref, dq_ref, sum_a, sum_b, br_all, mixed_out,
-    total, do_ref, delta_ref, got_a, got_b, *sems,
+    q_ref, og_ref, att_ref, lse_ref, kv_ref, sum_0, pair_ref, br_ref, mixed_ref,
+    dkv_ref, dq_ref, in_grad, out_grad, br_all, mixed_out,
+    total, do_ref, delta_ref, own_a, own_b, got_a, got_b, sum_a, sum_b, last_0, last_a, last_b,
+    *sems,
 ):
     c, m = place()
     first_half = 2 * c
@@ -924,23 +934,52 @@
     across = (flip(c, 2), m)
     mates = [(c, lax.rem(m + k, MP)) for k in range(1, MP)]
     greet(peers + [across] + mates, 4 + MP - 1)
-    sa, ra, sm, rm, loc = sems[:5]
-    ring = mp_ring(br_ref, slots(br_all), sems[5:8])
+    sa, ra, sb, rb, sm, rm, loc = sems[:7]
+    ring = mp_ring(br_ref, slots(br_all), sems[7:10])
 
     def first_copies():
         copies = [
             remote(
-                pair_ref.at[pl.ds(0, FIRST), lax.rem(x + k, 4)],
+                pair_ref.at[pl.ds(0, 2), lax.rem(x + k, 4)],
                 got_a.at[k - 1], sa.at[k], ra.at[k], peers[k - 1],
             )
             for k in range(1, 4)
         ]
-        copies.append(
+        copies.append(remote(pair_ref.at[2, :, 1 - y], got_b, sa.at[0], ra.at[0], across))
+        return copies
+
+    def own_copies():
+        return [
+            pltpu.make_async_copy(pair_ref.at[pl.ds(0, 2), x], own_a, loc.at[1]),
+            pltpu.make_async_copy(pair_ref.at[2, :, y], own_b, loc.at[2]),
+        ]
+
+    def sum_0_copy():
+        return remote(sum_0.at[1 - y], last_0, sb.at[0], rb.at[0], across)
+
+    def second_copies():
+        copies = [
             remote(
-                pair_ref.at[pl.ds(FIRST, 4 - FIRST), :, 1 - y], got_b, sa.at[0], ra.at[0], across
+                sum_b.at[lax.rem(x + k, 4)], last_b.at[k - 1], sb.at[k], rb.at[k], peers[k - 1]
             )
-        )
+            for k in range(1, 4)
+        ]
+        copies.append(remote(sum_a.at[:, 1 - y], last_a, sb.at[4], rb.at[4], across))
         return copies
+
+    def middle():
+        for copy in first_copies() + own_copies():
+            copy.wait()
+        for e in range(2):
+            for j in range(2):
+                term = own_a[e, j].astype(f32)
+                for k in range(3):
+                    term = term + got_a[k, e, j].astype(f32)
+                sum_a[e, j] = term.astype(bf16)
+        for j in range(4):
+            sum_b[j] = (own_b[j].astype(f32) + got_b[j].astype(f32)).astype(bf16)
+        for copy in second_copies():
+            copy.start()
 
     def mixed_copies():
         copies = []
@@ -952,9 +991,9 @@
         return copies
 
     def own_mixed():
-        return pltpu.make_async_copy(mixed_ref.at[m], mixed_out.at[m], loc)
-
-    for copy in first_copies():
+        return pltpu.make_async_copy(mixed_ref.at[m], mixed_out.at[m], loc.at[0])
+
+    for copy in first_copies() + own_copies() + [sum_0_copy()]:
         copy.start()
     ring.start()
     low = lanes(HALF) < HEAD
@@ -1004,6 +1043,10 @@
             for copy in mixed_copies():
                 copy.start()
 
+        @pl.when(index == 22)
+        def _():
+            middle()
+
         @pl.when(diagonal)
         def _():
             work(part, slot, True)
@@ -1022,24 +1065,29 @@
 
     lax.fori_loop(0, 2 * CTX, write, 0)
     ring.finish()
-    for copy in first_copies():
+    sum_0_copy().wait()
+    for copy in second_copies():
         copy.wait()
-    for e in range(FIRST):
-        for j in range(2):
-            term = pair_ref[e, x, j].astype(f32)
-            for k in range(3):
-                term = term + got_a[k, e, j].astype(f32)
-            sum_a[e, j] = term.astype(bf16)
-    for e in range(4 - FIRST):
-        for j in range(4):
-            term = pair_ref[FIRST + e, j, y].astype(f32) + got_b[e, j].astype(f32)
-            sum_b[e, j] = term.astype(bf16)
+
+    def put(at, term):
+        in_grad[at] = term[:, :1024]
+        out_grad[at] = term[:, 1024:].T
+
+    put(0, sum_0[y].astype(f32) + last_0[...].astype(f32))
+    for e in range(2):
+        put(1 + e, sum_a[e, y].astype(f32) + last_a[e].astype(f32))
+    term = sum_b[x].astype(f32)
+    for k in range(3):
+        term = term + last_b[k].astype(f32)
+    put(3, term)
     for copy in mixed_copies():
         copy.wait()
     own_mixed().wait()
 
 
-def attention_back(q_rows, out_grad, attended, lse, kv_all, pair, branch_grad, mixed):
+def attention_back(
+    q_rows, out_grad, attended, lse, kv_all, sum_first, pair, branch_grad, mixed
+):
     rows = q_rows.shape[1]
     wide = pair.shape[-1]
     return pl.pallas_call(
@@ -1047,23 +1095,31 @@
         out_shape=[
             shape(kv_all.shape, bf16),
             shape((2, 2 * HEAD, rows), f32),
-            shape((FIRST, 2, 64, wide)),
-            shape((4 - FIRST, 4, 64, wide)),
+            shape((4, 64, 1024), f32),
+            shape((4, 512, 64), f32),
             shape((MP, TOK, 1024)),
             shape((MP, TOK, 1024)),
         ],
-        in_specs=[VM] * 6 + [ANY] * 2,
+        in_specs=[VM] * 6 + [ANY] * 3,
         out_specs=[VM] * 4 + [ANY] * 2,
         scratch_shapes=[
             pltpu.VMEM(kv_all.shape, f32),
             pltpu.VMEM(q_rows.shape, bf16),
             pltpu.VMEM((2, 1, rows), f32),
-            pltpu.VMEM((3, FIRST, 2, 64, wide), bf16),
-            pltpu.VMEM((4 - FIRST, 4, 64, wide), bf16),
+            pltpu.VMEM((2, 2, 64, wide), bf16),
+            pltpu.VMEM((4, 64, wide), bf16),
+            pltpu.VMEM((3, 2, 2, 64, wide), bf16),
+            pltpu.VMEM((4, 64, wide), bf16),
+            pltpu.VMEM((2, 2, 64, wide), bf16),
+            pltpu.VMEM((4, 64, wide), bf16),
+            pltpu.VMEM((64, wide), bf16),
+            pltpu.VMEM((2, 64, wide), bf16),
+            pltpu.VMEM((3, 64, wide), bf16),
         ]
         + [pltpu.SemaphoreType.DMA((4,))] * 2
+        + [pltpu.SemaphoreType.DMA((5,))] * 2
         + [pltpu.SemaphoreType.DMA((MP,))] * 2
-        + [pltpu.SemaphoreType.DMA]
+        + [pltpu.SemaphoreType.DMA((3,))]
         + MP_SEMS,
         compiler_params=pltpu.CompilerParams(
             vmem_limit_bytes=VMEM_LIMIT, collective_id=11, has_side_effects=True
@@ -1071,7 +1127,7 @@
         cost_estimate=pl.CostEstimate(
             flops=33 * 10 * HALF * rows * 256, bytes_accessed=1 << 24, transcendentals=33 * HALF * rows
         ),
-    )(q_rows, out_grad, attended, lse, kv_all, pair, branch_grad, mixed)
+    )(q_rows, out_grad, attended, lse, kv_all, sum_first, pair, branch_grad, mixed)
 
 
 def phases(positions, head_width):
@@ -1231,11 +1287,12 @@
     row_grads = jnp.einsum(
         "esf,edf->esd", d_gate_up, in_w, preferred_element_type=f32
     ).astype(bf16)
+    row_grads = lax.optimization_barrier(row_grads)
     routed_terms = contract(placing, row_grads.reshape(4 * capacity, 1024), 0, 0)
     routed_terms = routed_terms.astype(bf16).reshape(MP, TOK, 1024)
     share = jnp.sum(jnp.where(place_bool, slot_share[:, :, None], 0.0), axis=1)
     share = jnp.pad(share.reshape(4, MP, TOK).transpose(1, 0, 2), ((0, 0), (0, 4), (0, 0)))
-    routed_got, share_got, pair = scatter_rows(
+    routed_got, share_got, pair, sum_first = scatter_rows(
         routed_terms, share, d_produced, active, incoming, d_gate_up
     )
 
@@ -1276,10 +1333,9 @@
         outputs_kernel, 5, [out_grad_terms], [shape((MP, TOK, 128))], [MP, MP, 1], 1 << 20
     )
     out_grad = out_grad.reshape(BLOCK, 128)
-    pair = pair.reshape(4, 4, 2, 64, 1536)
-
-    dkv_terms, dq_cols, sum_a, sum_b, branch_rows, mixed_got = attention_back(
-        q_rows, out_grad, attended, lse, kv_all, pair, branch_grad, mixed
+
+    dkv_terms, dq_cols, expert_in, expert_out, branch_rows, mixed_got = attention_back(
+        q_rows, out_grad, attended, lse, kv_all, sum_first, pair, branch_grad, mixed
     )
     outputs = (hidden_own + jnp.sum(mixed_got.astype(f32), axis=0)).astype(bf16)
     dkv = keys_grad(dkv_terms.reshape(4, 2, 2, BLOCK, 128))
@@ -1311,7 +1367,7 @@
         ],
         axis=1,
     )
-    sums, expert_in, expert_out = small_sums(small.reshape(CTX, MP, 8, 128), sum_a, sum_b)
+    sums = small_sums(small.reshape(CTX, MP, 8, 128))
     return (
         outputs,
         input_grad,

time: 508 us -> 510 us (level)
    pallas_call x1, Pallas kernels: 28 us -> 18.3 us  [small_sums(): pl.pallas_call(sums_kernel, out_shape=shape(dims, f32), in_specs=[VM], ou...]
    dot_general x0 -> x1, matrix products: none -> 9.72 us  [body(): jnp.einsum('esf,edf->esd', d_gate_up, in_w, preferred_element_type=f32)]
    pallas_call x1, Pallas kernels: 64.1 us -> 72.1 us  [attention(): pl.pallas_call(forward_kernel, out_shape=[shape((BLOCK, 128), f32), shape...]
where the time goes in v5:
time: 510 us; the launch traced here: 502 us
  Pallas kernels  408 us (80%)
  matrix products  43.3 us (8%)
  other arithmetic  22.8 us (4%)
  local copies, waits for them, and re-layouts  20.2 us (4%)
  starting transfers between devices  5.96 us (1%)
    pallas_call x3, Pallas kernels, comm_call(): pl.pallas_call(kernel, out_shape=outs, in_specs=[ANY] * len(arrays), out_...  99.5 us
    pallas_call x1, Pallas kernels, attention_back(): pl.pallas_call(backward_kernel, out_shape=[shape(kv_all.shape, bf16), sha...  80.2 us
    pallas_call x1, Pallas kernels, attention(): pl.pallas_call(forward_kernel, out_shape=[shape((BLOCK, 128), f32), shape...  72.1 us
    pallas_call x1, Pallas kernels, keys_and_values(): pl.pallas_call(keys_kernel, out_shape=[shape((BLOCK, 1024)), shape((2, 2...  36.5 us
    pallas_call x1, Pallas kernels, finish(): pl.pallas_call(finish_kernel, out_shape=[shape((MP, TOK, 256)), shape((CT...  36 us
    pallas_call x1, Pallas kernels, scatter_rows(): pl.pallas_call(scatter_kernel, out_shape=[shape((MP, TOK, 1024)), shape((...  34.6 us
    pallas_call x1, Pallas kernels, keys_grad(): pl.pallas_call(keys_grad_kernel, out_shape=shape((BLOCK, 128), f32), in_s...  31.1 us
    pallas_call x1, Pallas kernels, small_sums(): pl.pallas_call(sums_kernel, out_shape=shape(dims, f32), in_specs=[VM], ou...  18.3 us
  transfers between devices with their start and end apart: 1, of which 0 were waited for; matrix products, arithmetic and copies ran while one was open for 3% of the time, Pallas kernels for 12%

profile of v5, /device:TPU:65, one launch (start us, length us, event | category | flops | bytes accessed | tf_op | source)
XLA Modules:
  0.0 502.1 jit_solution(575001123713571444)
XLA Ops:
  0.7 6.0 %collective-permute-start = (bf16[128,1024]{1,0:T(8,128)(2,1)}, bf16[128,1024]{1,0:T(8,128)(2,1)S(1)}, u32[]{:S(2)}, u32[]{:S(2)}) collective-permute-start(bf16[128,1024]{1,0:T(8,128)(2,1)} %param.25), channel_id=1, source_target_pairs={{0,0},{1,1},{2,2},{3,3},{4,124},{5,125},{6,126},{7,127},{8,8},{9,9... | collective-permute-start | bytes 786440 | tf_op jit(solution)/shard_map/ppermute | solution.py:1159
  13.1 60.0 %shard_map.212 = (bf16[8,128,1024]{2,1,0:T(8,128)(2,1)}, s32[8,16,128]{2,1,0:T(8,128)}, bf16[16,64,512]{2,1,0:T(8,128)(2,1)}) custom-call(bf16[128,1024]{1,0:T(8,128)(2,1)} %x_ref.1, s32[16,128]{1,0:T(8,128)} %add_add_fusion.id_ref, bf16[64,512]{1,0:T(8,128)(2,1)} %concatenate.21.w_ref), custom_call_target="tpu_custom_call" | custom-call | bytes 4194304 | tf_op jit(solution)/shard_map/pallas_call | solution.py:54
  74.7 2.1 convert_reduce_fusion.3
  83.9 36.5 %shard_map.213 = (bf16[1024,1024]{1,0:T(8,128)(2,1)}, bf16[2,1024,128]{2,1,0:T(8,128)(2,1)}, bf16[16,1024,128]{2,1,0:T(8,128)(2,1)}, bf16[8,128,1024]{2,1,0:T(8,128)(2,1)}) custom-call(bf16[1024,1024]{1,0:T(8,128)(2,1)} %bitcast.84, f32[1,1024]{1,0:T(1,128)} %bitcast.93, bf16[1024,256]{1,0:T(8,128)(2,1)} %slice.69.w_ref.qw_ref, ...), custom_call_target="tpu_custom_call" | custom-call | tf_op jit(solution)/shard_map/pallas_call | solution.py:361
  120.5 72.1 %shard_map.214 = (f32[1024,128]{1,0:T(8,128)}, bf16[1024,128]{1,0:T(8,128)(2,1)}, f32[2,1,1024]{2,1,0:T(1,128)}, bf16[4,1024,1024]{2,1,0:T(8,128)(2,1)}, bf16[8,...) custom-call(bf16[2,1024,128]{2,1,0:T(8,128)(2,1)} %get-tuple-element.47.q_ref, bf16[32,512,128]{2,1,0:T(8,128)(2,1)} %bitcast.103, ...), custom_call_target="tpu_custom_call" | custom-call | flops 17716740096 | bytes 8388608 | tf_op jit(solution)/shard_map/pallas_call | solution.py:897
  192.6 31.0 %shard_map.215 = (bf16[8,1024,128]{2,1,0:T(8,128)(2,1)}, bf16[4,1024,512]{2,1,0:T(8,128)(2,1)}) custom-call(bf16[1024,128]{1,0:T(8,128)(2,1)} %get-tuple-element.50.a_ref.rows_ref, bf16[4,64,512]{2,1,0:T(8,128)(2,1)} %bitcast.90), custom_call_target="tpu_custom_call" | custom-call | bytes 8388608 | tf_op jit(solution)/shard_map/pallas_call | solution.py:54
  223.6 4.7 multiply_reduce_fusion
  230.7 3.3 convolution_convert_fusion
  234.0 2.7 fusion.46
  240.9 2.9 fusion
  245.3 4.5 fusion.7
  250.1 2.1 multiply_convert_fusion.4
  252.2 9.7 %convolution_convert_fusion.1 = bf16[4,288,1024]{2,1,0:T(8,128)(2,1)S(1)} fusion(bf16[4,1024,1024]{2,1,0:T(8,128)(2,1)} %get-tuple-element.54, bf16[4,288,512]{2,1,0:T(8,128)(2,1)S(1)} %get-tuple-element.130, bf16[4,288,512]{2,1,0:T(8,128)(2,1)S(1)} %get-tuple-element.129), kind=kOutput, calls=%fused_computation.36 | convolution fusion | flops 2421817344 | bytes 13107200 | tf_op jit(solution)/shard_map/esf,edf->esd/dot_general | solution.py:1287
  263.8 4.2 bitcast_convert_fusion
  268.6 34.6 %shard_map.216 = (bf16[8,128,1024]{2,1,0:T(8,128)(2,1)}, f32[8,8,128]{2,1,0:T(8,128)}, bf16[3,4,2,64,1536]{4,3,2,1,0:T(8,128)(2,1)}, bf16[2,64,1536]{2,1,0:T(8,128)(2,1)}) custom-call(bf16[8,128,1024]{2,1,0:T(8,128)(2,1)} %bitcast.82, f32[8,8,128]{2,1,0:T(8,128)} %pad.4.b_ref, bf16[4,288,1024]{2,1,0:T(8,128)(2,1)} %copy-done.4, ...), custom_call_target="tpu_custom_call" | custom-call | tf_op jit(solution)/shard_map/pallas_call | solution.py:483
  303.3 2.0 convert_reduce_fusion.1
  306.5 1.9 fusion.43
  310.0 8.5 %shard_map.217 = bf16[8,128,128]{2,1,0:T(8,128)(2,1)} custom-call(bf16[8,128,128]{2,1,0:T(8,128)(2,1)} %fusion.18.a_ref), custom_call_target="tpu_custom_call" | custom-call | bytes 1048576 | tf_op jit(solution)/shard_map/pallas_call | solution.py:54
  318.5 80.2 %shard_map.218 = (bf16[32,512,128]{2,1,0:T(8,128)(2,1)}, f32[2,128,1024]{2,1,0:T(8,128)}, f32[4,64,1024]{2,1,0:T(8,128)}, f32[4,512,64]{2,1,0:T(8,128)}, bf16[8,...) custom-call(bf16[2,1024,128]{2,1,0:T(8,128)(2,1)} %get-tuple-element.47.q_ref, bf16[1024,128]{1,0:T(8,128)(2,1)} %bitcast.92, ...), custom_call_target="tpu_custom_call" | custom-call | flops 44291850240 | bytes 16777216 | tf_op jit(solution)/shard_map/pallas_call | solution.py:1093
  398.8 31.1 %shard_map.219.dkv_ref = f32[1024,128]{1,0:T(8,128)} custom-call(bf16[4,2,2,1024,128]{4,3,2,1,0:T(8,128)(2,1)} %bitcast.74), custom_call_target="tpu_custom_call" | custom-call | tf_op jit(solution)/shard_map/pallas_call | solution.py:590
  432.2 36.0 %shard_map.220 = (bf16[8,128,256]{2,1,0:T(8,128)(2,1)}, bf16[16,64,384]{2,1,0:T(8,128)(2,1)}, bf16[128,1024]{1,0:T(8,128)(2,1)}, bf16[128,1024]{1,0:T(8,128)(2,1)}) custom-call(f32[2,128,1024]{2,1,0:T(8,128)} %get-tuple-element.61.dq_ref, f32[1024,128]{1,0:T(8,128)} %shard_map.219.dkv_ref, f32[32,1024]{1,0:T(8,128)} %get-tuple-element.45.cos_ref, ...), custom_call_target="tpu_custom_call" | custom-call | tf_op jit(solution)/shard_map/pallas_call | solution.py:730
  471.1 3.9 fusion.31
  476.5 18.3 %shard_map.221 = f32[8,128]{1,0:T(8,128)} custom-call(f32[16,8,8,128]{3,2,1,0:T(8,128)} %maximum_maximum_fusion.a_ref), custom_call_target="tpu_custom_call" | custom-call | tf_op jit(solution)/shard_map/pallas_call | solution.py:784
  496.3 2.3 copy.67
  (113 shorter events, 40.0 us)
Async XLA Ops:
  0.6 9.5 %copy-start = (s32[1024]{0:T(1024)S(1)}, s32[1024]{0:T(1024)}, u32[]{:S(2)}) copy-start(s32[1024]{0:T(1024)} %param.14) | copy-start | bytes 12292
  0.7 82.5 %collective-permute-start = (bf16[128,1024]{1,0:T(8,128)(2,1)}, bf16[128,1024]{1,0:T(8,128)(2,1)S(1)}, u32[]{:S(2)}, u32[]{:S(2)}) collective-permute-start(bf16[128,1024]{1,0:T(8,128)(2,1)} %param.25), channel_id=1, source_target_pairs={{0,0},{1,1},{2,2},{3,3},{4,124},{5,125},{6,126},{7,127},{8,8},{9,9... | collective-permute-start | bytes 786440 | tf_op jit(solution)/shard_map/ppermute | solution.py:1159
  73.0 6.5 %copy-start.7 = (bf16[16,64,512]{2,1,0:T(8,128)(2,1)S(1)}, bf16[16,64,512]{2,1,0:T(8,128)(2,1)}, u32[]{:S(2)}) copy-start(bf16[16,64,512]{2,1,0:T(8,128)(2,1)} %get-tuple-element.43) | copy-start | bytes 3145732
  120.4 103.1 %copy-start.11 = (bf16[8,128,1024]{2,1,0:T(8,128)(2,1)S(1)}, bf16[8,128,1024]{2,1,0:T(8,128)(2,1)}, u32[]{:S(2)}) copy-start(bf16[8,128,1024]{2,1,0:T(8,128)(2,1)} %get-tuple-element.42) | copy-start | bytes 6291460
  228.3 78.1 %copy-start.2 = (f32[1024,1024]{1,0:T(8,128)}, f32[1024,1024]{1,0:T(8,128)S(1)}, u32[]{:S(2)}) copy-start(f32[1024,1024]{1,0:T(8,128)S(1)} %get-tuple-element.138) | copy-start | bytes 12582916
  228.5 2.2 copy-start.12
  228.5 5.5 %slice-start = ((s8[8388608]{0:T(1024)(128)(4,1)}), s8[4194304]{0:T(1024)(128)(4,1)S(1)}, s32[]{:S(2)}) async-start(s8[8388608]{0:T(1024)(128)(4,1)} %bitcast.106), calls=%async_computation | async-start | bytes 8388608
  230.7 3.4 slice-start.1
  234.0 2.7 copy-start.8
  236.7 2.6 copy-start.6
  237.5 3.2 copy-start.3
  239.3 1.6 copy-start.20
  250.1 2.1 copy-start.4
  303.3 2.0 copy-start.21
  305.8 2.6 copy-start.9
  308.4 10.1 %copy-start.13 = (bf16[128,1024]{1,0:T(8,128)(2,1)}, bf16[128,1024]{1,0:T(8,128)(2,1)S(1)}, u32[]{:S(2)}) copy-start(bf16[128,1024]{1,0:T(8,128)(2,1)S(1)} %multiply_convert_fusion.6.br_ref) | copy-start | bytes 786436
  398.8 31.2 %copy-start.10 = (bf16[8,128,1024]{2,1,0:T(8,128)(2,1)S(1)}, bf16[8,128,1024]{2,1,0:T(8,128)(2,1)}, u32[]{:S(2)}) copy-start(bf16[8,128,1024]{2,1,0:T(8,128)(2,1)} %get-tuple-element.65) | copy-start | bytes 6291460
  432.2 38.9 %copy-start.5 = (bf16[128,1024]{1,0:T(8,128)(2,1)S(1)}, bf16[128,1024]{1,0:T(8,128)(2,1)}, u32[]{:S(2)}) copy-start(bf16[128,1024]{1,0:T(8,128)(2,1)} %x_ref.1) | copy-start | bytes 786436
  432.2 38.9 %copy-start.18 = (f32[1024]{0:T(1024)S(1)}, f32[1024]{0:T(1024)}, u32[]{:S(2)}) copy-start(f32[1024]{0:T(1024)} %get-tuple-element.120) | copy-start | bytes 12292
  475.0 23.6 %copy-start.17 = (bf16[128,1024]{1,0:T(8,128)(2,1)S(1)}, bf16[128,1024]{1,0:T(8,128)(2,1)}, u32[]{:S(2)}) copy-start(bf16[128,1024]{1,0:T(8,128)(2,1)} %get-tuple-element.69) | copy-start | bytes 786436
  475.4 24.2 %copy-start.16 = (bf16[128,1024]{1,0:T(8,128)(2,1)S(1)}, bf16[128,1024]{1,0:T(8,128)(2,1)}, u32[]{:S(2)}) copy-start(bf16[128,1024]{1,0:T(8,128)(2,1)} %get-tuple-element.156) | copy-start | bytes 786436
  476.5 24.4 %copy-start.14 = (f32[4,64,1024]{2,1,0:T(8,128)S(1)}, f32[4,64,1024]{2,1,0:T(8,128)}, u32[]{:S(2)}) copy-start(f32[4,64,1024]{2,1,0:T(8,128)} %get-tuple-element.165) | copy-start | bytes 3145732
  494.8 5.5 %copy-start.19 = (f32[8,128]{1,0:T(8,128)S(1)}, f32[8,128]{1,0:T(8,128)}, u32[]{:S(2)}) copy-start(f32[8,128]{1,0:T(8,128)} %shard_map.221) | copy-start | bytes 12292
  496.3 5.6 %copy-start.1 = (s32[1024]{0:T(1024)S(1)}, s32[1024]{0:T(1024)}, u32[]{:S(2)}) copy-start(s32[1024]{0:T(1024)} %param.14) | copy-start | bytes 12292
  (1 other events, 0.7 us)

commit v6 on v5

--- a/solution.py
+++ b/solution.py
@@ -275,11 +275,13 @@
         own_id.start()
 
     for k in range(1, MP):
+        if k == 3:
+            ring.relay_near()
+            ring.relay_own()
+        if k == 5:
+            ring.relay_far()
         x_copies[k].start()
         id_copies[k].start()
-    ring.relay_near()
-    ring.relay_own()
-    ring.relay_far()
     ring.finish()
     for k in range(1, MP):
         x_copies[k].wait()
@@ -748,18 +750,44 @@
     )(dq, dkv, cosine, sine, normed, branch_rows, out_rows, hidden_grad, outputs)
 
 
-def sums_kernel(a_ref, out, got, part, got2, s1, r1, s2, r2):
+def sums_kernel(
+    small_ref, qg_ref, qw_ref, x_ref, gain_ref, hid_ref, w_ref,
+    out, ig_ref, wq_ref, wk_ref, wv_ref, wo_ref,
+    terms, got, part, got2, s1, r1, s2, r2,
+):
     c, m = place()
     peers = [(lax.rem(c + k, CTX), m) for k in range(1, CTX)]
     mates = [(c, lax.rem(m + k, MP)) for k in range(1, MP)]
-    greet(peers + mates, CTX - 1 + MP - 1)
+    barrier = pltpu.get_barrier_semaphore()
+    for target in peers + mates:
+        pl.semaphore_signal(barrier, inc=1, device_id=target, device_id_type=MESH)
+    grads = contract(qg_ref[0], qw_ref[0], 1, 1)
+    for h in range(1, MP):
+        grads = grads + contract(qg_ref[h], qw_ref[h], 1, 1)
+    x = x_ref[...].astype(f32)
+    inverse = lax.rsqrt(jnp.mean(x * x, axis=1, keepdims=True) + epsilon)
+    scaled = x * inverse
+    inner = grads * gain_ref[...]
+    gain_grad = jnp.sum(grads * scaled, axis=0, keepdims=True)
+    columns = jnp.broadcast_to(gain_grad, (128, 1024)).T
+    terms[...] = jnp.where(lanes(1024) == 32, columns, small_ref[...]).reshape(terms.shape)
+    pl.semaphore_wait(barrier, CTX - 1 + MP - 1)
     copies = []
     for k in range(1, CTX):
         to = lax.rem(c + k, CTX)
-        copy = remote(a_ref.at[to], got.at[k], s1.at[k], r1.at[k], peers[k - 1])
+        copy = remote(terms.at[to], got.at[k], s1.at[k], r1.at[k], peers[k - 1])
         copy.start()
         copies.append(copy)
-    total = a_ref[c]
+    ig = inverse * (inner - scaled * jnp.mean(inner * scaled, axis=1, keepdims=True))
+    ig_ref[...] = (ig + hid_ref[...].astype(f32)).astype(bf16)
+    weights = w_ref[0].astype(f32)
+    for k in range(1, CTX):
+        weights = weights + w_ref[k].astype(f32)
+    wq_ref[...] = weights[:, :128]
+    wk_ref[...] = weights[:, 128:192]
+    wv_ref[...] = weights[:, 192:256]
+    wo_ref[...] = weights[:, 256:].T
+    total = terms[c]
     for copy in copies:
         copy.wait()
     for k in range(1, CTX):
@@ -779,14 +807,22 @@
     out[...] = last
 
 
-def small_sums(terms):
-    dims = terms.shape[2:]
+def last_sums(small, qkv_got, qkv_w_all, x, gain, hidden_grad, w_got):
+    dims = (8, 128)
     return pl.pallas_call(
         sums_kernel,
-        out_shape=shape(dims, f32),
-        in_specs=[VM],
-        out_specs=VM,
+        out_shape=[
+            shape(dims, f32),
+            shape((TOK, 1024)),
+            shape((64, 128), f32),
+            shape((64, 64), f32),
+            shape((64, 64), f32),
+            shape((128, 64), f32),
+        ],
+        in_specs=[VM] * 7,
+        out_specs=[VM] * 6,
         scratch_shapes=[
+            pltpu.VMEM((CTX, MP) + dims, f32),
             pltpu.VMEM((CTX, MP) + dims, f32),
             pltpu.VMEM((MP,) + dims, f32),
             pltpu.VMEM((MP,) + dims, f32),
@@ -795,8 +831,10 @@
             pltpu.SemaphoreType.DMA((MP,)),
             pltpu.SemaphoreType.DMA((MP,)),
         ],
-        compiler_params=pltpu.CompilerParams(collective_id=9, has_side_effects=True),
-    )(terms)
+        compiler_params=pltpu.CompilerParams(
+            vmem_limit_bytes=VMEM_LIMIT, collective_id=9, has_side_effects=True
+        ),
+    )(small, qkv_got, qkv_w_all, x, gain, hidden_grad, w_got)
 
 
 def unit(index, first_half):
@@ -849,24 +887,24 @@
     def step(index, carry):
         part, slot, diagonal = unit(index, first_half)
 
-        @pl.when(index == 7)
+        @pl.when(index == 11)
+        def _():
+            for ring in weights_rings:
+                ring.relay_near()
+                ring.relay_own()
+
+        @pl.when(index == 16)
         def _():
             for ring in rows_rings:
                 ring.relay_near()
                 ring.relay_own()
 
-        @pl.when(index == 9)
-        def _():
-            for ring in weights_rings:
-                ring.relay_own()
-                ring.relay_near()
-
-        @pl.when(index == 14)
+        @pl.when(index == 24)
         def _():
             for ring in rows_rings:
                 ring.relay_far()
 
-        @pl.when(index == 21)
+        @pl.when(index == 25)
         def _():
             for ring in weights_rings:
                 ring.relay_far()
@@ -993,9 +1031,9 @@
     def own_mixed():
         return pltpu.make_async_copy(mixed_ref.at[m], mixed_out.at[m], loc.at[0])
 
+    ring.start()
     for copy in first_copies() + own_copies() + [sum_0_copy()]:
         copy.start()
-    ring.start()
     low = lanes(HALF) < HEAD
     for part in range(2):
         rows = slice(part * HALF, part * HALF + HALF)
@@ -1031,21 +1069,24 @@
     def step(index, carry):
         part, slot, diagonal = unit(index, first_half)
 
-        @pl.when(index == 5)
+        @pl.when(index == 1)
+        def _():
+            own_mixed().start()
+            for copy in mixed_copies():
+                copy.start()
+
+        @pl.when(index == 18)
         def _():
             ring.relay_near()
             ring.relay_own()
 
-        @pl.when(index == 10)
+        @pl.when(index == 25)
+        def _():
+            middle()
+
+        @pl.when(index == 27)
         def _():
             ring.relay_far()
-            own_mixed().start()
-            for copy in mixed_copies():
-                copy.start()
-
-        @pl.when(index == 22)
-        def _():
-            middle()
 
         @pl.when(diagonal)
         def _():
@@ -1284,6 +1325,7 @@
     d_gate_up = jnp.concatenate(
         [d_active * up_part * slope, d_active * silu_part], axis=-1
     ).astype(bf16)
+    d_gate_up = lax.optimization_barrier(d_gate_up)
     row_grads = jnp.einsum(
         "esf,edf->esd", d_gate_up, in_w, preferred_element_type=f32
     ).astype(bf16)
@@ -1350,32 +1392,26 @@
         hidden_grad.astype(bf16),
         outputs,
     )
-    w_grad = jnp.sum(w_got.astype(f32), axis=0)
-    normed_grad = jnp.einsum(
-        "htf,hdf->td", qkv_got, qkv_w_all, preferred_element_type=f32
-    )
-    scaled_one, inverse_one = normalize(layer_input.astype(f32))
-    input_grad, gain_one_grad = norm_back(normed_grad, scaled_one, inverse_one, gain_one)
-    input_grad = (input_grad + hidden_grad_home.astype(f32)).astype(bf16)
-
     small = jnp.concatenate(
         [
             router_grad,
-            gain_one_grad[:, None],
+            jnp.zeros((1024, 1), f32),
             gain_two_grad[:, None],
             jnp.zeros((1024, 94), f32),
         ],
         axis=1,
     )
-    sums = small_sums(small.reshape(CTX, MP, 8, 128))
+    sums, input_grad, query_grad, key_grad, value_grad, attn_out_grad = last_sums(
+        small, qkv_got, qkv_w_all, layer_input, gain_one[None, :], hidden_grad_home, w_got
+    )
     return (
         outputs,
         input_grad,
         sums[:, 32],
-        w_grad[:, :128],
-        w_grad[:, 128:192],
-        w_grad[:, 192:256],
-        w_grad[:, 256:].T,
+        query_grad,
+        key_grad,
+        value_grad,
+        attn_out_grad,
         sums[:, 33],
         sums[:, :32],
         expert_in,

time: 510 us -> 470 us (0.922)
  Pallas kernels: 408 us -> 378 us
  matrix products: 43.3 us -> 35.4 us
  other arithmetic: 22.8 us -> 16.7 us
    pallas_call x1, Pallas kernels: 72.1 us -> 56.8 us  [attention(): pl.pallas_call(forward_kernel, out_shape=[shape((BLOCK, 128), f32), shape...]
    pallas_call x1, Pallas kernels: 80.2 us -> 66 us  [attention_back(): pl.pallas_call(backward_kernel, out_shape=[shape(kv_all.shape, bf16), sha...]
    dot_general x1, matrix products: 9.72 us -> 3.89 us  [body(): jnp.einsum('esf,edf->esd', d_gate_up, in_w, preferred_element_type=f32)]
    unnamed x54 -> x69, local copies, waits for them, and re-layouts: 10.2 us -> 15.9 us
  transfers between devices with their start and end apart: 1 -> 1, of which waited for: 0 -> 0; matrix products, arithmetic and copies ran while one was open for 3% -> 3% of each run, Pallas kernels for 12% -> 13%
where the time goes in v6:
time: 470 us; the launch traced here: 462 us
  Pallas kernels  378 us (80%)
  matrix products  35.4 us (8%)
  local copies, waits for them, and re-layouts  24.3 us (5%)
  other arithmetic  16.7 us (4%)
  starting transfers between devices  5.96 us (1%)
    pallas_call x3, Pallas kernels, comm_call(): pl.pallas_call(kernel, out_shape=outs, in_specs=[ANY] * len(arrays), out_...  97.9 us
    pallas_call x1, Pallas kernels, attention_back(): pl.pallas_call(backward_kernel, out_shape=[shape(kv_all.shape, bf16), sha...  66 us
    pallas_call x1, Pallas kernels, attention(): pl.pallas_call(forward_kernel, out_shape=[shape((BLOCK, 128), f32), shape...  56.8 us
    pallas_call x1, Pallas kernels, finish(): pl.pallas_call(finish_kernel, out_shape=[shape((MP, TOK, 256)), shape((CT...  35.7 us
    pallas_call x1, Pallas kernels, scatter_rows(): pl.pallas_call(scatter_kernel, out_shape=[shape((MP, TOK, 1024)), shape((...  35.2 us
    pallas_call x1, Pallas kernels, keys_and_values(): pl.pallas_call(keys_kernel, out_shape=[shape((BLOCK, 1024)), shape((2, 2...  34.3 us
    pallas_call x1, Pallas kernels, keys_grad(): pl.pallas_call(keys_grad_kernel, out_shape=shape((BLOCK, 128), f32), in_s...  32.5 us
    pallas_call x1, Pallas kernels, last_sums(): pl.pallas_call(sums_kernel, out_shape=[shape(dims, f32), shape((TOK, 1024...  20 us
  transfers between devices with their start and end apart: 1, of which 0 were waited for; matrix products, arithmetic and copies ran while one was open for 3% of the time, Pallas kernels for 13%

profile of v6, /device:TPU:65, one launch (start us, length us, event | category | flops | bytes accessed | tf_op | source)
XLA Modules:
  0.0 462.4 jit_solution(17614739968020377251)
XLA Ops:
  0.7 6.0 %collective-permute-start = (bf16[128,1024]{1,0:T(8,128)(2,1)}, bf16[128,1024]{1,0:T(8,128)(2,1)S(1)}, u32[]{:S(2)}, u32[]{:S(2)}) collective-permute-start(bf16[128,1024]{1,0:T(8,128)(2,1)} %param.25), channel_id=1, source_target_pairs={{0,0},{1,1},{2,2},{3,3},{4,124},{5,125},{6,126},{7,127},{8,8},{9,9... | collective-permute-start | bytes 786440 | tf_op jit(solution)/shard_map/ppermute | solution.py:1200
  12.0 58.8 %shard_map.212 = (bf16[8,128,1024]{2,1,0:T(8,128)(2,1)}, s32[8,16,128]{2,1,0:T(8,128)}, bf16[16,64,512]{2,1,0:T(8,128)(2,1)}) custom-call(bf16[128,1024]{1,0:T(8,128)(2,1)} %x_ref.3, s32[16,128]{1,0:T(8,128)} %add_add_fusion.id_ref, bf16[64,512]{1,0:T(8,128)(2,1)} %concatenate.14.w_ref), custom_call_target="tpu_custom_call" | custom-call | bytes 4194304 | tf_op jit(solution)/shard_map/pallas_call | solution.py:54
  77.0 1.8 bitcast_compare_fusion
  80.6 34.3 %shard_map.213 = (bf16[1024,1024]{1,0:T(8,128)(2,1)}, bf16[2,1024,128]{2,1,0:T(8,128)(2,1)}, bf16[16,1024,128]{2,1,0:T(8,128)(2,1)}, bf16[8,128,1024]{2,1,0:T(8,128)(2,1)}) custom-call(bf16[1024,1024]{1,0:T(8,128)(2,1)} %bitcast.79, f32[1,1024]{1,0:T(1,128)} %bitcast.90, bf16[1024,256]{1,0:T(8,128)(2,1)} %slice.53.w_ref.qw_ref, ...), custom_call_target="tpu_custom_call" | custom-call | tf_op jit(solution)/shard_map/pallas_call | solution.py:363
  114.8 56.8 %shard_map.214 = (f32[1024,128]{1,0:T(8,128)}, bf16[1024,128]{1,0:T(8,128)(2,1)}, f32[2,1,1024]{2,1,0:T(1,128)}, bf16[4,1024,1024]{2,1,0:T(8,128)(2,1)}, bf16[8,...) custom-call(bf16[2,1024,128]{2,1,0:T(8,128)(2,1)} %get-tuple-element.53.q_ref, bf16[32,512,128]{2,1,0:T(8,128)(2,1)} %bitcast.100, ...), custom_call_target="tpu_custom_call" | custom-call | flops 17716740096 | bytes 8388608 | tf_op jit(solution)/shard_map/pallas_call | solution.py:935
  171.6 30.5 %shard_map.215 = (bf16[8,1024,128]{2,1,0:T(8,128)(2,1)}, bf16[4,1024,512]{2,1,0:T(8,128)(2,1)}) custom-call(bf16[1024,128]{1,0:T(8,128)(2,1)} %get-tuple-element.56.a_ref.rows_ref, bf16[4,64,512]{2,1,0:T(8,128)(2,1)} %bitcast.85), custom_call_target="tpu_custom_call" | custom-call | bytes 8388608 | tf_op jit(solution)/shard_map/pallas_call | solution.py:54
  202.2 4.8 %multiply_reduce_fusion = (f32[1024]{0:T(1024)S(1)}, f32[1024,1024]{1,0:T(8,128)S(1)}) fusion(bf16[8,1024,128]{2,1,0:T(8,128)(2,1)} %get-tuple-element.57, bf16[8,128,1024]{2,1,0:T(8,128)(2,1)} %get-tuple-element.55, bf16[1024,1024]{1,0:T(8,128)(2,1)S(1)} %bitcast.80), kind=kOutput, calls=%fused_computation.22 | convolution fusion | flops 2152725504 | bytes 10489856 | tf_op jit(solution)/shard_map/dot_general | solution.py:1276
  209.3 3.3 convolution_convert_fusion
  213.9 2.7 fusion.35
  217.5 1.8 copy-done.6
  220.8 2.9 fusion
  225.3 4.6 %fusion.7 = bf16[1024,1024]{1,0:T(8,128)(2,1)} fusion(bf16[4,288,1024]{2,1,0:T(8,128)(2,1)S(1)} %convolution_convert_fusion.2, f32[4,288]{1,0:T(4,128)S(1)} %get-tuple-element.134, s32[4,1024]{1,0:T(4,128)S(1)} %fusion.21), kind=kOutput, calls=%fused_computation.15 | convolution fusion | flops 2422734848 | bytes 4477440 | tf_op jit(solution)/shard_map/dot_general | solution.py:30
  230.3 2.1 multiply_convert_fusion.4
  234.2 3.9 convolution_convert_fusion.1
  238.1 5.9 %bitcast_convert_fusion = bf16[1024,1024]{1,0:T(8,128)(2,1)} fusion(bf16[4,288,1024]{2,1,0:T(8,128)(2,1)} %convolution_convert_fusion.1, s32[4,1024]{1,0:T(4,128)S(1)} %fusion.21), kind=kOutput, calls=%fused_computation.16 | convolution fusion | flops 2418147328 | bytes 4472832 | tf_op jit(solution)/shard_map/dot_general | solution.py:30
  244.6 35.2 %shard_map.216 = (bf16[8,128,1024]{2,1,0:T(8,128)(2,1)}, f32[8,8,128]{2,1,0:T(8,128)}, bf16[3,4,2,64,1536]{4,3,2,1,0:T(8,128)(2,1)}, bf16[2,64,1536]{2,1,0:T(8,128)(2,1)}) custom-call(bf16[8,128,1024]{2,1,0:T(8,128)(2,1)} %bitcast.78, f32[8,8,128]{2,1,0:T(8,128)} %pad.4.b_ref, bf16[4,288,1024]{2,1,0:T(8,128)(2,1)} %copy-done.4, ...), custom_call_target="tpu_custom_call" | custom-call | tf_op jit(solution)/shard_map/pallas_call | solution.py:485
  279.8 2.0 convert_reduce_fusion.1
  283.1 1.9 fusion.33
  286.6 8.6 %shard_map.217 = bf16[8,128,128]{2,1,0:T(8,128)(2,1)} custom-call(bf16[8,128,128]{2,1,0:T(8,128)(2,1)} %fusion.18.a_ref), custom_call_target="tpu_custom_call" | custom-call | bytes 1048576 | tf_op jit(solution)/shard_map/pallas_call | solution.py:54
  295.2 66.0 %shard_map.218 = (bf16[32,512,128]{2,1,0:T(8,128)(2,1)}, f32[2,128,1024]{2,1,0:T(8,128)}, f32[4,64,1024]{2,1,0:T(8,128)}, f32[4,512,64]{2,1,0:T(8,128)}, bf16[8,...) custom-call(bf16[2,1024,128]{2,1,0:T(8,128)(2,1)} %get-tuple-element.53.q_ref, bf16[1024,128]{1,0:T(8,128)(2,1)} %bitcast.87, ...), custom_call_target="tpu_custom_call" | custom-call | flops 44291850240 | bytes 16777216 | tf_op jit(solution)/shard_map/pallas_call | solution.py:1134
  361.2 32.5 %shard_map.219.dkv_ref = f32[1024,128]{1,0:T(8,128)} custom-call(bf16[4,2,2,1024,128]{4,3,2,1,0:T(8,128)(2,1)} %bitcast.70), custom_call_target="tpu_custom_call" | custom-call | tf_op jit(solution)/shard_map/pallas_call | solution.py:592
  394.3 1.8 add_convert_fusion.y_ref
  396.1 35.7 %shard_map.220 = (bf16[8,128,256]{2,1,0:T(8,128)(2,1)}, bf16[16,64,384]{2,1,0:T(8,128)(2,1)}, bf16[128,1024]{1,0:T(8,128)(2,1)}, bf16[128,1024]{1,0:T(8,128)(2,1)}) custom-call(f32[2,128,1024]{2,1,0:T(8,128)} %get-tuple-element.67.dq_ref, f32[1024,128]{1,0:T(8,128)} %shard_map.219.dkv_ref, f32[32,1024]{1,0:T(8,128)} %get-tuple-element.51.cos_ref, ...), custom_call_target="tpu_custom_call" | custom-call | tf_op jit(solution)/shard_map/pallas_call | solution.py:732
  432.8 20.0 %shard_map.221 = (f32[8,128]{1,0:T(8,128)}, bf16[128,1024]{1,0:T(8,128)(2,1)}, f32[64,128]{1,0:T(8,128)}, f32[64,64]{1,0:T(8,128)}, f32[64,64]{1,0:T(8,128)}, /*index=5*/f32[128,64]{1,0:T(8,128)}) custom-call(f32[1024,128]{1,0:T(8,128)} %maximum_maximum_fusion.small_ref, bf16[8,128,256]{2,1,0:T(8,128)(2,1)} %get-tuple-element.73.qg_ref, ...), custom_call_target="tpu_custom_call" | custom-call | tf_op jit(solution)/shard_map/pallas_call | solution.py:812
  (121 shorter events, 37.1 us)
Async XLA Ops:
  0.6 8.4 %copy-start = (s32[1024]{0:T(1024)S(1)}, s32[1024]{0:T(1024)}, u32[]{:S(2)}) copy-start(s32[1024]{0:T(1024)} %param.14) | copy-start | bytes 12292
  0.7 79.2 %collective-permute-start = (bf16[128,1024]{1,0:T(8,128)(2,1)}, bf16[128,1024]{1,0:T(8,128)(2,1)S(1)}, u32[]{:S(2)}, u32[]{:S(2)}) collective-permute-start(bf16[128,1024]{1,0:T(8,128)(2,1)} %param.25), channel_id=1, source_target_pairs={{0,0},{1,1},{2,2},{3,3},{4,124},{5,125},{6,126},{7,127},{8,8},{9,9... | collective-permute-start | bytes 786440 | tf_op jit(solution)/shard_map/ppermute | solution.py:1200
  70.8 4.3 copy-start.7
  114.8 87.3 %copy-start.11 = (bf16[8,128,1024]{2,1,0:T(8,128)(2,1)S(1)}, bf16[8,128,1024]{2,1,0:T(8,128)(2,1)}, u32[]{:S(2)}) copy-start(bf16[8,128,1024]{2,1,0:T(8,128)(2,1)} %get-tuple-element.48) | copy-start | bytes 6291460
  206.9 76.1 %copy-start.2 = (f32[1024,1024]{1,0:T(8,128)}, f32[1024,1024]{1,0:T(8,128)S(1)}, u32[]{:S(2)}) copy-start(f32[1024,1024]{1,0:T(8,128)S(1)} %get-tuple-element.144) | copy-start | bytes 12582916
  207.1 6.8 %slice-start = ((s8[8388608]{0:T(1024)(128)(4,1)}), s8[4194304]{0:T(1024)(128)(4,1)S(1)}, s32[]{:S(2)}) async-start(s8[8388608]{0:T(1024)(128)(4,1)} %bitcast.103), calls=%async_computation | async-start | bytes 8388608
  209.3 4.7 %slice-start.1 = ((s8[8388608]{0:T(1024)(128)(4,1)}), s8[4194304]{0:T(1024)(128)(4,1)S(1)}, s32[]{:S(2)}) async-start(s8[8388608]{0:T(1024)(128)(4,1)} %bitcast.103), calls=%async_computation.1 | async-start | bytes 8388608
  216.6 2.6 copy-start.6
  217.5 3.2 copy-start.3
  229.9 3.0 slice-start.2
  230.3 4.0 slice-start.3
  234.2 3.9 copy-start.5
  282.4 2.6 copy-start.9
  285.0 10.1 %copy-start.13 = (bf16[128,1024]{1,0:T(8,128)(2,1)}, bf16[128,1024]{1,0:T(8,128)(2,1)S(1)}, u32[]{:S(2)}) copy-start(bf16[128,1024]{1,0:T(8,128)(2,1)S(1)} %multiply_convert_fusion.6.br_ref) | copy-start | bytes 786436
  361.2 32.7 %copy-start.10 = (bf16[8,128,1024]{2,1,0:T(8,128)(2,1)S(1)}, bf16[8,128,1024]{2,1,0:T(8,128)(2,1)}, u32[]{:S(2)}) copy-start(bf16[8,128,1024]{2,1,0:T(8,128)(2,1)} %get-tuple-element.71) | copy-start | bytes 6291460
  432.8 23.2 %copy-start.14 = (f32[4,512,64]{2,1,0:T(8,128)S(1)}, f32[4,512,64]{2,1,0:T(8,128)}, u32[]{:S(2)}) copy-start(f32[4,512,64]{2,1,0:T(8,128)} %get-tuple-element.128) | copy-start | bytes 1572868
  432.8 24.3 %copy-start.17 = (bf16[128,1024]{1,0:T(8,128)(2,1)S(1)}, bf16[128,1024]{1,0:T(8,128)(2,1)}, u32[]{:S(2)}) copy-start(bf16[128,1024]{1,0:T(8,128)(2,1)} %get-tuple-element.161) | copy-start | bytes 786436
  452.9 4.9 %copy-start.18 = (bf16[128,1024]{1,0:T(8,128)(2,1)S(1)}, bf16[128,1024]{1,0:T(8,128)(2,1)}, u32[]{:S(2)}) copy-start(bf16[128,1024]{1,0:T(8,128)(2,1)} %get-tuple-element.162) | copy-start | bytes 786436
  452.9 5.6 %copy-start.23 = (f32[64,128]{1,0:T(8,128)S(1)}, f32[64,128]{1,0:T(8,128)}, u32[]{:S(2)}) copy-start(f32[64,128]{1,0:T(8,128)} %get-tuple-element.164) | copy-start | bytes 98308
  452.9 6.2 %copy-start.22 = (f32[64,64]{1,0:T(8,128)S(1)}, f32[64,64]{1,0:T(8,128)}, u32[]{:S(2)}) copy-start(f32[64,64]{1,0:T(8,128)} %get-tuple-element.165) | copy-start | bytes 49156
  452.9 6.8 %copy-start.21 = (f32[64,64]{1,0:T(8,128)S(1)}, f32[64,64]{1,0:T(8,128)}, u32[]{:S(2)}) copy-start(f32[64,64]{1,0:T(8,128)} %get-tuple-element.166) | copy-start | bytes 49156
  452.9 7.5 %copy-start.19 = (f32[8,128]{1,0:T(8,128)S(1)}, f32[8,128]{1,0:T(8,128)}, u32[]{:S(2)}) copy-start(f32[8,128]{1,0:T(8,128)} %get-tuple-element.78) | copy-start | bytes 12292
  452.9 8.0 %copy-start.15 = (f32[4,64,1024]{2,1,0:T(8,128)S(1)}, f32[4,64,1024]{2,1,0:T(8,128)}, u32[]{:S(2)}) copy-start(f32[4,64,1024]{2,1,0:T(8,128)} %get-tuple-element.170) | copy-start | bytes 3145732
  456.0 6.0 %copy-start.1 = (s32[1024]{0:T(1024)S(1)}, s32[1024]{0:T(1024)}, u32[]{:S(2)}) copy-start(s32[1024]{0:T(1024)} %param.14) | copy-start | bytes 12292
  (6 other events, 10.0 us)

commit v7 on v6

--- a/solution.py
+++ b/solution.py
@@ -87,7 +87,10 @@
         def relay(slot, part, at, to):
             return copy(dst(slot, part), dst(slot, part), at, to)
 
-        self.own = lambda: pltpu.make_async_copy(own, dst(index, None), loc)
+        self.own = None
+        if own is not None:
+            self.own = lambda: pltpu.make_async_copy(own, dst(index, None), loc)
+        own = dst(index, None) if own is None else own
         self.to_near = copy(own, dst(index, None), 0, me_near)
         self.plus_own = copy(own, dst(index, None), 1, plus)
         self.minus_own = copy(own, dst(index, None), 2, minus)
@@ -126,7 +129,8 @@
                 self.over(at).start()
 
     def start(self):
-        self.own().start()
+        if self.own is not None:
+            self.own().start()
         for copy in (self.to_near, self.plus_own, self.minus_own):
             copy().start()
         self.cross(0)
@@ -167,7 +171,8 @@
         if self.over is not None:
             for at in range(10):
                 self.over(at).wait()
-        self.own().wait()
+        if self.own is not None:
+            self.own().wait()
 
 
 def mp_ring(own, dst, sems):
@@ -232,70 +237,60 @@
 CTX_SEMS = MP_SEMS + [pltpu.SemaphoreType.DMA((10,)), pltpu.SemaphoreType.DMA((10,))]
 
 
-def start_kernel(x_ref, id_ref, w_ref, xo, ido, wo, xs, xr, ids, idr, loc, *sems):
+def start_kernel(x_ref, id_ref, w_ref, xo, ido, wo, s1, r1, loc, *sems):
     c, m = place()
     upper = m >= MP // 2
-    t = jnp.where(upper, CTX - 1 - c, c)
-    signals = []
-    for k in range(1, MP):
-        sender = lax.rem(m + k, MP)
-        signals.append((jnp.where(sender >= MP // 2, CTX - 1 - c, c), sender))
-    signals += ctx_neighbours()
-    barrier = pltpu.get_barrier_semaphore()
-    for target in signals:
-        pl.semaphore_signal(barrier, inc=1, device_id=target, device_id_type=MESH)
+    opposite = (CTX - 1 - c, m)
+    greet([opposite] + ctx_neighbours() + mp_neighbours(), 8)
+    ring = ctx_ring(w_ref, slots(wo), sems[0:5])
+    rings = [
+        mp_ring(None, slots(xo), sems[5:8]),
+        mp_ring(None, slots(ido), sems[8:11]),
+    ]
+    moves = [
+        remote(x_ref, xo.at[m], s1.at[0], r1.at[0], opposite),
+        remote(id_ref, ido.at[m], s1.at[1], r1.at[1], opposite),
+    ]
+    stays = [
+        pltpu.make_async_copy(x_ref, xo.at[m], loc.at[0]),
+        pltpu.make_async_copy(id_ref, ido.at[m], loc.at[1]),
+    ]
 
     @pl.when(upper)
     def _():
-        pl.semaphore_signal(barrier, inc=1, device_id=(CTX - 1 - c, m), device_id_type=MESH)
-        pl.semaphore_wait(barrier, MP + 4)
+        for copy in moves:
+            copy.start()
 
     @pl.when(jnp.logical_not(upper))
     def _():
-        pl.semaphore_wait(barrier, MP + 3)
-
-    ring = ctx_ring(w_ref, slots(wo), sems)
+        for copy in stays:
+            copy.start()
+
     ring.start()
-    x_copies, id_copies = [], []
-    for k in range(MP):
-        target = (t, lax.rem(m + k, MP))
-        x_copies.append(remote(x_ref, xo.at[m], xs.at[k], xr.at[k], target))
-        id_copies.append(remote(id_ref, ido.at[m], ids.at[k], idr.at[k], target))
-    own_x = pltpu.make_async_copy(x_ref, xo.at[m], loc.at[0])
-    own_id = pltpu.make_async_copy(id_ref, ido.at[m], loc.at[1])
 
     @pl.when(upper)
     def _():
-        x_copies[0].start()
-        id_copies[0].start()
+        for copy in moves:
+            copy.wait()
 
     @pl.when(jnp.logical_not(upper))
     def _():
-        own_x.start()
-        own_id.start()
-
-    for k in range(1, MP):
-        if k == 3:
-            ring.relay_near()
-            ring.relay_own()
-        if k == 5:
-            ring.relay_far()
-        x_copies[k].start()
-        id_copies[k].start()
+        for copy in stays:
+            copy.wait()
+
+    for one in rings:
+        one.start()
+    ring.relay_near()
+    ring.relay_own()
+    for one in rings:
+        one.relay_near()
+        one.relay_own()
+    ring.relay_far()
+    for one in rings:
+        one.relay_far()
+    for one in rings:
+        one.finish()
     ring.finish()
-    for k in range(1, MP):
-        x_copies[k].wait()
-        id_copies[k].wait()
-
-    @pl.when(upper)
-    def _():
-        x_copies[0].wait()
-        id_copies[0].wait()
-
-    @pl.when(jnp.logical_not(upper))
-    def _():
-        own_x.wait()
-        own_id.wait()
 
 
 def lanes(rows):
@@ -507,10 +502,12 @@
     )(routed_terms, share, d_produced, active, incoming, d_gate_up)
 
 
-def outputs_kernel(a_ref, ao, s1, r1, loc):
+def outputs_kernel(a_ref, hid_ref, ao, hid_out, s1, r1, loc):
     c, m = place()
+    upper = m >= MP // 2
+    opposite = (CTX - 1 - c, m)
     mates = [(c, lax.rem(m + k, MP)) for k in range(1, MP)]
-    greet(mates, MP - 1)
+    greet(mates + [opposite], MP)
     own_a = pltpu.make_async_copy(a_ref.at[m], ao.at[m], loc.at[0])
     own_a.start()
     copies = []
@@ -519,9 +516,28 @@
         copies.append(remote(a_ref.at[to], ao.at[m], s1.at[k], r1.at[k], mates[k - 1]))
     for copy in copies:
         copy.start()
+    move = remote(hid_ref, hid_out, s1.at[0], r1.at[0], opposite)
+    stay = pltpu.make_async_copy(hid_ref, hid_out, loc.at[1])
+
+    @pl.when(upper)
+    def _():
+        move.start()
+
+    @pl.when(jnp.logical_not(upper))
+    def _():
+        stay.start()
+
     for copy in copies:
         copy.wait()
     own_a.wait()
+
+    @pl.when(upper)
+    def _():
+        move.wait()
+
+    @pl.when(jnp.logical_not(upper))
+    def _():
+        stay.wait()
 
 
 def keys_grad_kernel(
@@ -614,9 +630,9 @@
 
 
 def finish_kernel(
-    dq_ref, dkv_ref, cos_ref, sin_ref, normed_ref, br_ref, rows_ref, hid_ref, y_ref,
-    ao, go, hid_out, y_out,
-    d_qkv, terms, s1, r1, s2, r2, s3, r3, loc,
+    dq_ref, dkv_ref, cos_ref, sin_ref, normed_ref, br_ref, rows_ref,
+    ao, go,
+    d_qkv, terms, s1, r1, s2, r2, loc,
 ):
     c, m = place()
     upper = m >= MP // 2
@@ -639,25 +655,6 @@
     @pl.when(jnp.logical_not(upper))
     def _():
         pl.semaphore_wait(barrier, MP + CTX - 2)
-
-    home = [
-        remote(hid_ref, hid_out, s3.at[0], r3.at[0], (t, m)),
-        remote(y_ref, y_out, s3.at[1], r3.at[1], (t, m)),
-    ]
-    stay = [
-        pltpu.make_async_copy(hid_ref, hid_out, loc.at[2]),
-        pltpu.make_async_copy(y_ref, y_out, loc.at[3]),
-    ]
-
-    @pl.when(upper)
-    def _():
-        for copy in home:
-            copy.start()
-
-    @pl.when(jnp.logical_not(upper))
-    def _():
-        for copy in stay:
-            copy.start()
 
     low = lanes(TOK) < HEAD
     for i in range(MP):
@@ -718,44 +715,41 @@
     @pl.when(upper)
     def _():
         a_copies[0].wait()
-        for copy in home:
-            copy.wait()
 
     @pl.when(jnp.logical_not(upper))
     def _():
         own_a.wait()
-        for copy in stay:
-            copy.wait()
-
-
-def finish(dq, dkv, cosine, sine, normed, branch_rows, out_rows, hidden_grad, outputs):
+
+
+def finish(dq, dkv, cosine, sine, normed, branch_rows, out_rows):
     return pl.pallas_call(
         finish_kernel,
         out_shape=[
             shape((MP, TOK, 256)),
             shape((CTX, 64, 384)),
-            shape((TOK, 1024)),
-            shape((TOK, 1024)),
         ],
-        in_specs=[VM] * 7 + [ANY] * 2,
-        out_specs=[ANY] * 4,
+        in_specs=[VM] * 7,
+        out_specs=[ANY] * 2,
         scratch_shapes=[
             pltpu.VMEM((MP, TOK, 256), bf16),
             pltpu.VMEM((CTX, 64, 384), bf16),
         ]
-        + [pltpu.SemaphoreType.DMA((n,)) for n in (MP, MP, CTX, CTX, 2, 2, 4)],
+        + [pltpu.SemaphoreType.DMA((n,)) for n in (MP, MP, CTX, CTX, 2)],
         compiler_params=pltpu.CompilerParams(
             vmem_limit_bytes=VMEM_LIMIT, collective_id=8, has_side_effects=True
         ),
-    )(dq, dkv, cosine, sine, normed, branch_rows, out_rows, hidden_grad, outputs)
+    )(dq, dkv, cosine, sine, normed, branch_rows, out_rows)
 
 
 def sums_kernel(
-    small_ref, qg_ref, qw_ref, x_ref, gain_ref, hid_ref, w_ref,
-    out, ig_ref, wq_ref, wk_ref, wv_ref, wo_ref,
-    terms, got, part, got2, s1, r1, s2, r2,
+    small_ref, qg_ref, qw_ref, x_ref, gain_ref, hid_ref, w_ref, y_ref,
+    out, ig_ref, wq_ref, wk_ref, wv_ref, wo_ref, y_out,
+    terms, got, part, got2, s1, r1, s2, r2, loc,
 ):
     c, m = place()
+    upper = m >= MP // 2
+    move = remote(y_ref, y_out, s1.at[0], r1.at[0], (CTX - 1 - c, m))
+    stay = pltpu.make_async_copy(y_ref, y_out, loc)
     peers = [(lax.rem(c + k, CTX), m) for k in range(1, CTX)]
     mates = [(c, lax.rem(m + k, MP)) for k in range(1, MP)]
     barrier = pltpu.get_barrier_semaphore()
@@ -778,6 +772,15 @@
         copy = remote(terms.at[to], got.at[k], s1.at[k], r1.at[k], peers[k - 1])
         copy.start()
         copies.append(copy)
+
+    @pl.when(upper)
+    def _():
+        move.start()
+
+    @pl.when(jnp.logical_not(upper))
+    def _():
+        stay.start()
+
     ig = inverse * (inner - scaled * jnp.mean(inner * scaled, axis=1, keepdims=True))
     ig_ref[...] = (ig + hid_ref[...].astype(f32)).astype(bf16)
     weights = w_ref[0].astype(f32)
@@ -806,8 +809,16 @@
         last = last + got2[k]
     out[...] = last
 
-
-def last_sums(small, qkv_got, qkv_w_all, x, gain, hidden_grad, w_got):
+    @pl.when(upper)
+    def _():
+        move.wait()
+
+    @pl.when(jnp.logical_not(upper))
+    def _():
+        stay.wait()
+
+
+def last_sums(small, qkv_got, qkv_w_all, x, gain, hidden_grad, w_got, outputs):
     dims = (8, 128)
     return pl.pallas_call(
         sums_kernel,
@@ -818,9 +829,10 @@
             shape((64, 64), f32),
             shape((64, 64), f32),
             shape((128, 64), f32),
+            shape((TOK, 1024)),
         ],
-        in_specs=[VM] * 7,
-        out_specs=[VM] * 6,
+        in_specs=[VM] * 7 + [ANY],
+        out_specs=[VM] * 6 + [ANY],
         scratch_shapes=[
             pltpu.VMEM((CTX, MP) + dims, f32),
             pltpu.VMEM((CTX, MP) + dims, f32),
@@ -830,11 +842,12 @@
             pltpu.SemaphoreType.DMA((CTX,)),
             pltpu.SemaphoreType.DMA((MP,)),
             pltpu.SemaphoreType.DMA((MP,)),
+            pltpu.SemaphoreType.DMA,
         ],
         compiler_params=pltpu.CompilerParams(
             vmem_limit_bytes=VMEM_LIMIT, collective_id=9, has_side_effects=True
         ),
-    )(small, qkv_got, qkv_w_all, x, gain, hidden_grad, w_got)
+    )(small, qkv_got, qkv_w_all, x, gain, hidden_grad, w_got, outputs)
 
 
 def unit(index, first_half):
@@ -1243,7 +1256,7 @@
             shape((MP, 16, TOK), jnp.int32),
             shape((CTX, 64, 512)),
         ],
-        [MP, MP, MP, MP, 2] + CTX_SEMS,
+        [2, 2, 2] + CTX_SEMS + MP_SEMS * 2,
         4 << 20,
     )
     inputs = x_all.reshape(BLOCK, 1024).astype(f32)
@@ -1371,8 +1384,13 @@
     out_grad_terms = jnp.einsum(
         "td,hfd->htf", branch_grad, out_w_all, preferred_element_type=f32
     ).astype(bf16)
-    (out_grad,) = comm_call(
-        outputs_kernel, 5, [out_grad_terms], [shape((MP, TOK, 128))], [MP, MP, 1], 1 << 20
+    out_grad, hidden_grad_home = comm_call(
+        outputs_kernel,
+        5,
+        [out_grad_terms, hidden_grad.astype(bf16)],
+        [shape((MP, TOK, 128)), shape((TOK, 1024))],
+        [MP, MP, 2],
+        1 << 20,
     )
     out_grad = out_grad.reshape(BLOCK, 128)
 
@@ -1381,7 +1399,7 @@
     )
     outputs = (hidden_own + jnp.sum(mixed_got.astype(f32), axis=0)).astype(bf16)
     dkv = keys_grad(dkv_terms.reshape(4, 2, 2, BLOCK, 128))
-    qkv_got, w_got, hidden_grad_home, outputs = finish(
+    qkv_got, w_got = finish(
         dq_cols,
         dkv,
         cosine,
@@ -1389,8 +1407,6 @@
         normed,
         branch_rows.reshape(BLOCK, 1024),
         out_rows,
-        hidden_grad.astype(bf16),
-        outputs,
     )
     small = jnp.concatenate(
         [
@@ -1401,8 +1417,15 @@
         ],
         axis=1,
     )
-    sums, input_grad, query_grad, key_grad, value_grad, attn_out_grad = last_sums(
-        small, qkv_got, qkv_w_all, layer_input, gain_one[None, :], hidden_grad_home, w_got
+    sums, input_grad, query_grad, key_grad, value_grad, attn_out_grad, outputs = last_sums(
+        small,
+        qkv_got,
+        qkv_w_all,
+        layer_input,
+        gain_one[None, :],
+        hidden_grad_home,
+        w_got,
+        outputs,
     )
     return (
         outputs,

time: 470 us -> 451 us (0.960)
  Pallas kernels: 378 us -> 358 us
    pallas_call x3, Pallas kernels: 97.9 us -> 83.1 us  [comm_call(): pl.pallas_call(kernel, out_shape=outs, in_specs=[ANY] * len(arrays), out_...]
    pallas_call x1, Pallas kernels: 35.7 us -> 23.7 us  [finish(): pl.pallas_call(finish_kernel, out_shape=[shape((MP, TOK, 256)), shape((CT...]
    pallas_call x1, Pallas kernels: 20 us -> 25.2 us  [last_sums(): pl.pallas_call(sums_kernel, out_shape=[shape(dims, f32), shape((TOK, 1024...]
    unnamed x69 -> x63, local copies, waits for them, and re-layouts: 15.9 us -> 17.1 us
  transfers between devices with their start and end apart: 1 -> 1, of which waited for: 0 -> 0; matrix products, arithmetic and copies ran while one was open for 3% -> 3% of each run, Pallas kernels for 13% -> 9%
where the time goes in v7:
time: 451 us; the launch traced here: 443 us
  Pallas kernels  358 us (79%)
  matrix products  32.6 us (7%)
  local copies, waits for them, and re-layouts  26.3 us (6%)
  other arithmetic  18.4 us (4%)
  starting transfers between devices  5.96 us (1%)
    pallas_call x3, Pallas kernels, comm_call(): pl.pallas_call(kernel, out_shape=outs, in_specs=[ANY] * len(arrays), out_...  83.1 us
    pallas_call x1, Pallas kernels, attention_back(): pl.pallas_call(backward_kernel, out_shape=[shape(kv_all.shape, bf16), sha...  66.1 us
    pallas_call x1, Pallas kernels, attention(): pl.pallas_call(forward_kernel, out_shape=[shape((BLOCK, 128), f32), shape...  58 us
    pallas_call x1, Pallas kernels, scatter_rows(): pl.pallas_call(scatter_kernel, out_shape=[shape((MP, TOK, 1024)), shape((...  35.3 us
    pallas_call x1, Pallas kernels, keys_and_values(): pl.pallas_call(keys_kernel, out_shape=[shape((BLOCK, 1024)), shape((2, 2...  33.4 us
    pallas_call x1, Pallas kernels, keys_grad(): pl.pallas_call(keys_grad_kernel, out_shape=shape((BLOCK, 128), f32), in_s...  32.9 us
    pallas_call x1, Pallas kernels, last_sums(): pl.pallas_call(sums_kernel, out_shape=[shape(dims, f32), shape((TOK, 1024...  25.2 us
    pallas_call x1, Pallas kernels, finish(): pl.pallas_call(finish_kernel, out_shape=[shape((MP, TOK, 256)), shape((CT...  23.7 us
  transfers between devices with their start and end apart: 1, of which 0 were waited for; matrix products, arithmetic and copies ran while one was open for 3% of the time, Pallas kernels for 9%

profile of v7, /device:TPU:65, one launch (start us, length us, event | category | flops | bytes accessed | tf_op | source)
XLA Modules:
  0.0 442.6 jit_solution(8404963607717175066)
XLA Ops:
  0.7 6.0 %collective-permute-start = (bf16[128,1024]{1,0:T(8,128)(2,1)}, bf16[128,1024]{1,0:T(8,128)(2,1)S(1)}, u32[]{:S(2)}, u32[]{:S(2)}) collective-permute-start(bf16[128,1024]{1,0:T(8,128)(2,1)} %param.25), channel_id=1, source_target_pairs={{0,0},{1,1},{2,2},{3,3},{4,124},{5,125},{6,126},{7,127},{8,8},{9,9... | collective-permute-start | bytes 786440 | tf_op jit(solution)/shard_map/ppermute | solution.py:1213
  12.0 38.0 %shard_map.212 = (bf16[8,128,1024]{2,1,0:T(8,128)(2,1)}, s32[8,16,128]{2,1,0:T(8,128)}, bf16[16,64,512]{2,1,0:T(8,128)(2,1)}) custom-call(bf16[128,1024]{1,0:T(8,128)(2,1)} %x_ref.3, s32[16,128]{1,0:T(8,128)} %add_add_fusion.id_ref, bf16[64,512]{1,0:T(8,128)(2,1)} %concatenate.14.w_ref), custom_call_target="tpu_custom_call" | custom-call | bytes 4194304 | tf_op jit(solution)/shard_map/pallas_call | solution.py:54
  53.3 1.9 slice.53.w_ref.qw_ref
  59.8 33.4 %shard_map.213 = (bf16[1024,1024]{1,0:T(8,128)(2,1)}, bf16[2,1024,128]{2,1,0:T(8,128)(2,1)}, bf16[16,1024,128]{2,1,0:T(8,128)(2,1)}, bf16[8,128,1024]{2,1,0:T(8,128)(2,1)}) custom-call(bf16[1024,1024]{1,0:T(8,128)(2,1)} %bitcast.80, f32[1,1024]{1,0:T(1,128)} %bitcast.88, bf16[1024,256]{1,0:T(8,128)(2,1)} %slice.53.w_ref.qw_ref, ...), custom_call_target="tpu_custom_call" | custom-call | tf_op jit(solution)/shard_map/pallas_call | solution.py:358
  93.2 58.0 %shard_map.214 = (f32[1024,128]{1,0:T(8,128)}, bf16[1024,128]{1,0:T(8,128)(2,1)}, f32[2,1,1024]{2,1,0:T(1,128)}, bf16[4,1024,1024]{2,1,0:T(8,128)(2,1)}, bf16[8,...) custom-call(bf16[2,1024,128]{2,1,0:T(8,128)(2,1)} %get-tuple-element.54.q_ref, bf16[32,512,128]{2,1,0:T(8,128)(2,1)} %bitcast.99, ...), custom_call_target="tpu_custom_call" | custom-call | flops 17716740096 | bytes 8388608 | tf_op jit(solution)/shard_map/pallas_call | solution.py:948
  151.2 30.7 %shard_map.215 = (bf16[8,1024,128]{2,1,0:T(8,128)(2,1)}, bf16[4,1024,512]{2,1,0:T(8,128)(2,1)}) custom-call(bf16[1024,128]{1,0:T(8,128)(2,1)} %get-tuple-element.56.a_ref.rows_ref, bf16[4,64,512]{2,1,0:T(8,128)(2,1)} %bitcast.85), custom_call_target="tpu_custom_call" | custom-call | bytes 8388608 | tf_op jit(solution)/shard_map/pallas_call | solution.py:54
  182.0 4.8 %multiply_reduce_fusion = (f32[1024]{0:T(1024)S(1)}, f32[1024,1024]{1,0:T(8,128)S(1)}) fusion(bf16[8,1024,128]{2,1,0:T(8,128)(2,1)} %get-tuple-element.57, bf16[8,128,1024]{2,1,0:T(8,128)(2,1)} %get-tuple-element.58, bf16[1024,1024]{1,0:T(8,128)(2,1)S(1)} %bitcast.81), kind=kOutput, calls=%fused_computation.23 | convolution fusion | flops 2152725504 | bytes 10489856 | tf_op jit(solution)/shard_map/dot_general | solution.py:1289
  189.0 3.3 convolution_convert_fusion
  193.6 2.7 fusion.35
  200.5 2.9 fusion
  204.9 4.6 %fusion.7 = bf16[1024,1024]{1,0:T(8,128)(2,1)} fusion(bf16[4,288,1024]{2,1,0:T(8,128)(2,1)S(1)} %convolution_convert_fusion.2, f32[4,288]{1,0:T(4,128)S(1)} %get-tuple-element.136, s32[4,1024]{1,0:T(4,128)S(1)} %fusion.21), kind=kOutput, calls=%fused_computation.15 | convolution fusion | flops 2422734848 | bytes 4477440 | tf_op jit(solution)/shard_map/dot_general | solution.py:30
  210.1 2.0 multiply_convert_fusion.4
  214.0 2.9 convolution_convert_fusion.1
  216.9 4.2 bitcast_convert_fusion
  221.7 35.3 %shard_map.216 = (bf16[8,128,1024]{2,1,0:T(8,128)(2,1)}, f32[8,8,128]{2,1,0:T(8,128)}, bf16[3,4,2,64,1536]{4,3,2,1,0:T(8,128)(2,1)}, bf16[2,64,1536]{2,1,0:T(8,128)(2,1)}) custom-call(bf16[8,128,1024]{2,1,0:T(8,128)(2,1)} %bitcast.79, f32[8,8,128]{2,1,0:T(8,128)} %pad.4.b_ref, bf16[4,288,1024]{2,1,0:T(8,128)(2,1)} %copy-done.4, ...), custom_call_target="tpu_custom_call" | custom-call | tf_op jit(solution)/shard_map/pallas_call | solution.py:480
  257.8 2.0 convert_reduce_fusion.1
  261.0 1.9 fusion.33
  264.5 14.4 %shard_map.217 = (bf16[8,128,128]{2,1,0:T(8,128)(2,1)}, bf16[128,1024]{1,0:T(8,128)(2,1)}) custom-call(bf16[8,128,128]{2,1,0:T(8,128)(2,1)} %fusion.18.a_ref, bf16[128,1024]{1,0:T(8,128)(2,1)} %get-tuple-element.139.hid_ref), custom_call_target="tpu_custom_call" | custom-call | bytes 1048576 | tf_op jit(solution)/shard_map/pallas_call | solution.py:54
  279.0 66.1 %shard_map.218 = (bf16[32,512,128]{2,1,0:T(8,128)(2,1)}, f32[2,128,1024]{2,1,0:T(8,128)}, f32[4,64,1024]{2,1,0:T(8,128)}, f32[4,512,64]{2,1,0:T(8,128)}, bf16[8,...) custom-call(bf16[2,1024,128]{2,1,0:T(8,128)(2,1)} %get-tuple-element.54.q_ref, bf16[1024,128]{1,0:T(8,128)(2,1)} %bitcast.101, ...), custom_call_target="tpu_custom_call" | custom-call | flops 44291850240 | bytes 16777216 | tf_op jit(solution)/shard_map/pallas_call | solution.py:1147
  345.1 2.0 convert_reduce_fusion
  347.1 1.8 add_convert_fusion.y_ref
  349.0 32.9 %shard_map.219.dkv_ref = f32[1024,128]{1,0:T(8,128)} custom-call(bf16[4,2,2,1024,128]{4,3,2,1,0:T(8,128)(2,1)} %bitcast.70), custom_call_target="tpu_custom_call" | custom-call | tf_op jit(solution)/shard_map/pallas_call | solution.py:608
  382.1 23.7 %shard_map.220 = (bf16[8,128,256]{2,1,0:T(8,128)(2,1)}, bf16[16,64,384]{2,1,0:T(8,128)(2,1)}) custom-call(f32[2,128,1024]{2,1,0:T(8,128)} %get-tuple-element.69.dq_ref, f32[1024,128]{1,0:T(8,128)} %shard_map.219.dkv_ref, f32[32,1024]{1,0:T(8,128)} %get-tuple-element.52.cos_ref, f32[32,1024]{1,0:T(8,128)} %get-tuple-element.53.sin_ref, ...), custom_call_target="tpu_custom_call" | custom-call | tf_op jit(solution)/shard_map/pallas_call | solution.py:725
  406.8 25.2 %shard_map.221 = (f32[8,128]{1,0:T(8,128)}, bf16[128,1024]{1,0:T(8,128)(2,1)}, f32[64,128]{1,0:T(8,128)}, f32[64,64]{1,0:T(8,128)}, f32[64,64]{1,0:T(8,128)}, /*...) custom-call(f32[1024,128]{1,0:T(8,128)} %maximum_maximum_fusion.small_ref, bf16[8,128,256]{2,1,0:T(8,128)(2,1)} %get-tuple-element.73.qg_ref, ...), custom_call_target="tpu_custom_call" | custom-call | tf_op jit(solution)/shard_map/pallas_call | solution.py:823
  (115 shorter events, 40.4 us)
Async XLA Ops:
  0.6 8.4 %copy-start = (s32[1024]{0:T(1024)S(1)}, s32[1024]{0:T(1024)}, u32[]{:S(2)}) copy-start(s32[1024]{0:T(1024)} %param.14) | copy-start | bytes 12292
  0.7 58.5 %collective-permute-start = (bf16[128,1024]{1,0:T(8,128)(2,1)}, bf16[128,1024]{1,0:T(8,128)(2,1)S(1)}, u32[]{:S(2)}, u32[]{:S(2)}) collective-permute-start(bf16[128,1024]{1,0:T(8,128)(2,1)} %param.25), channel_id=1, source_target_pairs={{0,0},{1,1},{2,2},{3,3},{4,124},{5,125},{6,126},{7,127},{8,8},{9,9... | collective-permute-start | bytes 786440 | tf_op jit(solution)/shard_map/ppermute | solution.py:1213
  50.0 5.2 %copy-start.7 = (bf16[16,64,512]{2,1,0:T(8,128)(2,1)S(1)}, bf16[16,64,512]{2,1,0:T(8,128)(2,1)}, u32[]{:S(2)}) copy-start(bf16[16,64,512]{2,1,0:T(8,128)(2,1)} %get-tuple-element.50) | copy-start | bytes 3145732
  93.2 88.8 %copy-start.10 = (bf16[8,128,1024]{2,1,0:T(8,128)(2,1)S(1)}, bf16[8,128,1024]{2,1,0:T(8,128)(2,1)}, u32[]{:S(2)}) copy-start(bf16[8,128,1024]{2,1,0:T(8,128)(2,1)} %get-tuple-element.49) | copy-start | bytes 6291460
  186.8 74.3 %copy-start.2 = (f32[1024,1024]{1,0:T(8,128)}, f32[1024,1024]{1,0:T(8,128)S(1)}, u32[]{:S(2)}) copy-start(f32[1024,1024]{1,0:T(8,128)S(1)} %get-tuple-element.146) | copy-start | bytes 12582916
  186.8 2.2 copy-start.11
  186.8 6.8 %slice-start = ((s8[8388608]{0:T(1024)(128)(4,1)}), s8[4194304]{0:T(1024)(128)(4,1)S(1)}, s32[]{:S(2)}) async-start(s8[8388608]{0:T(1024)(128)(4,1)} %bitcast.103), calls=%async_computation | async-start | bytes 8388608
  189.0 4.7 %slice-start.1 = ((s8[8388608]{0:T(1024)(128)(4,1)}), s8[4194304]{0:T(1024)(128)(4,1)S(1)}, s32[]{:S(2)}) async-start(s8[8388608]{0:T(1024)(128)(4,1)} %bitcast.103), calls=%async_computation.1 | async-start | bytes 8388608
  196.3 2.6 copy-start.6
  197.1 3.2 copy-start.3
  209.7 3.0 slice-start.2
  210.1 2.1 copy-start.4
  210.1 4.0 slice-start.3
  214.0 2.9 copy-start.5
  260.4 2.6 copy-start.9
  263.0 16.0 %copy-start.12 = (bf16[128,1024]{1,0:T(8,128)(2,1)}, bf16[128,1024]{1,0:T(8,128)(2,1)S(1)}, u32[]{:S(2)}) copy-start(bf16[128,1024]{1,0:T(8,128)(2,1)S(1)} %multiply_convert_fusion.5.br_ref) | copy-start | bytes 786436
  406.8 28.4 %copy-start.13 = (f32[4,512,64]{2,1,0:T(8,128)S(1)}, f32[4,512,64]{2,1,0:T(8,128)}, u32[]{:S(2)}) copy-start(f32[4,512,64]{2,1,0:T(8,128)} %get-tuple-element.130) | copy-start | bytes 1572868
  432.1 6.0 %copy-start.16 = (bf16[128,1024]{1,0:T(8,128)(2,1)S(1)}, bf16[128,1024]{1,0:T(8,128)(2,1)}, u32[]{:S(2)}) copy-start(bf16[128,1024]{1,0:T(8,128)(2,1)} %get-tuple-element.164) | copy-start | bytes 786436
  432.1 6.7 %copy-start.21 = (f32[64,128]{1,0:T(8,128)S(1)}, f32[64,128]{1,0:T(8,128)}, u32[]{:S(2)}) copy-start(f32[64,128]{1,0:T(8,128)} %get-tuple-element.166) | copy-start | bytes 98308
  432.1 7.3 %copy-start.20 = (f32[64,64]{1,0:T(8,128)S(1)}, f32[64,64]{1,0:T(8,128)}, u32[]{:S(2)}) copy-start(f32[64,64]{1,0:T(8,128)} %get-tuple-element.167) | copy-start | bytes 49156
  432.1 7.9 %copy-start.19 = (f32[64,64]{1,0:T(8,128)S(1)}, f32[64,64]{1,0:T(8,128)}, u32[]{:S(2)}) copy-start(f32[64,64]{1,0:T(8,128)} %get-tuple-element.168) | copy-start | bytes 49156
  432.1 8.5 %copy-start.17 = (f32[8,128]{1,0:T(8,128)S(1)}, f32[8,128]{1,0:T(8,128)}, u32[]{:S(2)}) copy-start(f32[8,128]{1,0:T(8,128)} %get-tuple-element.80) | copy-start | bytes 12292
  432.1 9.1 %copy-start.14 = (f32[4,64,1024]{2,1,0:T(8,128)S(1)}, f32[4,64,1024]{2,1,0:T(8,128)}, u32[]{:S(2)}) copy-start(f32[4,64,1024]{2,1,0:T(8,128)} %get-tuple-element.172) | copy-start | bytes 3145732
  435.2 6.9 %copy-start.1 = (s32[1024]{0:T(1024)S(1)}, s32[1024]{0:T(1024)}, u32[]{:S(2)}) copy-start(s32[1024]{0:T(1024)} %param.14) | copy-start | bytes 12292
  (3 other events, 3.7 us)

commit v8 on v7

--- a/solution.py
+++ b/solution.py
@@ -502,12 +502,10 @@
     )(routed_terms, share, d_produced, active, incoming, d_gate_up)
 
 
-def outputs_kernel(a_ref, hid_ref, ao, hid_out, s1, r1, loc):
+def outputs_kernel(a_ref, ao, s1, r1, loc):
     c, m = place()
-    upper = m >= MP // 2
-    opposite = (CTX - 1 - c, m)
     mates = [(c, lax.rem(m + k, MP)) for k in range(1, MP)]
-    greet(mates + [opposite], MP)
+    greet(mates, MP - 1)
     own_a = pltpu.make_async_copy(a_ref.at[m], ao.at[m], loc.at[0])
     own_a.start()
     copies = []
@@ -516,28 +514,9 @@
         copies.append(remote(a_ref.at[to], ao.at[m], s1.at[k], r1.at[k], mates[k - 1]))
     for copy in copies:
         copy.start()
-    move = remote(hid_ref, hid_out, s1.at[0], r1.at[0], opposite)
-    stay = pltpu.make_async_copy(hid_ref, hid_out, loc.at[1])
-
-    @pl.when(upper)
-    def _():
-        move.start()
-
-    @pl.when(jnp.logical_not(upper))
-    def _():
-        stay.start()
-
     for copy in copies:
         copy.wait()
     own_a.wait()
-
-    @pl.when(upper)
-    def _():
-        move.wait()
-
-    @pl.when(jnp.logical_not(upper))
-    def _():
-        stay.wait()
 
 
 def keys_grad_kernel(
@@ -973,8 +952,8 @@
 
 
 def backward_kernel(
-    q_ref, og_ref, att_ref, lse_ref, kv_ref, sum_0, pair_ref, br_ref, mixed_ref,
-    dkv_ref, dq_ref, in_grad, out_grad, br_all, mixed_out,
+    q_ref, og_ref, att_ref, lse_ref, kv_ref, sum_0, pair_ref, br_ref, mixed_ref, hid_ref,
+    dkv_ref, dq_ref, in_grad, out_grad, br_all, mixed_out, hid_out,
     total, do_ref, delta_ref, own_a, own_b, got_a, got_b, sum_a, sum_b, last_0, last_a, last_b,
     *sems,
 ):
@@ -984,8 +963,12 @@
     peers = [(lax.rem(c + 4 * k, CTX), m) for k in range(1, 4)]
     across = (flip(c, 2), m)
     mates = [(c, lax.rem(m + k, MP)) for k in range(1, MP)]
-    greet(peers + [across] + mates, 4 + MP - 1)
+    upper = m >= MP // 2
+    opposite = (CTX - 1 - c, m)
+    greet(peers + [across, opposite] + mates, 5 + MP - 1)
     sa, ra, sb, rb, sm, rm, loc = sems[:7]
+    move = remote(hid_ref, hid_out, sm.at[0], rm.at[0], opposite)
+    stay = pltpu.make_async_copy(hid_ref, hid_out, loc.at[3])
     ring = mp_ring(br_ref, slots(br_all), sems[7:10])
 
     def first_copies():
@@ -1088,6 +1071,14 @@
             for copy in mixed_copies():
                 copy.start()
 
+        @pl.when(jnp.logical_and(index == 1, upper))
+        def _():
+            move.start()
+
+        @pl.when(jnp.logical_and(index == 1, jnp.logical_not(upper)))
+        def _():
+            stay.start()
+
         @pl.when(index == 18)
         def _():
             ring.relay_near()
@@ -1138,9 +1129,17 @@
         copy.wait()
     own_mixed().wait()
 
+    @pl.when(upper)
+    def _():
+        move.wait()
+
+    @pl.when(jnp.logical_not(upper))
+    def _():
+        stay.wait()
+
 
 def attention_back(
-    q_rows, out_grad, attended, lse, kv_all, sum_first, pair, branch_grad, mixed
+    q_rows, out_grad, attended, lse, kv_all, sum_first, pair, branch_grad, mixed, hidden_grad
 ):
     rows = q_rows.shape[1]
     wide = pair.shape[-1]
@@ -1153,9 +1152,10 @@
             shape((4, 512, 64), f32),
             shape((MP, TOK, 1024)),
             shape((MP, TOK, 1024)),
+            shape((TOK, 1024)),
         ],
-        in_specs=[VM] * 6 + [ANY] * 3,
-        out_specs=[VM] * 4 + [ANY] * 2,
+        in_specs=[VM] * 6 + [ANY] * 4,
+        out_specs=[VM] * 4 + [ANY] * 3,
         scratch_shapes=[
             pltpu.VMEM(kv_all.shape, f32),
             pltpu.VMEM(q_rows.shape, bf16),
@@ -1173,7 +1173,7 @@
         + [pltpu.SemaphoreType.DMA((4,))] * 2
         + [pltpu.SemaphoreType.DMA((5,))] * 2
         + [pltpu.SemaphoreType.DMA((MP,))] * 2
-        + [pltpu.SemaphoreType.DMA((3,))]
+        + [pltpu.SemaphoreType.DMA((4,))]
         + MP_SEMS,
         compiler_params=pltpu.CompilerParams(
             vmem_limit_bytes=VMEM_LIMIT, collective_id=11, has_side_effects=True
@@ -1181,7 +1181,9 @@
         cost_estimate=pl.CostEstimate(
             flops=33 * 10 * HALF * rows * 256, bytes_accessed=1 << 24, transcendentals=33 * HALF * rows
         ),
-    )(q_rows, out_grad, attended, lse, kv_all, sum_first, pair, branch_grad, mixed)
+    )(
+        q_rows, out_grad, attended, lse, kv_all, sum_first, pair, branch_grad, mixed, hidden_grad
+    )
 
 
 def phases(positions, head_width):
@@ -1384,18 +1386,16 @@
     out_grad_terms = jnp.einsum(
         "td,hfd->htf", branch_grad, out_w_all, preferred_element_type=f32
     ).astype(bf16)
-    out_grad, hidden_grad_home = comm_call(
-        outputs_kernel,
-        5,
-        [out_grad_terms, hidden_grad.astype(bf16)],
-        [shape((MP, TOK, 128)), shape((TOK, 1024))],
-        [MP, MP, 2],
-        1 << 20,
+    (out_grad,) = comm_call(
+        outputs_kernel, 5, [out_grad_terms], [shape((MP, TOK, 128))], [MP, MP, 1], 1 << 20
     )
     out_grad = out_grad.reshape(BLOCK, 128)
 
-    dkv_terms, dq_cols, expert_in, expert_out, branch_rows, mixed_got = attention_back(
-        q_rows, out_grad, attended, lse, kv_all, sum_first, pair, branch_grad, mixed
+    dkv_terms, dq_cols, expert_in, expert_out, branch_rows, mixed_got, hidden_grad_home = (
+        attention_back(
+            q_rows, out_grad, attended, lse, kv_all, sum_first, pair, branch_grad, mixed,
+            hidden_grad.astype(bf16),
+        )
     )
     outputs = (hidden_own + jnp.sum(mixed_got.astype(f32), axis=0)).astype(bf16)
     dkv = keys_grad(dkv_terms.reshape(4, 2, 2, BLOCK, 128))

time: 451 us -> 451 us (level)
    pallas_call x1, Pallas kernels: 66.1 us -> 76.1 us  [attention_back(): pl.pallas_call(backward_kernel, out_shape=[shape(kv_all.shape, bf16), sha...]
    pallas_call x3, Pallas kernels: 83.1 us -> 77.5 us  [comm_call(): pl.pallas_call(kernel, out_shape=outs, in_specs=[ANY] * len(arrays), out_...]
where the time goes in v8:
time: 451 us; the launch traced here: 443 us
  Pallas kernels  358 us (79%)
  matrix products  32.3 us (7%)
  local copies, waits for them, and re-layouts  26.4 us (6%)
  other arithmetic  18.3 us (4%)
  starting transfers between devices  5.96 us (1%)
    pallas_call x3, Pallas kernels, comm_call(): pl.pallas_call(kernel, out_shape=outs, in_specs=[ANY] * len(arrays), out_...  77.5 us
    pallas_call x1, Pallas kernels, attention_back(): pl.pallas_call(backward_kernel, out_shape=[shape(kv_all.shape, bf16), sha...  76.1 us
    pallas_call x1, Pallas kernels, attention(): pl.pallas_call(forward_kernel, out_shape=[shape((BLOCK, 128), f32), shape...  58 us
    pallas_call x1, Pallas kernels, scatter_rows(): pl.pallas_call(scatter_kernel, out_shape=[shape((MP, TOK, 1024)), shape((...  35.3 us
    pallas_call x1, Pallas kernels, keys_and_values(): pl.pallas_call(keys_kernel, out_shape=[shape((BLOCK, 1024)), shape((2, 2...  33.4 us
    pallas_call x1, Pallas kernels, keys_grad(): pl.pallas_call(keys_grad_kernel, out_shape=shape((BLOCK, 128), f32), in_s...  29.2 us
    pallas_call x1, Pallas kernels, last_sums(): pl.pallas_call(sums_kernel, out_shape=[shape(dims, f32), shape((TOK, 1024...  25.8 us
    pallas_call x1, Pallas kernels, finish(): pl.pallas_call(finish_kernel, out_shape=[shape((MP, TOK, 256)), shape((CT...  23.1 us
  transfers between devices with their start and end apart: 1, of which 0 were waited for; matrix products, arithmetic and copies ran while one was open for 3% of the time, Pallas kernels for 9%

profile of v8, /device:TPU:65, one launch (start us, length us, event | category | flops | bytes accessed | tf_op | source)
XLA Modules:
  0.0 443.0 jit_solution(10808756245369237364)
XLA Ops:
  0.7 6.0 %collective-permute-start = (bf16[128,1024]{1,0:T(8,128)(2,1)}, bf16[128,1024]{1,0:T(8,128)(2,1)S(1)}, u32[]{:S(2)}, u32[]{:S(2)}) collective-permute-start(bf16[128,1024]{1,0:T(8,128)(2,1)} %param.25), channel_id=1, source_target_pairs={{0,0},{1,1},{2,2},{3,3},{4,124},{5,125},{6,126},{7,127},{8,8},{9,9... | collective-permute-start | bytes 786440 | tf_op jit(solution)/shard_map/ppermute | solution.py:1215
  12.0 38.0 %shard_map.212 = (bf16[8,128,1024]{2,1,0:T(8,128)(2,1)}, s32[8,16,128]{2,1,0:T(8,128)}, bf16[16,64,512]{2,1,0:T(8,128)(2,1)}) custom-call(bf16[128,1024]{1,0:T(8,128)(2,1)} %x_ref.3, s32[16,128]{1,0:T(8,128)} %add_add_fusion.id_ref, bf16[64,512]{1,0:T(8,128)(2,1)} %concatenate.14.w_ref), custom_call_target="tpu_custom_call" | custom-call | bytes 4194304 | tf_op jit(solution)/shard_map/pallas_call | solution.py:54
  53.3 1.9 slice.53.w_ref.qw_ref
  59.8 33.4 %shard_map.213 = (bf16[1024,1024]{1,0:T(8,128)(2,1)}, bf16[2,1024,128]{2,1,0:T(8,128)(2,1)}, bf16[16,1024,128]{2,1,0:T(8,128)(2,1)}, bf16[8,128,1024]{2,1,0:T(8,128)(2,1)}) custom-call(bf16[1024,1024]{1,0:T(8,128)(2,1)} %bitcast.80, f32[1,1024]{1,0:T(1,128)} %bitcast.89, bf16[1024,256]{1,0:T(8,128)(2,1)} %slice.53.w_ref.qw_ref, ...), custom_call_target="tpu_custom_call" | custom-call | tf_op jit(solution)/shard_map/pallas_call | solution.py:358
  93.2 58.0 %shard_map.214 = (f32[1024,128]{1,0:T(8,128)}, bf16[1024,128]{1,0:T(8,128)(2,1)}, f32[2,1,1024]{2,1,0:T(1,128)}, bf16[4,1024,1024]{2,1,0:T(8,128)(2,1)}, bf16[8,...) custom-call(bf16[2,1024,128]{2,1,0:T(8,128)(2,1)} %get-tuple-element.53.q_ref, bf16[32,512,128]{2,1,0:T(8,128)(2,1)} %bitcast.100, ...), custom_call_target="tpu_custom_call" | custom-call | flops 17716740096 | bytes 8388608 | tf_op jit(solution)/shard_map/pallas_call | solution.py:927
  151.3 30.7 %shard_map.215 = (bf16[8,1024,128]{2,1,0:T(8,128)(2,1)}, bf16[4,1024,512]{2,1,0:T(8,128)(2,1)}) custom-call(bf16[1024,128]{1,0:T(8,128)(2,1)} %get-tuple-element.55.a_ref.rows_ref, bf16[4,64,512]{2,1,0:T(8,128)(2,1)} %bitcast.85), custom_call_target="tpu_custom_call" | custom-call | bytes 8388608 | tf_op jit(solution)/shard_map/pallas_call | solution.py:54
  182.0 4.8 %multiply_reduce_fusion = (f32[1024]{0:T(1024)S(1)}, f32[1024,1024]{1,0:T(8,128)S(1)}) fusion(bf16[8,1024,128]{2,1,0:T(8,128)(2,1)} %get-tuple-element.56, bf16[8,128,1024]{2,1,0:T(8,128)(2,1)} %get-tuple-element.57, bf16[1024,1024]{1,0:T(8,128)(2,1)S(1)} %bitcast.81), kind=kOutput, calls=%fused_computation.23 | convolution fusion | flops 2152725504 | bytes 10489856 | tf_op jit(solution)/shard_map/dot_general | solution.py:1291
  189.0 3.3 convolution_convert_fusion
  193.7 2.6 fusion.35
  197.1 1.8 copy-done.6
  200.5 2.8 fusion
  204.8 4.6 %fusion.7 = bf16[1024,1024]{1,0:T(8,128)(2,1)} fusion(bf16[4,288,1024]{2,1,0:T(8,128)(2,1)S(1)} %convolution_convert_fusion.2, f32[4,288]{1,0:T(4,128)S(1)} %get-tuple-element.134, s32[4,1024]{1,0:T(4,128)S(1)} %fusion.21), kind=kOutput, calls=%fused_computation.15 | convolution fusion | flops 2422734848 | bytes 4477440 | tf_op jit(solution)/shard_map/dot_general | solution.py:30
  209.9 2.0 multiply_convert_fusion.4
  213.8 2.9 convolution_convert_fusion.1
  216.7 4.2 bitcast_convert_fusion
  221.5 35.3 %shard_map.216 = (bf16[8,128,1024]{2,1,0:T(8,128)(2,1)}, f32[8,8,128]{2,1,0:T(8,128)}, bf16[3,4,2,64,1536]{4,3,2,1,0:T(8,128)(2,1)}, bf16[2,64,1536]{2,1,0:T(8,128)(2,1)}) custom-call(bf16[8,128,1024]{2,1,0:T(8,128)(2,1)} %bitcast.79, f32[8,8,128]{2,1,0:T(8,128)} %pad.4.b_ref, bf16[4,288,1024]{2,1,0:T(8,128)(2,1)} %copy-done.4, ...), custom_call_target="tpu_custom_call" | custom-call | tf_op jit(solution)/shard_map/pallas_call | solution.py:480
  257.6 2.0 convert_reduce_fusion.1
  260.9 1.9 fusion.33
  264.3 8.8 %shard_map.217 = bf16[8,128,128]{2,1,0:T(8,128)(2,1)} custom-call(bf16[8,128,128]{2,1,0:T(8,128)(2,1)} %fusion.18.a_ref), custom_call_target="tpu_custom_call" | custom-call | bytes 1048576 | tf_op jit(solution)/shard_map/pallas_call | solution.py:54
  273.1 76.1 %shard_map.218 = (bf16[32,512,128]{2,1,0:T(8,128)(2,1)}, f32[2,128,1024]{2,1,0:T(8,128)}, f32[4,64,1024]{2,1,0:T(8,128)}, f32[4,512,64]{2,1,0:T(8,128)}, bf16[8,...) custom-call(bf16[2,1024,128]{2,1,0:T(8,128)(2,1)} %get-tuple-element.53.q_ref, ...), custom_call_target="tpu_custom_call" | custom-call | flops 44291850240 | bytes 16777216 | tf_op jit(solution)/shard_map/pallas_call | solution.py:1146
  349.2 2.0 convert_reduce_fusion
  353.1 29.2 %shard_map.219.dkv_ref = f32[1024,128]{1,0:T(8,128)} custom-call(bf16[4,2,2,1024,128]{4,3,2,1,0:T(8,128)(2,1)} %bitcast.70), custom_call_target="tpu_custom_call" | custom-call | tf_op jit(solution)/shard_map/pallas_call | solution.py:587
  382.5 23.1 %shard_map.220 = (bf16[8,128,256]{2,1,0:T(8,128)(2,1)}, bf16[16,64,384]{2,1,0:T(8,128)(2,1)}) custom-call(f32[2,128,1024]{2,1,0:T(8,128)} %get-tuple-element.67.dq_ref, f32[1024,128]{1,0:T(8,128)} %shard_map.219.dkv_ref, f32[32,1024]{1,0:T(8,128)} %get-tuple-element.51.cos_ref, f32[32,1024]{1,0:T(8,128)} %get-tuple-element.52.sin_ref, ...), custom_call_target="tpu_custom_call" | custom-call | tf_op jit(solution)/shard_map/pallas_call | solution.py:704
  406.6 25.8 %shard_map.221 = (f32[8,128]{1,0:T(8,128)}, bf16[128,1024]{1,0:T(8,128)(2,1)}, f32[64,128]{1,0:T(8,128)}, f32[64,64]{1,0:T(8,128)}, f32[64,64]{1,0:T(8,128)}, /*...) custom-call(f32[1024,128]{1,0:T(8,128)} %maximum_maximum_fusion.small_ref, bf16[8,128,256]{2,1,0:T(8,128)(2,1)} %get-tuple-element.71.qg_ref, ...), custom_call_target="tpu_custom_call" | custom-call | tf_op jit(solution)/shard_map/pallas_call | solution.py:802
  (115 shorter events, 40.4 us)
Async XLA Ops:
  0.6 8.4 %copy-start = (s32[1024]{0:T(1024)S(1)}, s32[1024]{0:T(1024)}, u32[]{:S(2)}) copy-start(s32[1024]{0:T(1024)} %param.14) | copy-start | bytes 12292
  0.7 58.5 %collective-permute-start = (bf16[128,1024]{1,0:T(8,128)(2,1)}, bf16[128,1024]{1,0:T(8,128)(2,1)S(1)}, u32[]{:S(2)}, u32[]{:S(2)}) collective-permute-start(bf16[128,1024]{1,0:T(8,128)(2,1)} %param.25), channel_id=1, source_target_pairs={{0,0},{1,1},{2,2},{3,3},{4,124},{5,125},{6,126},{7,127},{8,8},{9,9... | collective-permute-start | bytes 786440 | tf_op jit(solution)/shard_map/ppermute | solution.py:1215
  50.0 5.2 %copy-start.7 = (bf16[16,64,512]{2,1,0:T(8,128)(2,1)S(1)}, bf16[16,64,512]{2,1,0:T(8,128)(2,1)}, u32[]{:S(2)}) copy-start(bf16[16,64,512]{2,1,0:T(8,128)(2,1)} %get-tuple-element.49) | copy-start | bytes 3145732
  93.2 88.8 %copy-start.10 = (bf16[8,128,1024]{2,1,0:T(8,128)(2,1)S(1)}, bf16[8,128,1024]{2,1,0:T(8,128)(2,1)}, u32[]{:S(2)}) copy-start(bf16[8,128,1024]{2,1,0:T(8,128)(2,1)} %get-tuple-element.48) | copy-start | bytes 6291460
  186.8 74.1 %copy-start.2 = (f32[1024,1024]{1,0:T(8,128)}, f32[1024,1024]{1,0:T(8,128)S(1)}, u32[]{:S(2)}) copy-start(f32[1024,1024]{1,0:T(8,128)S(1)} %get-tuple-element.144) | copy-start | bytes 12582916
  186.8 2.2 copy-start.11
  186.8 6.8 %slice-start = ((s8[8388608]{0:T(1024)(128)(4,1)}), s8[4194304]{0:T(1024)(128)(4,1)S(1)}, s32[]{:S(2)}) async-start(s8[8388608]{0:T(1024)(128)(4,1)} %bitcast.103), calls=%async_computation | async-start | bytes 8388608
  189.0 4.7 %slice-start.1 = ((s8[8388608]{0:T(1024)(128)(4,1)}), s8[4194304]{0:T(1024)(128)(4,1)S(1)}, s32[]{:S(2)}) async-start(s8[8388608]{0:T(1024)(128)(4,1)} %bitcast.103), calls=%async_computation.1 | async-start | bytes 8388608
  196.3 2.6 copy-start.6
  197.0 3.3 copy-start.3
  209.5 3.0 slice-start.2
  209.9 2.0 copy-start.4
  209.9 4.0 slice-start.3
  213.8 2.9 copy-start.5
  260.2 2.6 copy-start.9
  262.8 10.3 %copy-start.12 = (bf16[128,1024]{1,0:T(8,128)(2,1)}, bf16[128,1024]{1,0:T(8,128)(2,1)S(1)}, u32[]{:S(2)}) copy-start(bf16[128,1024]{1,0:T(8,128)(2,1)S(1)} %multiply_convert_fusion.5.br_ref) | copy-start | bytes 786436
  406.6 29.0 %copy-start.13 = (f32[4,512,64]{2,1,0:T(8,128)S(1)}, f32[4,512,64]{2,1,0:T(8,128)}, u32[]{:S(2)}) copy-start(f32[4,512,64]{2,1,0:T(8,128)} %get-tuple-element.128) | copy-start | bytes 1572868
  432.4 6.0 %copy-start.16 = (bf16[128,1024]{1,0:T(8,128)(2,1)S(1)}, bf16[128,1024]{1,0:T(8,128)(2,1)}, u32[]{:S(2)}) copy-start(bf16[128,1024]{1,0:T(8,128)(2,1)} %get-tuple-element.162) | copy-start | bytes 786436
  432.5 6.7 %copy-start.21 = (f32[64,128]{1,0:T(8,128)S(1)}, f32[64,128]{1,0:T(8,128)}, u32[]{:S(2)}) copy-start(f32[64,128]{1,0:T(8,128)} %get-tuple-element.164) | copy-start | bytes 98308
  432.5 7.3 %copy-start.20 = (f32[64,64]{1,0:T(8,128)S(1)}, f32[64,64]{1,0:T(8,128)}, u32[]{:S(2)}) copy-start(f32[64,64]{1,0:T(8,128)} %get-tuple-element.165) | copy-start | bytes 49156
  432.5 7.9 %copy-start.19 = (f32[64,64]{1,0:T(8,128)S(1)}, f32[64,64]{1,0:T(8,128)}, u32[]{:S(2)}) copy-start(f32[64,64]{1,0:T(8,128)} %get-tuple-element.166) | copy-start | bytes 49156
  432.5 8.5 %copy-start.17 = (f32[8,128]{1,0:T(8,128)S(1)}, f32[8,128]{1,0:T(8,128)}, u32[]{:S(2)}) copy-start(f32[8,128]{1,0:T(8,128)} %get-tuple-element.78) | copy-start | bytes 12292
  432.5 9.1 %copy-start.14 = (f32[4,64,1024]{2,1,0:T(8,128)S(1)}, f32[4,64,1024]{2,1,0:T(8,128)}, u32[]{:S(2)}) copy-start(f32[4,64,1024]{2,1,0:T(8,128)} %get-tuple-element.170) | copy-start | bytes 3145732
  435.6 6.9 %copy-start.1 = (s32[1024]{0:T(1024)S(1)}, s32[1024]{0:T(1024)}, u32[]{:S(2)}) copy-start(s32[1024]{0:T(1024)} %param.14) | copy-start | bytes 12292
  (3 other events, 3.7 us)
